TPU v7x, 32 devices: a whole 2x2x4 slice. The times are simulated.
32 devices in a mesh: dp: 4 (over y, x), expert: 8 (over z, core).
Axes of the slice: x: 2, y: 2, z: 4, core: 2. Of those that a mesh axis runs over, the one named last changes fastest.
Arguments:
- tokens: bfloat16 [2048, 2048], P(('dp', 'expert')), may hold values from -6 to 6
- expert_ids: int32 [2048, 8], P(('dp', 'expert')), may hold values from 0 to 31, all different within a row; in each aligned block of 64 rows (0 to 63, 64 to 127, ...) at most 24 rows name the same one
- gate_fixed: int32 [2048, 8], P(('dp', 'expert')), may hold values from 1 to 65535
- scorer_id: int32 [128], P(('dp', 'expert')), may hold values from 0 to 1
- direction_tags: bfloat16 [2, 2048], replicated, may hold values from -6 to 6
- w_gate: bfloat16 [32, 2048, 512], P('expert'), may hold values from -0.125 to 0.125
- w_up: bfloat16 [32, 2048, 512], P('expert'), may hold values from -0.125 to 0.125
- w_down: bfloat16 [32, 512, 2048], P('expert'), may hold values from -0.25 to 0.25
- score_head: float32 [2048], replicated, may hold values from -0.125 to 0.125
Outputs:
- mixed: bfloat16 [2048, 2048], P(('dp', 'expert'))
- pair_score: float32 [128], P(('dp', 'expert'))
Inputs may be any that keep to these rules, and one draw needn't show every extreme that they name: `expert_ids`: each row names 8 different experts. Among the rows of one device no expert is named by more than 24 rows, and in some devices' rows an expert is named by exactly 24.
All inputs are finite; a program needn't handle non-finite values.
Results may differ from a plain program's by a relative error of at most 0.04.
Values may be sent and summed in bfloat16 or wider, within the bound.
No kernel may reach another device: no remote copies, remote signals or barrier semaphores. Data moves between devices by JAX's collectives and lax.ppermute only.
A program may use at most 64 MiB of HBM per device.

v0:
```python
import jax
import jax.numpy as jnp
from jax import lax
from jax.sharding import PartitionSpec as P

SEQ_LEN = 16
MOST = 24


def from_partner(block, axis, bit):
    count = lax.axis_size(axis)
    route = []
    for low in range(count):
        high = low | 1 << bit
        if high != low and high < count:
            route += [(low, high), (high, low)]
    return lax.ppermute(block, axis, route)


def route_ranks(expert_ids, expert_total):
    flat_ids = expert_ids.reshape(-1)
    entry_count = flat_ids.shape[0]
    onehot = flat_ids[:, None] == jnp.arange(expert_total, dtype=jnp.int32)[None, :]
    positions = jnp.arange(entry_count, dtype=jnp.int32)
    earlier = (positions[:, None] > positions[None, :]).astype(jnp.bfloat16)
    counts = jnp.dot(earlier, onehot.astype(jnp.bfloat16), preferred_element_type=jnp.float32)
    rank_in = jnp.sum(jnp.where(onehot, counts, 0.0), axis=1).astype(jnp.int32)
    return rank_in.reshape(expert_ids.shape)


def body(
    tokens, expert_ids, gate_fixed, scorer_id, direction_tags, w_gate, w_up, w_down, score_head
):
    expert_count = lax.axis_size("expert")
    per_device = w_gate.shape[0]
    tok_rows, model_width = tokens.shape
    top_count = expert_ids.shape[1]
    which_tag = jnp.repeat(scorer_id, SEQ_LEN)[:, None]
    tag_rows = jnp.where(
        which_tag == 1, direction_tags[1][None, :], direction_tags[0][None, :]
    ).astype(jnp.float32)
    inputs = (tokens.astype(jnp.float32) + tag_rows).astype(jnp.bfloat16)
    fixed_val = gate_fixed.astype(jnp.float32)
    weight = fixed_val / jnp.sum(fixed_val, axis=1, keepdims=True)
    rank_in = route_ranks(expert_ids, per_device * expert_count)
    inputs_all, ids_all, weight_all, rank_all = (
        lax.all_gather(inputs, "expert", axis=0, tiled=True),
        lax.all_gather(expert_ids, "expert", axis=0, tiled=True),
        lax.all_gather(weight.astype(jnp.bfloat16), "expert", axis=0, tiled=True).astype(
            weight.dtype
        ),
        lax.all_gather(rank_in, "expert", axis=0, tiled=True),
    )
    my_index = lax.axis_index("expert")
    local_count = per_device * MOST
    ids_cube = ids_all.reshape(expert_count, tok_rows, top_count)
    rank_cube = rank_all.reshape(expert_count, tok_rows, top_count)
    weight_cube = weight_all.reshape(expert_count, tok_rows, top_count)
    local_slot = ids_cube - my_index * per_device
    is_mine = (local_slot >= 0) & (local_slot < per_device)
    local_key = jnp.where(is_mine, local_slot * MOST + rank_cube, -1)
    match = (
        local_key[:, None, :, :] == jnp.arange(local_count, dtype=jnp.int32)[None, :, None, None]
    )
    picker = jnp.any(match, axis=3).astype(jnp.bfloat16)
    slot_weight = jnp.sum(jnp.where(match, weight_cube[:, None, :, :], 0.0), axis=(2, 3)).reshape(
        expert_count, per_device, MOST
    )
    inputs_cube = inputs_all.reshape(expert_count, tok_rows, model_width)
    row_block = jnp.einsum(
        "sqt,std->sqd", picker, inputs_cube, preferred_element_type=jnp.float32
    ).astype(jnp.bfloat16)
    row_block = row_block.reshape(expert_count, per_device, MOST, model_width)
    gate_proj = jnp.einsum("nemd,edf->nemf", row_block, w_gate, preferred_element_type=jnp.float32)
    up_proj = jnp.einsum("nemd,edf->nemf", row_block, w_up, preferred_element_type=jnp.float32)
    hidden = (jax.nn.silu(gate_proj) * up_proj).astype(jnp.bfloat16)
    down_out = jnp.einsum("nemf,efd->nemd", hidden, w_down, preferred_element_type=jnp.float32)
    result = (slot_weight[..., None] * down_out).astype(jnp.bfloat16)
    partial_value = jnp.einsum(
        "sqt,sqd->std",
        picker,
        result.reshape(expert_count, local_count, model_width),
        preferred_element_type=jnp.float32,
    )
    partial_value = partial_value.reshape(expert_count * tok_rows, model_width)
    received = lax.all_to_all(
        partial_value.astype(jnp.bfloat16), "expert", split_axis=0, concat_axis=0, tiled=True
    ).astype(partial_value.dtype)
    summed = received.reshape(expert_count, tok_rows, model_width).sum(axis=0)
    mixed = summed.astype(jnp.bfloat16)
    token_score = jnp.dot(mixed.astype(jnp.float32), score_head, precision=lax.Precision.HIGHEST)
    seq_score = token_score.reshape(-1, SEQ_LEN).sum(axis=1)
    partner = from_partner(seq_score, "dp", lax.axis_size("dp").bit_length() - 2)
    pair_score = jnp.abs(seq_score - partner) + 0.5 * (seq_score + partner)
    return (mixed, pair_score)


def solution(mesh):
    return jax.shard_map(
        body,
        mesh=mesh,
        in_specs=(
            P(("dp", "expert"), None),
            P(("dp", "expert"), None),
            P(("dp", "expert"), None),
            P(("dp", "expert")),
            P(),
            P("expert", None, None),
            P("expert", None, None),
            P("expert", None, None),
            P(),
        ),
        out_specs=(P(("dp", "expert"), None), P(("dp", "expert"))),
        check_vma=False,
    )
```

profile of v0, /device:TPU:0, one launch (start us, length us, event | category | flops | bytes accessed | tf_op | source)
XLA Modules:
  0.0 145.9 jit_solution(13358383711363568817)
XLA Ops:
  7.2 0.0 copy-start
  7.2 0.0 all-gather.5.cloned.1.call-start
  7.2 0.7 broadcast_compare_fusion
  7.9 0.1 broadcast_in_dim.68
  8.0 0.1 eq.52
  8.1 0.8 slice_reduce_fusion.1
  8.9 1.8 %add_convert_fusion = bf16[64,2048]{1,0:T(8,128)(2,1)} fusion(bf16[64,2048]{1,0:T(8,128)(2,1)} %param.9, pred[64]{0:T(512)(128)(4,1)S(1)} %eq.52, bf16[2048]{0:T(1024)(128)(2,1)S(1)} %get-tuple-element.3, bf16[2048]{0:T(1024)(128)(2,1)S(1)} %get-tuple-element.2), kind=kLoop, calls=%fused_computation.26 | loop fusion | flops 655360 | bytes 532544 | tf_op jit(solution)/shard_map/convert_element_type | solution.py:42
  10.7 0.0 all-gather.5.cloned.1.call-update
  10.7 0.8 copy.28
  11.5 0.1 eq.43
  11.6 0.3 fusion.24
  11.9 0.1 reshape.70
  11.9 0.1 copy.29
  12.0 15.9 %all-gather = s32[8,64,8]{1,2,0:T(8,128)S(1)} all-gather(s32[1,64,8]{1,2,0:T(8,128)} %bitcast.68), channel_id=1, replica_groups=mesh['dp'=4,'expert'=8] {'expert'}, dimensions={0}, use_global_device_ids=true | all-gather | bytes 18432 | tf_op jit(solution)/shard_map/all_gather | solution.py:48
  27.9 14.1 %all-gather.1 = s32[8,64,8]{1,2,0:T(8,128)S(1)} all-gather(s32[1,64,8]{1,2,0:T(8,128)S(1)} %copy.29), channel_id=1, replica_groups=mesh['dp'=4,'expert'=8] {'expert'}, dimensions={0}, use_global_device_ids=true | all-gather | bytes 18432 | tf_op jit(solution)/shard_map/all_gather | solution.py:52
  42.0 0.1 copy.30
  42.1 0.7 convert_reduce_fusion
  42.8 0.7 fusion.27
  43.5 12.7 %all-gather.2 = bf16[8,64,8]{1,2,0:T(8,128)(2,1)S(1)} all-gather(bf16[1,64,8]{1,2,0:T(8,128)(2,1)S(1)} %fusion.27), channel_id=1, replica_groups=mesh['dp'=4,'expert'=8] {'expert'}, dimensions={0}, use_global_device_ids=true | all-gather | bytes 9216 | tf_op jit(solution)/shard_map/all_gather | solution.py:49
  56.2 0.1 copy.31
  56.3 1.4 select_reduce_fusion
  57.7 0.1 mul.37
  57.8 0.9 fusion.11
  58.7 0.0 all-gather.5.cloned.1.call-done
  58.8 2.6 %convolution_convert_fusion = bf16[8,96,2048]{2,1,0:T(8,128)(2,1)S(1)} fusion(pred[8,96,64]{1,2,0:T(8,128)(4,1)S(1)} %fusion.11, bf16[8,64,2048]{2,1,0:T(8,128)(2,1)} %bitcast.66), kind=kOutput, calls=%fused_computation.8 | convolution fusion | flops 202899456 | bytes 5292032 | tf_op jit(solution)/shard_map/sqt,std->sqd/dot_general | solution.py:70
  61.4 0.0 copy-start.1
  61.4 1.7 %copy-done.1 = bf16[8,96,2048]{2,1,0:T(8,128)(2,1)} copy-done((bf16[8,96,2048]{2,1,0:T(8,128)(2,1)}, bf16[8,96,2048]{2,1,0:T(8,128)(2,1)S(1)}, u32[]{:S(2)}) %copy-start.1) | copy-done | bytes 3145752
  63.0 6.3 %fusion.4 = f32[4,8,24,512]{3,2,1,0:T(8,128)} fusion(bf16[4,2048,512]{2,1,0:T(8,128)(2,1)} %param.14, bf16[8,4,24,2048]{3,2,1,0:T(8,128)(2,1)S(1)} %bitcast.64), kind=kOutput, calls=%fused_computation.4 | convolution fusion | flops 1610612736 | bytes 13107200 | tf_op jit(solution)/shard_map/nemd,edf->nemf/dot_general | solution.py:74
  69.4 10.7 %fusion.6 = bf16[8,4,24,2048]{3,2,0,1:T(8,128)(2,1)S(1)} fusion(bf16[4,512,2048]{2,1,0:T(8,128)(2,1)} %param.16, f32[8,4,24]{2,0,1:T(8,128)S(1)} %copy.32, f32[4,8,24,512]{3,2,1,0:T(8,128)} %fusion.4, bf16[4,2048,512]{2,1,0:T(8,128)(2,1)} %param.15, bf16[8,4,24,2048]{3,2,1,0:T(8,128)(2,1)} %bitcast.65), kind=kOutput, calls=%fused_computation.7 | convolution fusion | flops 3226730496 | bytes 24644608 | tf_op jit(solution)/shard_map/nemf,efd->nemd/dot_general | solution.py:77
  80.0 0.4 copy.35
  80.4 0.7 convolution_convert_fusion.1
  81.2 52.2 %all_to_all.6 = bf16[8,64,2048]{2,1,0:T(8,128)(2,1)S(1)} all-to-all(bf16[8,64,2048]{2,1,0:T(8,128)(2,1)S(1)} %convolution_convert_fusion.1), channel_id=1, replica_groups=mesh['dp'=4,'expert'=8] {'expert'}, dimensions={0} | all-to-all | bytes 4194304 | tf_op jit(solution)/shard_map/all_to_all | solution.py:86
  133.4 0.4 reduce_sum.51
  133.8 0.0 copy-done
  133.8 0.0 copy-start.2
  133.8 1.0 fusion.29
  134.8 0.1 reduce_sum.52
  134.9 1.6 %collective-permute-start = (f32[4]{0:T(128)S(1)}, f32[4]{0:T(128)S(1)}, u32[]{:S(2)}, u32[]{:S(2)}) collective-permute-start(f32[4]{0:T(128)S(1)} %reduce_sum.52), channel_id=1, source_target_pairs={{0,16},{16,0},{8,24},{24,8},{1,17},{17,1},{9,25},{25,9},{2,18},{18... | collective-permute-start | bytes 56 | tf_op jit(solution)/shard_map/ppermute | solution.py:17
  136.5 2.0 %collective-permute-done = f32[4]{0:T(128)S(1)} collective-permute-done((f32[4]{0:T(128)S(1)}, f32[4]{0:T(128)S(1)}, u32[]{:S(2)}, u32[]{:S(2)}) %collective-permute-start) | collective-permute-done | bytes 48 | tf_op jit(solution)/shard_map/ppermute | solution.py:17
  138.5 0.5 multiply_add_fusion
  139.1 0.0 copy-done.2
  (3 shorter events, 0.0 us)
Async XLA Ops:
  7.2 126.6 %copy-start = (f32[2048]{0:T(1024)S(1)}, f32[2048]{0:T(1024)}, u32[]{:S(2)}) copy-start(f32[2048]{0:T(1024)} %param.17) | copy-start | bytes 24580
  7.2 51.6 %all-gather.5.cloned.1.call-start = ((), (), s32[]{:S(2)}) async-start(), calls=%async_computation.1 | async-start | bytes 2359296 | tf_op jit(solution)/shard_map/all_gather | solution.py:47
  61.4 1.7 %copy-start.1 = (bf16[8,96,2048]{2,1,0:T(8,128)(2,1)}, bf16[8,96,2048]{2,1,0:T(8,128)(2,1)S(1)}, u32[]{:S(2)}) copy-start(bf16[8,96,2048]{2,1,0:T(8,128)(2,1)S(1)} %convolution_convert_fusion) | copy-start | bytes 9437188
  133.8 5.3 %copy-start.2 = (bf16[64,2048]{1,0:T(8,128)(2,1)}, bf16[64,2048]{1,0:T(8,128)(2,1)S(1)}, u32[]{:S(2)}) copy-start(bf16[64,2048]{1,0:T(8,128)(2,1)S(1)} %reduce_sum.51) | copy-start | bytes 786436
  134.9 3.6 %collective-permute-start = (f32[4]{0:T(128)S(1)}, f32[4]{0:T(128)S(1)}, u32[]{:S(2)}, u32[]{:S(2)}) collective-permute-start(f32[4]{0:T(128)S(1)} %reduce_sum.52), channel_id=1, source_target_pairs={{0,16},{16,0},{8,24},{24,8},{1,17},{17,1},{9,25},{25,9},{2,18},{18... | collective-permute-start | bytes 56 | tf_op jit(solution)/shard_map/ppermute | solution.py:17
Sparse Core Ops, SparseCore 0:
  10.8 32.1 all-gather.4
where the time goes:
time: 146 us
  blocking collectives  94.9 us (65%)
  matrix products  21.6 us (15%)
  between operations  14.2 us (10%)
  other arithmetic  7.16 us (5%)
  local copies, waits for them, and re-layouts  4.38 us (3%)
  waiting for transfers between devices  2.08 us (1%)
  starting transfers between devices  1.6 us (1%)
    all_to_all x1, blocking collectives, body(): lax.all_to_all(partial_value.astype(jnp.bfloat16), 'expert', split_axis=0...  52.2 us
    all_gather x1, blocking collectives, body(): lax.all_gather(expert_ids, 'expert', axis=0, tiled=True)  15.9 us
    all_gather x1, blocking collectives, body(): lax.all_gather(rank_in, 'expert', axis=0, tiled=True)  14.1 us
    all_gather x1, blocking collectives, body(): lax.all_gather(weight.astype(jnp.bfloat16), 'expert', axis=0, tiled=True)  12.7 us
    dot_general x1, matrix products, body(): jnp.einsum('nemf,efd->nemd', hidden, w_down, preferred_element_type=jnp.f...  10.7 us
    dot_general x1, matrix products, body(): jnp.einsum('nemd,edf->nemf', row_block, w_gate, preferred_element_type=jn...  6.33 us
  transfers between devices with their start and end apart: 2, of which 1 were waited for; matrix products, arithmetic and copies ran while one was open for 4% of the time, Pallas kernels for 0%

commit v1 on v0

v1 whole, which is shorter than its diff:
```python
import functools

import jax
import jax.numpy as jnp
from jax import lax
from jax.experimental import pallas as pl
from jax.experimental.pallas import tpu as pltpu
from jax.sharding import PartitionSpec as P

SEQ_LEN = 16
MOST = 24
META = 128
MIB = 1 << 20

VMEM = pl.BlockSpec(memory_space=pltpu.VMEM)
SMEM = pl.BlockSpec(memory_space=pltpu.SMEM)
ANY = pl.BlockSpec(memory_space=pl.ANY)


def prep_kernel(experts, tok_ref, ids_ref, gate_ref, scorer_ref, tags_ref, out_ref):
    rows, width = tok_ref.shape
    for s in range(rows // SEQ_LEN):
        span = pl.ds(s * SEQ_LEN, SEQ_LEN)
        tag = jnp.where(scorer_ref[s] == 1, tags_ref[1:2, :], tags_ref[0:1, :]).astype(jnp.float32)
        out_ref[span, 0:width] = (tok_ref[span, :].astype(jnp.float32) + tag).astype(jnp.bfloat16)
    fixed = gate_ref[...].astype(jnp.float32)
    weight = fixed / jnp.sum(fixed, axis=1, keepdims=True)
    high = weight.astype(jnp.bfloat16).astype(jnp.float32)
    low = weight - high
    ids = ids_ref[...]
    lane = lax.broadcasted_iota(jnp.int32, (rows, META), 1)
    meta = jnp.zeros((rows, META), jnp.float32)
    for k in range(ids.shape[1]):
        one = ids[:, k : k + 1]
        meta = meta + jnp.where(lane == one, high[:, k : k + 1], 0.0)
        meta = meta + jnp.where(lane == one + experts, low[:, k : k + 1], 0.0)
    out_ref[:, width : width + META] = meta.astype(jnp.bfloat16)


def pick_rows(meta, first, per_device, experts):
    rows = meta.shape[0]
    room = 2 * MOST
    lane = lax.broadcasted_iota(jnp.int32, meta.shape, 1)
    routed = (meta > 0) & (lane < experts)
    row = lax.broadcasted_iota(jnp.int32, (rows, rows), 0)
    col = lax.broadcasted_iota(jnp.int32, (rows, rows), 1)
    earlier = (row > col).astype(jnp.bfloat16)
    rank = jnp.dot(earlier, routed.astype(jnp.bfloat16), preferred_element_type=jnp.float32)
    rank = jnp.where(routed, rank, -1.0)
    slot = lax.broadcasted_iota(jnp.int32, (rows, per_device * room), 1)
    hit = jnp.zeros((rows, per_device * room), jnp.bool_)
    for e in range(per_device):
        mine = jnp.max(jnp.where(lane == first + e, rank, -1.0), axis=1, keepdims=True).astype(jnp.int32)
        hit = hit | ((mine >= 0) & (slot == mine + e * room))
    return hit.astype(jnp.float32).astype(jnp.bfloat16)


def ffn_kernel(groups, experts, *refs):
    total = sum(a + b for a, b in groups)
    x_refs, refs = refs[:total], refs[total:]
    wg_hbm, wu_hbm, wd_hbm, same_ref, other_ref, wg, wu, wd, g_ref, pick_ref, o_ref, sems = refs
    per_device, width, ff = wg_hbm.shape
    room = 2 * MOST
    first = lax.axis_index("expert") * per_device
    copies = []
    for e in range(per_device):
        for j, (src, dst) in enumerate(((wg_hbm, wg), (wu_hbm, wu), (wd_hbm, wd))):
            copy = pltpu.make_async_copy(src.at[e], dst.at[e], sems.at[e, j])
            copy.start()
            copies.append(copy)
    at = 0
    for k, (a, b) in enumerate(groups):
        halves = []
        for n in (a, b):
            value = x_refs[at][...]
            for i in range(1, n):
                value = value + x_refs[at + i][...]
            at += n
            halves.append(value)
        x = jnp.concatenate(halves, axis=0)
        pick = pick_rows(x[:, width:].astype(jnp.float32), first, per_device, experts)
        pick_ref[k] = pick
        picked = lax.dot_general(pick, x, (((0,), (0,)), ((), ())), preferred_element_type=jnp.float32)
        picked = picked.astype(jnp.bfloat16)
        for e in range(per_device):
            g_ref[e, k * room : (k + 1) * room, :] = picked[e * room : (e + 1) * room, :]
    lane = lax.broadcasted_iota(jnp.int32, (len(groups) * room, META), 1)
    for e in range(per_device):
        x = g_ref[e, :, 0:width]
        meta = g_ref[e, :, width:].astype(jnp.float32)
        mine = (lane == first + e) | (lane == first + e + experts)
        weight = jnp.sum(jnp.where(mine, meta, 0.0), axis=1, keepdims=True)
        copies[3 * e].wait()
        gate = jnp.dot(x, wg[e], preferred_element_type=jnp.float32)
        copies[3 * e + 1].wait()
        up = jnp.dot(x, wu[e], preferred_element_type=jnp.float32)
        hidden = (gate / (1.0 + jnp.exp(-gate)) * up * weight).astype(jnp.bfloat16)
        copies[3 * e + 2].wait()
        out = jnp.dot(hidden, wd[e], preferred_element_type=jnp.float32).astype(jnp.bfloat16)
        for k in range(len(groups)):
            o_ref[k, e * room : (e + 1) * room, :] = out[k * room : (k + 1) * room, :]
    for k in range(len(groups)):
        rows = jnp.dot(pick_ref[k], o_ref[k], preferred_element_type=jnp.float32).astype(jnp.bfloat16)
        half = rows.shape[0] // 2
        same_ref[k] = rows[:half]
        other_ref[k] = rows[half:]


def ffn(groups, experts, xs, w_gate, w_up, w_down):
    per_device, width, ff = w_gate.shape
    rows = xs[0].shape[0]
    chips = len(groups)
    room = 2 * MOST
    out = jax.ShapeDtypeStruct((chips, rows, width), jnp.bfloat16)
    return pl.pallas_call(
        functools.partial(ffn_kernel, groups, experts),
        out_shape=(out, out),
        in_specs=[VMEM] * len(xs) + [ANY] * 3,
        out_specs=(VMEM, VMEM),
        scratch_shapes=[
            pltpu.VMEM((per_device, width, ff), jnp.bfloat16),
            pltpu.VMEM((per_device, width, ff), jnp.bfloat16),
            pltpu.VMEM((per_device, ff, width), jnp.bfloat16),
            pltpu.VMEM((per_device, chips * room, width + META), jnp.bfloat16),
            pltpu.VMEM((chips, 2 * rows, per_device * room), jnp.bfloat16),
            pltpu.VMEM((chips, per_device * room, width), jnp.bfloat16),
            pltpu.SemaphoreType.DMA((per_device, 3)),
        ],
        compiler_params=pltpu.CompilerParams(vmem_limit_bytes=56 * MIB),
        cost_estimate=pl.CostEstimate(
            flops=6 * per_device * chips * room * width * ff,
            bytes_accessed=6 * per_device * width * ff,
            transcendentals=0,
        ),
        name="ffn",
    )(*xs, w_gate, w_up, w_down)


def finish_kernel(n_parts, *refs):
    parts, head_ref, mixed_ref, score_ref = refs[:n_parts], *refs[n_parts:]
    rows = mixed_ref.shape[0]
    total = parts[0][...].astype(jnp.float32)
    for part in parts[1:]:
        total = total + part[...].astype(jnp.float32)
    mixed = total.astype(jnp.bfloat16)
    mixed_ref[...] = mixed
    scored = mixed.astype(jnp.float32) * head_ref[...]
    for s in range(rows // SEQ_LEN):
        score_ref[s] = jnp.sum(scored[s * SEQ_LEN : (s + 1) * SEQ_LEN, :])


def send(x, route):
    return lax.ppermute(x, "expert", route)


def body(tokens, expert_ids, gate_fixed, scorer_id, direction_tags, w_gate, w_up, w_down, score_head):
    devices = lax.axis_size("expert")
    chips = devices // 2
    experts = w_gate.shape[0] * devices
    rows, width = tokens.shape
    x = pl.pallas_call(
        functools.partial(prep_kernel, experts),
        out_shape=jax.ShapeDtypeStruct((rows, width + META), jnp.bfloat16),
        in_specs=[VMEM, VMEM, VMEM, SMEM, VMEM],
        out_specs=VMEM,
        name="prep",
    )(tokens, expert_ids, gate_fixed, scorer_id, direction_tags)

    def exchange(block, k):
        return send(block, [(d, d ^ (2 * k)) for d in range(devices)])

    def core_swap(block):
        return send(block, [(d, d ^ 1) for d in range(devices)])

    hybrid = chips == 4
    middle = [(2 * a + c, 2 * b + c) for a, b in ((1, 2), (2, 1)) for c in (0, 1)]
    outward = [(2 * a + c, 2 * b + c) for a, b in ((1, 0), (2, 3)) for c in (0, 1)]
    inward = [(b, a) for a, b in outward]

    if hybrid:
        far = exchange(x, 2)
        near = exchange(x, 1)
        mid = send(x, middle)
        last = send(far, outward)
        held = [[x], [near], [far], [mid, last]]
    else:
        held = [[x]] + [[exchange(x, k)] for k in range(1, chips)]
    groups, xs = [], []
    for blocks in held:
        one = [core_swap(b) for b in blocks]
        groups.append((len(blocks), len(one)))
        xs += blocks + one
    same, other = ffn(tuple(groups), experts, xs, w_gate, w_up, w_down)
    swapped = core_swap(other)
    summed = (same.astype(jnp.float32) + swapped.astype(jnp.float32)).astype(jnp.bfloat16)
    if hybrid:
        early = send(summed[3], inward)
        far_sum = (summed[2].astype(jnp.float32) + early.astype(jnp.float32)).astype(jnp.bfloat16)
        parts = [summed[0], exchange(summed[1], 1), send(summed[3], middle), exchange(far_sum, 2)]
    else:
        parts = [summed[0]] + [exchange(summed[k], k) for k in range(1, chips)]
    mixed, seq_score = pl.pallas_call(
        functools.partial(finish_kernel, len(parts)),
        out_shape=(
            jax.ShapeDtypeStruct((rows, width), jnp.bfloat16),
            jax.ShapeDtypeStruct((rows // SEQ_LEN,), jnp.float32),
        ),
        in_specs=[VMEM] * len(parts) + [VMEM],
        out_specs=(VMEM, SMEM),
        name="finish",
    )(*parts, score_head.reshape(1, width))
    count = lax.axis_size("dp")
    partner = lax.ppermute(seq_score, "dp", [(d, d ^ (count // 2)) for d in range(count)])
    pair_score = jnp.abs(seq_score - partner) + 0.5 * (seq_score + partner)
    return mixed, pair_score


def solution(mesh):
    tokens, whole = P(("dp", "expert"), None), P()
    weights = P("expert", None, None)
    return jax.shard_map(
        body,
        mesh=mesh,
        in_specs=(tokens, tokens, tokens, P(("dp", "expert")), whole, weights, weights, weights, whole),
        out_specs=(tokens, P(("dp", "expert"))),
        check_vma=False,
    )
```

time: 146 us -> 85.7 us (0.59)
  blocking collectives: 94.9 us -> 0 us
  waiting for transfers between devices: 2.08 us -> 35.7 us
  starting transfers between devices: 1.6 us -> 23.4 us
  matrix products: 21.6 us -> 0 us
  Pallas kernels: 0 us -> 17.6 us
  between operations: 14.2 us -> 0.82 us
  other arithmetic: 7.16 us -> 2.84 us
    all_to_all x1 -> x0, blocking collectives: 52.2 us -> none  [body(): lax.all_to_all(partial_value.astype(jnp.bfloat16), 'expert', split_axis=0...]
    all_gather x3 -> x0, blocking collectives: 42.7 us -> none  [the longest x1 15.9 us: body(): lax.all_gather(expert_ids, 'expert', axis=0, tiled=True)]
    ppermute x1 -> x15, waiting for transfers between devices: 2.04 us -> 35.7 us  [the longest x14 33.6 us: send(): return lax.ppermute(x, 'expert', route)]
    ppermute x1 -> x15, starting transfers between devices: 1.56 us -> 23.4 us  [the longest x14 21.7 us: send(): return lax.ppermute(x, 'expert', route)]
    dot_general x6 -> x0, matrix products: 21.6 us -> none  [the longest x1 10.7 us: body(): jnp.einsum('nemf,efd->nemd', hidden, w_down, preferred_element_type=jnp.f...]
    pallas_call x0 -> x3, Pallas kernels: none -> 17.6 us  [the longest x1 13.4 us: ffn(): pl.pallas_call(functools.partial(ffn_kernel, groups, experts), out_shape=...]
    reduce_sum x4 -> x0, other arithmetic: 2.61 us -> none  [the longest x1 1.4 us: body(): jnp.sum(jnp.where(match, weight_cube[:, None, :, :], 0.0), axis=(2, 3))]
    unnamed x9 -> x26, local copies, waits for them, and re-layouts: 2.59 us -> 4.21 us
  transfers between devices with their start and end apart: 2 -> 15, of which waited for: 1 -> 8; matrix products, arithmetic and copies ran while one was open for 4% -> 0% of each run, Pallas kernels for 0% -> 0%
where the time goes in v1:
time: 85.7 us; the launch traced here: 85.3 us
  waiting for transfers between devices  35.7 us (42%)
  starting transfers between devices  23.4 us (27%)
  Pallas kernels  17.6 us (21%)
  local copies, waits for them, and re-layouts  4.97 us (6%)
  other arithmetic  2.84 us (3%)
    ppermute x14, waiting for transfers between devices, send(): return lax.ppermute(x, 'expert', route)  33.6 us
    ppermute x14, starting transfers between devices, send(): return lax.ppermute(x, 'expert', route)  21.7 us
    pallas_call x1, Pallas kernels, ffn(): pl.pallas_call(functools.partial(ffn_kernel, groups, experts), out_shape=...  13.4 us
    unnamed x26, local copies, waits for them, and re-layouts  4.21 us
    pallas_call x1, Pallas kernels, body(): pl.pallas_call(functools.partial(finish_kernel, len(parts)), out_shape=(j...  2.11 us
    pallas_call x1, Pallas kernels, body(): pl.pallas_call(functools.partial(prep_kernel, experts), out_shape=jax.Sha...  2.1 us
    ppermute x1, waiting for transfers between devices, body(): lax.ppermute(seq_score, 'dp', [(d, d ^ count // 2) for d in range(count)])  2.06 us
  transfers between devices with their start and end apart: 15, of which 8 were waited for; matrix products, arithmetic and copies ran while one was open for 0% of the time, Pallas kernels for 0%

profile of v1, /device:TPU:0, one launch (start us, length us, event | category | flops | bytes accessed | tf_op | source)
XLA Modules:
  0.0 85.3 jit_solution(9994467078388306088)
XLA Ops:
  0.6 1.4 %copy.11.ids_ref = s32[64,8]{1,0:T(8,128)} copy(s32[64,8]{0,1:T(8,128)} %param.10) | data formatting | bytes 4096 | tf_op args[1]
  2.0 1.4 %copy.12.gate_ref = s32[64,8]{1,0:T(8,128)} copy(s32[64,8]{0,1:T(8,128)} %param.11) | data formatting | bytes 4096 | tf_op args[2]
  3.4 2.1 %prep.1.refs_0_ = bf16[64,2176]{1,0:T(8,128)(2,1)} custom-call(bf16[64,2048]{1,0:T(8,128)(2,1)} %tok_ref.1, s32[64,8]{1,0:T(8,128)} %copy.11.ids_ref, s32[64,8]{1,0:T(8,128)} %copy.12.gate_ref, s32[4]{0:T(128)} %scorer_ref.1, bf16[2,2048]{1,0:T(2,128)(2,1)} %tags_ref.1), custom_call_target="tpu_custom_call" | custom-call | tf_op jit(solution)/shard_map/prep/pallas_call | solution.py:161
  5.5 4.0 %collective-permute-start.3 = (bf16[64,2176]{1,0:T(8,128)(2,1)}, bf16[64,2176]{1,0:T(8,128)(2,1)S(1)}, u32[]{:S(2)}, u32[]{:S(2)}) collective-permute-start(bf16[64,2176]{1,0:T(8,128)(2,1)} %prep.1.refs_0_), channel_id=1, source_target_pairs={{0,4},{1,5},{2,6},{3,7},{4,0},{5,1},{6,2},{7,3},{8,12},{9,13},{10,... | collective-permute-start | bytes 835592 | tf_op jit(solution)/shard_map/ppermute | solution.py:153
  9.5 0.7 collective-permute-start.5
  10.2 2.9 %collective-permute-start.1 = (bf16[64,2176]{1,0:T(8,128)(2,1)}, bf16[64,2176]{1,0:T(8,128)(2,1)S(1)}, u32[]{:S(2)}, u32[]{:S(2)}) collective-permute-start(bf16[64,2176]{1,0:T(8,128)(2,1)} %prep.1.refs_0_), channel_id=1, source_target_pairs={{0,2},{1,3},{2,0},{3,1},{4,6},{5,7},{6,4},{7,5},{8,10},{9,11},{10,... | collective-permute-start | bytes 835592 | tf_op jit(solution)/shard_map/ppermute | solution.py:153
  13.1 10.2 %collective-permute-done.3.refs_4_ = bf16[64,2176]{1,0:T(8,128)(2,1)S(1)} collective-permute-done((bf16[64,2176]{1,0:T(8,128)(2,1)}, bf16[64,2176]{1,0:T(8,128)(2,1)S(1)}, u32[]{:S(2)}, u32[]{:S(2)}) %collective-permute-start.3) | collective-permute-done | bytes 278560 | tf_op jit(solution)/shard_map/ppermute | solution.py:153
  23.2 0.0 copy-start
  23.2 1.3 %collective-permute-start.6 = (bf16[64,2176]{1,0:T(8,128)(2,1)S(1)}, bf16[64,2176]{1,0:T(8,128)(2,1)S(1)}, u32[]{:S(2)}, u32[]{:S(2)}) collective-permute-start(bf16[64,2176]{1,0:T(8,128)(2,1)S(1)} %collective-permute-done.3.refs_4_), channel_id=1, source_target_pairs={{2,0},{3,1},{4,6},{5,7},{10,8},{11,9},{12,14},{13,15},{18,16},{19,... | collective-permute-start | bytes 835592 | tf_op jit(solution)/shard_map/ppermute | solution.py:153
  24.5 0.1 collective-permute-start
  24.6 0.5 collective-permute-start.4
  25.1 0.0 collective-permute-done.5.refs_6_
  25.1 0.0 copy-start.1
  25.1 0.1 collective-permute-start.7
  25.2 0.0 collective-permute-done.1.refs_2_
  25.2 0.0 copy-start.2
  25.2 0.4 collective-permute-start.2
  25.6 6.5 %collective-permute-done.6.refs_7_ = bf16[64,2176]{1,0:T(8,128)(2,1)S(1)} collective-permute-done((bf16[64,2176]{1,0:T(8,128)(2,1)S(1)}, bf16[64,2176]{1,0:T(8,128)(2,1)S(1)}, u32[]{:S(2)}, u32[]{:S(2)}) %collective-permute-start.6) | collective-permute-done | bytes 278560 | tf_op jit(solution)/shard_map/ppermute | solution.py:153
  32.1 0.0 copy-start.3
  32.1 0.0 collective-permute-start.8
  32.1 0.0 collective-permute-done.refs_1_
  32.1 0.0 copy-start.4
  32.2 0.0 collective-permute-done.7.refs_8_
  32.2 0.0 copy-start.6
  32.2 0.0 collective-permute-done.4.refs_5_
  32.2 0.0 copy-start.5
  32.2 0.0 collective-permute-done.2.refs_3_
  32.2 0.0 copy-start.7
  32.2 1.5 %collective-permute-done.8.refs_9_ = bf16[64,2176]{1,0:T(8,128)(2,1)S(1)} collective-permute-done((bf16[64,2176]{1,0:T(8,128)(2,1)S(1)}, bf16[64,2176]{1,0:T(8,128)(2,1)S(1)}, u32[]{:S(2)}, u32[]{:S(2)}) %collective-permute-start.8) | collective-permute-done | bytes 278560 | tf_op jit(solution)/shard_map/ppermute | solution.py:153
  33.7 0.0 copy-done
  33.7 0.0 copy-done.1
  33.7 0.0 copy-done.2
  33.7 0.0 copy-done.3
  33.7 0.0 copy-done.4
  33.7 0.0 copy-done.6
  33.7 0.0 copy-done.5
  33.7 0.0 copy-done.7
  33.8 0.0 copy-start.8
  33.8 0.7 copy-done.8
  34.5 13.4 %ffn.1 = (bf16[4,64,2048]{2,1,0:T(8,128)(2,1)}, bf16[4,64,2048]{2,1,0:T(8,128)(2,1)}) custom-call(bf16[64,2176]{1,0:T(8,128)(2,1)} %prep.1.refs_0_, bf16[64,2176]{1,0:T(8,128)(2,1)} %copy-done.4, bf16[64,2176]{1,0:T(8,128)(2,1)} %copy-done.2, bf16[64,2176]{1,0:T(8,128)(2,1)} %copy-done.7, bf16[64,2176]{1,0:T(8,128)(2,1)} %copy-done, ...), custom_call_target="tpu_custom_call" | custom-call | flops 4831838208 | bytes 25165824 | tf_op jit(solution)/shard_map/ffn/pallas_call | solution.py:115
  47.9 0.2 collective-permute-start.9
  48.1 2.8 %collective-permute-done.9 = bf16[4,64,2048]{2,1,0:T(8,128)(2,1)S(1)} collective-permute-done((bf16[4,64,2048]{2,1,0:T(8,128)(2,1)}, bf16[4,64,2048]{2,1,0:T(8,128)(2,1)S(1)}, u32[]{:S(2)}, u32[]{:S(2)}) %collective-permute-start.9) | collective-permute-done | bytes 1048608 | tf_op jit(solution)/shard_map/ppermute | solution.py:153
  50.8 1.6 %add_convert_fusion = bf16[4,64,2048]{2,1,0:T(8,128)(2,1)S(1)} fusion(bf16[4,64,2048]{2,1,0:T(8,128)(2,1)S(1)} %collective-permute-done.9, bf16[4,64,2048]{2,1,0:T(8,128)(2,1)} %get-tuple-element.6), kind=kLoop, calls=%fused_computation | loop fusion | flops 2097152 | bytes 3145728 | tf_op jit(solution)/shard_map/convert_element_type | solution.py:195
  52.4 0.8 slice_bitcast_fusion.1
  53.2 1.4 %collective-permute-start.12 = (bf16[64,2048]{1,0:T(8,128)(2,1)S(1)}, bf16[64,2048]{1,0:T(8,128)(2,1)S(1)}, u32[]{:S(2)}, u32[]{:S(2)}) collective-permute-start(bf16[64,2048]{1,0:T(8,128)(2,1)S(1)} %get-tuple-element.10), channel_id=1, source_target_pairs={{0,2},{1,3},{6,4},{7,5},{8,10},{9,11},{14,12},{15,13},{16,18},{17,... | collective-permute-start | bytes 786440 | tf_op jit(solution)/shard_map/ppermute | solution.py:153
  54.6 0.7 collective-permute-start.11
  55.3 4.1 %collective-permute-start.10 = (bf16[64,2048]{1,0:T(8,128)(2,1)S(1)}, bf16[64,2048]{1,0:T(8,128)(2,1)S(1)}, u32[]{:S(2)}, u32[]{:S(2)}) collective-permute-start(bf16[64,2048]{1,0:T(8,128)(2,1)S(1)} %get-tuple-element.11), channel_id=1, source_target_pairs={{0,2},{1,3},{2,0},{3,1},{4,6},{5,7},{6,4},{7,5},{8,10},{9,11},{10,... | collective-permute-start | bytes 786440 | tf_op jit(solution)/shard_map/ppermute | solution.py:153
  59.4 1.9 %collective-permute-done.12 = bf16[64,2048]{1,0:T(8,128)(2,1)S(1)} collective-permute-done((bf16[64,2048]{1,0:T(8,128)(2,1)S(1)}, bf16[64,2048]{1,0:T(8,128)(2,1)S(1)}, u32[]{:S(2)}, u32[]{:S(2)}) %collective-permute-start.12) | collective-permute-done | bytes 262176 | tf_op jit(solution)/shard_map/ppermute | solution.py:153
  61.3 0.1 fusion
  61.3 5.4 %collective-permute-start.13 = (bf16[64,2048]{1,0:T(8,128)(2,1)S(1)}, bf16[64,2048]{1,0:T(8,128)(2,1)S(1)}, u32[]{:S(2)}, u32[]{:S(2)}) collective-permute-start(bf16[64,2048]{1,0:T(8,128)(2,1)S(1)} %fusion), channel_id=1, source_target_pairs={{0,4},{1,5},{2,6},{3,7},{4,0},{5,1},{6,2},{7,3},{8,12},{9,13},{10,... | collective-permute-start | bytes 786440 | tf_op jit(solution)/shard_map/ppermute | solution.py:153
  66.7 0.2 collective-permute-done.10.refs_1_
  66.9 0.0 copy-start.10
  66.9 0.0 collective-permute-done.11.refs_2_
  66.9 0.0 copy-start.9
  66.9 10.7 %collective-permute-done.13.refs_3_ = bf16[64,2048]{1,0:T(8,128)(2,1)S(1)} collective-permute-done((bf16[64,2048]{1,0:T(8,128)(2,1)S(1)}, bf16[64,2048]{1,0:T(8,128)(2,1)S(1)}, u32[]{:S(2)}, u32[]{:S(2)}) %collective-permute-start.13) | collective-permute-done | bytes 262176 | tf_op jit(solution)/shard_map/ppermute | solution.py:153
  77.5 0.0 copy-start.11
  77.6 0.0 copy-done.10
  77.6 0.0 copy-done.9
  77.6 0.7 copy-done.11
  78.3 2.1 %finish.1 = (bf16[64,2048]{1,0:T(8,128)(2,1)}, f32[4]{0:T(128)}) custom-call(bf16[64,2048]{1,0:T(8,128)(2,1)} %get-tuple-element.12.refs_0_, bf16[64,2048]{1,0:T(8,128)(2,1)} %copy-done.10, bf16[64,2048]{1,0:T(8,128)(2,1)} %copy-done.9, bf16[64,2048]{1,0:T(8,128)(2,1)} %copy-done.11, f32[1,2048]{1,0:T(1,128)} %bitcast.12), custom_call_target="tpu_custom_call" | custom-call | tf_op jit(solution)/shard_map/finish/pallas_call | solution.py:202
  80.4 1.7 %collective-permute-start.14 = (f32[4]{0:T(128)}, f32[4]{0:T(128)S(1)}, u32[]{:S(2)}, u32[]{:S(2)}) collective-permute-start(f32[4]{0:T(128)} %get-tuple-element.9), channel_id=1, source_target_pairs={{0,16},{8,24},{16,0},{24,8},{1,17},{9,25},{17,1},{25,9},{2,18},{10... | collective-permute-start | bytes 56 | tf_op jit(solution)/shard_map/ppermute | solution.py:213
  82.1 2.1 %collective-permute-done.14 = f32[4]{0:T(128)S(1)} collective-permute-done((f32[4]{0:T(128)}, f32[4]{0:T(128)S(1)}, u32[]{:S(2)}, u32[]{:S(2)}) %collective-permute-start.14) | collective-permute-done | bytes 48 | tf_op jit(solution)/shard_map/ppermute | solution.py:213
  84.1 1.2 %multiply_add_fusion = f32[4]{0:T(128)} fusion(f32[4]{0:T(128)} %get-tuple-element.9, f32[4]{0:T(128)S(1)} %collective-permute-done.14), kind=kLoop, calls=%fused_computation.7 | loop fusion | flops 20 | bytes 48 | tf_op jit(solution)/shard_map/add | solution.py:214
Async XLA Ops:
  5.5 17.7 %collective-permute-start.3 = (bf16[64,2176]{1,0:T(8,128)(2,1)}, bf16[64,2176]{1,0:T(8,128)(2,1)S(1)}, u32[]{:S(2)}, u32[]{:S(2)}) collective-permute-start(bf16[64,2176]{1,0:T(8,128)(2,1)} %prep.1.refs_0_), channel_id=1, source_target_pairs={{0,4},{1,5},{2,6},{3,7},{4,0},{5,1},{6,2},{7,3},{8,12},{9,13},{10,... | collective-permute-start | bytes 835592 | tf_op jit(solution)/shard_map/ppermute | solution.py:153
  9.5 15.6 %collective-permute-start.5 = (bf16[64,2176]{1,0:T(8,128)(2,1)}, bf16[64,2176]{1,0:T(8,128)(2,1)S(1)}, u32[]{:S(2)}, u32[]{:S(2)}) collective-permute-start(bf16[64,2176]{1,0:T(8,128)(2,1)} %prep.1.refs_0_), channel_id=1, source_target_pairs={{2,4},{3,5},{4,2},{5,3},{10,12},{11,13},{12,10},{13,11},{18,20},{1... | collective-permute-start | bytes 835592 | tf_op jit(solution)/shard_map/ppermute | solution.py:153
  10.2 15.0 %collective-permute-start.1 = (bf16[64,2176]{1,0:T(8,128)(2,1)}, bf16[64,2176]{1,0:T(8,128)(2,1)S(1)}, u32[]{:S(2)}, u32[]{:S(2)}) collective-permute-start(bf16[64,2176]{1,0:T(8,128)(2,1)} %prep.1.refs_0_), channel_id=1, source_target_pairs={{0,2},{1,3},{2,0},{3,1},{4,6},{5,7},{6,4},{7,5},{8,10},{9,11},{10,... | collective-permute-start | bytes 835592 | tf_op jit(solution)/shard_map/ppermute | solution.py:153
  23.2 10.5 %copy-start = (bf16[64,2176]{1,0:T(8,128)(2,1)}, bf16[64,2176]{1,0:T(8,128)(2,1)S(1)}, u32[]{:S(2)}) copy-start(bf16[64,2176]{1,0:T(8,128)(2,1)S(1)} %collective-permute-done.3.refs_4_) | copy-start | bytes 835588
  23.2 8.9 %collective-permute-start.6 = (bf16[64,2176]{1,0:T(8,128)(2,1)S(1)}, bf16[64,2176]{1,0:T(8,128)(2,1)S(1)}, u32[]{:S(2)}, u32[]{:S(2)}) collective-permute-start(bf16[64,2176]{1,0:T(8,128)(2,1)S(1)} %collective-permute-done.3.refs_4_), channel_id=1, source_target_pairs={{2,0},{3,1},{4,6},{5,7},{10,8},{11,9},{12,14},{13,15},{18,16},{19,... | collective-permute-start | bytes 835592 | tf_op jit(solution)/shard_map/ppermute | solution.py:153
  24.5 7.6 %collective-permute-start = (bf16[64,2176]{1,0:T(8,128)(2,1)}, bf16[64,2176]{1,0:T(8,128)(2,1)S(1)}, u32[]{:S(2)}, u32[]{:S(2)}) collective-permute-start(bf16[64,2176]{1,0:T(8,128)(2,1)} %prep.1.refs_0_), channel_id=1, source_target_pairs={{0,1},{1,0},{2,3},{3,2},{4,5},{5,4},{6,7},{7,6},{8,9},{9,8},{10,11... | collective-permute-start | bytes 835592 | tf_op jit(solution)/shard_map/ppermute | solution.py:153
  24.6 7.6 %collective-permute-start.4 = (bf16[64,2176]{1,0:T(8,128)(2,1)S(1)}, bf16[64,2176]{1,0:T(8,128)(2,1)S(1)}, u32[]{:S(2)}, u32[]{:S(2)}) collective-permute-start(bf16[64,2176]{1,0:T(8,128)(2,1)S(1)} %collective-permute-done.3.refs_4_), channel_id=1, source_target_pairs={{0,1},{1,0},{2,3},{3,2},{4,5},{5,4},{6,7},{7,6},{8,9},{9,8},{10,11... | collective-permute-start | bytes 835592 | tf_op jit(solution)/shard_map/ppermute | solution.py:153
  25.1 8.6 %copy-start.1 = (bf16[64,2176]{1,0:T(8,128)(2,1)}, bf16[64,2176]{1,0:T(8,128)(2,1)S(1)}, u32[]{:S(2)}) copy-start(bf16[64,2176]{1,0:T(8,128)(2,1)S(1)} %collective-permute-done.5.refs_6_) | copy-start | bytes 835588
  25.1 7.1 %collective-permute-start.7 = (bf16[64,2176]{1,0:T(8,128)(2,1)S(1)}, bf16[64,2176]{1,0:T(8,128)(2,1)S(1)}, u32[]{:S(2)}, u32[]{:S(2)}) collective-permute-start(bf16[64,2176]{1,0:T(8,128)(2,1)S(1)} %collective-permute-done.5.refs_6_), channel_id=1, source_target_pairs={{0,1},{1,0},{2,3},{3,2},{4,5},{5,4},{6,7},{7,6},{8,9},{9,8},{10,11... | collective-permute-start | bytes 835592 | tf_op jit(solution)/shard_map/ppermute | solution.py:153
  25.2 8.5 %copy-start.2 = (bf16[64,2176]{1,0:T(8,128)(2,1)}, bf16[64,2176]{1,0:T(8,128)(2,1)S(1)}, u32[]{:S(2)}) copy-start(bf16[64,2176]{1,0:T(8,128)(2,1)S(1)} %collective-permute-done.1.refs_2_) | copy-start | bytes 835588
  25.2 7.0 %collective-permute-start.2 = (bf16[64,2176]{1,0:T(8,128)(2,1)S(1)}, bf16[64,2176]{1,0:T(8,128)(2,1)S(1)}, u32[]{:S(2)}, u32[]{:S(2)}) collective-permute-start(bf16[64,2176]{1,0:T(8,128)(2,1)S(1)} %collective-permute-done.1.refs_2_), channel_id=1, source_target_pairs={{0,1},{1,0},{2,3},{3,2},{4,5},{5,4},{6,7},{7,6},{8,9},{9,8},{10,11... | collective-permute-start | bytes 835592 | tf_op jit(solution)/shard_map/ppermute | solution.py:153
  32.1 1.6 %copy-start.3 = (bf16[64,2176]{1,0:T(8,128)(2,1)}, bf16[64,2176]{1,0:T(8,128)(2,1)S(1)}, u32[]{:S(2)}) copy-start(bf16[64,2176]{1,0:T(8,128)(2,1)S(1)} %collective-permute-done.6.refs_7_) | copy-start | bytes 835588
  32.1 1.6 %collective-permute-start.8 = (bf16[64,2176]{1,0:T(8,128)(2,1)S(1)}, bf16[64,2176]{1,0:T(8,128)(2,1)S(1)}, u32[]{:S(2)}, u32[]{:S(2)}) collective-permute-start(bf16[64,2176]{1,0:T(8,128)(2,1)S(1)} %collective-permute-done.6.refs_7_), channel_id=1, source_target_pairs={{0,1},{1,0},{2,3},{3,2},{4,5},{5,4},{6,7},{7,6},{8,9},{9,8},{10,11... | collective-permute-start | bytes 835592 | tf_op jit(solution)/shard_map/ppermute | solution.py:153
  32.1 1.6 %copy-start.4 = (bf16[64,2176]{1,0:T(8,128)(2,1)}, bf16[64,2176]{1,0:T(8,128)(2,1)S(1)}, u32[]{:S(2)}) copy-start(bf16[64,2176]{1,0:T(8,128)(2,1)S(1)} %collective-permute-done.refs_1_) | copy-start | bytes 835588
  32.2 1.6 %copy-start.6 = (bf16[64,2176]{1,0:T(8,128)(2,1)}, bf16[64,2176]{1,0:T(8,128)(2,1)S(1)}, u32[]{:S(2)}) copy-start(bf16[64,2176]{1,0:T(8,128)(2,1)S(1)} %collective-permute-done.7.refs_8_) | copy-start | bytes 835588
  32.2 1.6 %copy-start.5 = (bf16[64,2176]{1,0:T(8,128)(2,1)}, bf16[64,2176]{1,0:T(8,128)(2,1)S(1)}, u32[]{:S(2)}) copy-start(bf16[64,2176]{1,0:T(8,128)(2,1)S(1)} %collective-permute-done.4.refs_5_) | copy-start | bytes 835588
  32.2 1.5 %copy-start.7 = (bf16[64,2176]{1,0:T(8,128)(2,1)}, bf16[64,2176]{1,0:T(8,128)(2,1)S(1)}, u32[]{:S(2)}) copy-start(bf16[64,2176]{1,0:T(8,128)(2,1)S(1)} %collective-permute-done.2.refs_3_) | copy-start | bytes 835588
  33.8 0.7 copy-start.8
  47.9 2.9 %collective-permute-start.9 = (bf16[4,64,2048]{2,1,0:T(8,128)(2,1)}, bf16[4,64,2048]{2,1,0:T(8,128)(2,1)S(1)}, u32[]{:S(2)}, u32[]{:S(2)}) collective-permute-start(bf16[4,64,2048]{2,1,0:T(8,128)(2,1)} %get-tuple-element.7), channel_id=1, source_target_pairs={{0,1},{1,0},{2,3},{3,2},{4,5},{5,4},{6,7},{7,6},{8,9},{9,8},{10,11... | collective-permute-start | bytes 3145736 | tf_op jit(solution)/shard_map/ppermute | solution.py:153
  53.2 8.1 %collective-permute-start.12 = (bf16[64,2048]{1,0:T(8,128)(2,1)S(1)}, bf16[64,2048]{1,0:T(8,128)(2,1)S(1)}, u32[]{:S(2)}, u32[]{:S(2)}) collective-permute-start(bf16[64,2048]{1,0:T(8,128)(2,1)S(1)} %get-tuple-element.10), channel_id=1, source_target_pairs={{0,2},{1,3},{6,4},{7,5},{8,10},{9,11},{14,12},{15,13},{16,18},{17,... | collective-permute-start | bytes 786440 | tf_op jit(solution)/shard_map/ppermute | solution.py:153
  54.6 12.2 %collective-permute-start.11 = (bf16[64,2048]{1,0:T(8,128)(2,1)S(1)}, bf16[64,2048]{1,0:T(8,128)(2,1)S(1)}, u32[]{:S(2)}, u32[]{:S(2)}) collective-permute-start(bf16[64,2048]{1,0:T(8,128)(2,1)S(1)} %get-tuple-element.10), channel_id=1, source_target_pairs={{2,4},{3,5},{4,2},{5,3},{10,12},{11,13},{12,10},{13,11},{18,20},{1... | collective-permute-start | bytes 786440 | tf_op jit(solution)/shard_map/ppermute | solution.py:153
  55.3 11.5 %collective-permute-start.10 = (bf16[64,2048]{1,0:T(8,128)(2,1)S(1)}, bf16[64,2048]{1,0:T(8,128)(2,1)S(1)}, u32[]{:S(2)}, u32[]{:S(2)}) collective-permute-start(bf16[64,2048]{1,0:T(8,128)(2,1)S(1)} %get-tuple-element.11), channel_id=1, source_target_pairs={{0,2},{1,3},{2,0},{3,1},{4,6},{5,7},{6,4},{7,5},{8,10},{9,11},{10,... | collective-permute-start | bytes 786440 | tf_op jit(solution)/shard_map/ppermute | solution.py:153
  61.3 16.2 %collective-permute-start.13 = (bf16[64,2048]{1,0:T(8,128)(2,1)S(1)}, bf16[64,2048]{1,0:T(8,128)(2,1)S(1)}, u32[]{:S(2)}, u32[]{:S(2)}) collective-permute-start(bf16[64,2048]{1,0:T(8,128)(2,1)S(1)} %fusion), channel_id=1, source_target_pairs={{0,4},{1,5},{2,6},{3,7},{4,0},{5,1},{6,2},{7,3},{8,12},{9,13},{10,... | collective-permute-start | bytes 786440 | tf_op jit(solution)/shard_map/ppermute | solution.py:153
  66.9 10.7 %copy-start.10 = (bf16[64,2048]{1,0:T(8,128)(2,1)}, bf16[64,2048]{1,0:T(8,128)(2,1)S(1)}, u32[]{:S(2)}) copy-start(bf16[64,2048]{1,0:T(8,128)(2,1)S(1)} %collective-permute-done.10.refs_1_) | copy-start | bytes 786436
  66.9 10.7 %copy-start.9 = (bf16[64,2048]{1,0:T(8,128)(2,1)}, bf16[64,2048]{1,0:T(8,128)(2,1)S(1)}, u32[]{:S(2)}) copy-start(bf16[64,2048]{1,0:T(8,128)(2,1)S(1)} %collective-permute-done.11.refs_2_) | copy-start | bytes 786436
  77.5 0.7 copy-start.11
  80.4 3.7 %collective-permute-start.14 = (f32[4]{0:T(128)}, f32[4]{0:T(128)S(1)}, u32[]{:S(2)}, u32[]{:S(2)}) collective-permute-start(f32[4]{0:T(128)} %get-tuple-element.9), channel_id=1, source_target_pairs={{0,16},{8,24},{16,0},{24,8},{1,17},{9,25},{17,1},{25,9},{2,18},{10... | collective-permute-start | bytes 56 | tf_op jit(solution)/shard_map/ppermute | solution.py:213

commit v2 on v1

v2 whole, which is shorter than its diff:
```python
import functools

import jax
import jax.numpy as jnp
from jax import lax
from jax.experimental import pallas as pl
from jax.experimental.pallas import tpu as pltpu
from jax.sharding import PartitionSpec as P

SEQ_LEN = 16
MOST = 24
META = 128
MIB = 1 << 20

VMEM = pl.BlockSpec(memory_space=pltpu.VMEM)
SMEM = pl.BlockSpec(memory_space=pltpu.SMEM)
HBM = pl.BlockSpec(memory_space=pltpu.HBM)


def prep_kernel(experts, tok_ref, ids_ref, gate_ref, scorer_ref, tags_ref, out_ref):
    rows, width = tok_ref.shape
    for s in range(rows // SEQ_LEN):
        span = pl.ds(s * SEQ_LEN, SEQ_LEN)
        tag = jnp.where(scorer_ref[s] == 1, tags_ref[1:2, :], tags_ref[0:1, :]).astype(jnp.float32)
        out_ref[span, 0:width] = (tok_ref[span, :].astype(jnp.float32) + tag).astype(jnp.bfloat16)
    fixed = gate_ref[...].astype(jnp.float32)
    weight = fixed / jnp.sum(fixed, axis=0, keepdims=True)
    high = weight.astype(jnp.bfloat16).astype(jnp.float32)
    low = weight - high
    ids = ids_ref[...]
    place = lax.broadcasted_iota(jnp.int32, (META, rows), 0)
    meta = jnp.zeros((META, rows), jnp.float32)
    for k in range(ids.shape[0]):
        one = ids[k : k + 1, :]
        meta = meta + jnp.where(place == one, high[k : k + 1, :], 0.0)
        meta = meta + jnp.where(place == one + experts, low[k : k + 1, :], 0.0)
    out_ref[:, width : width + META] = meta.T.astype(jnp.bfloat16)


def pick_rows(meta, first, per_device, experts):
    rows = meta.shape[0]
    room = 2 * MOST
    lane = lax.broadcasted_iota(jnp.int32, meta.shape, 1)
    routed = (meta > 0) & (lane < experts)
    row = lax.broadcasted_iota(jnp.int32, (rows, rows), 0)
    col = lax.broadcasted_iota(jnp.int32, (rows, rows), 1)
    earlier = (row > col).astype(jnp.bfloat16)
    rank = jnp.dot(earlier, routed.astype(jnp.bfloat16), preferred_element_type=jnp.float32)
    rank = jnp.where(routed, rank, -1.0)
    slot = lax.broadcasted_iota(jnp.int32, (rows, per_device * room), 1)
    hit = jnp.zeros((rows, per_device * room), jnp.bool_)
    for e in range(per_device):
        mine = jnp.max(jnp.where(lane == first + e, rank, -1.0), axis=1, keepdims=True).astype(jnp.int32)
        hit = hit | ((mine >= 0) & (slot == mine + e * room))
    return hit.astype(jnp.float32).astype(jnp.bfloat16)


def ffn_kernel(chips, experts, *refs):
    x_refs, (wg, wu, wd), refs = refs[: 2 * chips], refs[2 * chips : 2 * chips + 3], refs[2 * chips + 3 :]
    out_refs, (g_ref, pick_ref, o_ref) = refs[: 2 * chips], refs[2 * chips :]
    per_device, width, ff = wg.shape
    room = 2 * MOST
    first = lax.axis_index("expert") * per_device
    for k in range(chips):
        x = jnp.concatenate([x_refs[2 * k][...], x_refs[2 * k + 1][...]], axis=0)
        pick = pick_rows(x[:, width:].astype(jnp.float32), first, per_device, experts)
        pick_ref[k] = pick
        picked = lax.dot_general(pick, x, (((0,), (0,)), ((), ())), preferred_element_type=jnp.float32)
        picked = picked.astype(jnp.bfloat16)
        for e in range(per_device):
            g_ref[e, k * room : (k + 1) * room, :] = picked[e * room : (e + 1) * room, :]
    lane = lax.broadcasted_iota(jnp.int32, (chips * room, META), 1)
    for e in range(per_device):
        x = g_ref[e, :, 0:width]
        meta = g_ref[e, :, width:].astype(jnp.float32)
        mine = (lane == first + e) | (lane == first + e + experts)
        weight = jnp.sum(jnp.where(mine, meta, 0.0), axis=1, keepdims=True)
        gate = jnp.dot(x, wg[e], preferred_element_type=jnp.float32)
        up = jnp.dot(x, wu[e], preferred_element_type=jnp.float32)
        hidden = (gate / (1.0 + jnp.exp(-gate)) * up * weight).astype(jnp.bfloat16)
        out = jnp.dot(hidden, wd[e], preferred_element_type=jnp.float32).astype(jnp.bfloat16)
        for k in range(chips):
            o_ref[k, e * room : (e + 1) * room, :] = out[k * room : (k + 1) * room, :]
    for k in range(chips):
        rows = jnp.dot(pick_ref[k], o_ref[k], preferred_element_type=jnp.float32).astype(jnp.bfloat16)
        half = rows.shape[0] // 2
        out_refs[2 * k][...] = rows[:half]
        out_refs[2 * k + 1][...] = rows[half:]


def far_memory(x):
    return pltpu.with_memory_space_constraint(x, pltpu.HBM)


def load_kernel(x_ref, *refs):
    count = (len(refs) - 1) // 2
    sems = refs[-1]
    copies = []
    for j in range(count):
        for e in range(refs[j].shape[0]):
            copy = pltpu.make_async_copy(refs[j].at[e], refs[count + j].at[e], sems.at[j, e])
            copy.start()
            copies.append(copy)
    for copy in copies:
        copy.wait()


def load(after, *arrays):
    return pl.pallas_call(
        load_kernel,
        out_shape=[pltpu.VMEM(a.shape, a.dtype) for a in arrays],
        in_specs=[VMEM] + [HBM] * len(arrays),
        out_specs=[VMEM] * len(arrays),
        scratch_shapes=[pltpu.SemaphoreType.DMA((len(arrays), arrays[0].shape[0]))],
        compiler_params=pltpu.CompilerParams(vmem_limit_bytes=MIB),
        cost_estimate=pl.CostEstimate(
            flops=0, bytes_accessed=sum(a.size * a.dtype.itemsize for a in arrays), transcendentals=0
        ),
        name="load_weights",
    )(near_memory(after), *map(far_memory, arrays))


def near_memory(x):
    return pltpu.with_memory_space_constraint(x, pltpu.VMEM)


def ffn(name, sources, experts, weights):
    per_device, width, ff = weights[0].shape
    xs = [near_memory(x) for pair in sources for x in pair]
    rows = xs[0].shape[0]
    chips = len(sources)
    room = 2 * MOST
    outs = pl.pallas_call(
        functools.partial(ffn_kernel, chips, experts),
        out_shape=[pltpu.VMEM((rows, width), jnp.bfloat16)] * (2 * chips),
        in_specs=[VMEM] * (len(xs) + 3),
        out_specs=[VMEM] * (2 * chips),
        scratch_shapes=[
            pltpu.VMEM((per_device, chips * room, width + META), jnp.bfloat16),
            pltpu.VMEM((chips, 2 * rows, per_device * room), jnp.bfloat16),
            pltpu.VMEM((chips, per_device * room, width), jnp.bfloat16),
        ],
        compiler_params=pltpu.CompilerParams(vmem_limit_bytes=16 * MIB),
        cost_estimate=pl.CostEstimate(
            flops=6 * per_device * chips * room * width * ff,
            bytes_accessed=6 * per_device * width * ff,
            transcendentals=0,
        ),
        name=name,
    )(*xs, *map(near_memory, weights))
    return [(outs[2 * k], outs[2 * k + 1]) for k in range(chips)]


def finish_kernel(n_parts, *refs):
    parts, head_ref, mixed_ref, score_ref = refs[:n_parts], *refs[n_parts:]
    rows = mixed_ref.shape[0]
    total = parts[0][...].astype(jnp.float32)
    for part in parts[1:]:
        total = total + part[...].astype(jnp.float32)
    mixed = total.astype(jnp.bfloat16)
    mixed_ref[...] = mixed
    for s, score in enumerate(sequence_scores(mixed, head_ref[...])):
        score_ref[s] = score


def sequence_scores(rows, head):
    scored = rows.astype(jnp.float32) * head
    return [jnp.sum(scored[at : at + SEQ_LEN, :]) for at in range(0, rows.shape[0], SEQ_LEN)]


def on_inner_chip():
    chip = lax.axis_index("expert") // 2
    return (chip == 1) | (chip == 2)


def score_tile(tile, row, rows, head):
    at = lax.broadcasted_iota(jnp.int32, tile.shape, 0)
    lane = lax.broadcasted_iota(jnp.int32, tile.shape, 1)
    for s, score in enumerate(sequence_scores(rows, head)):
        tile = jnp.where((at == row) & (lane == s), score, tile)
    return tile


def own_kernel(own_ref, swapped_ref, near_ref, relayed_ref, head_ref, sum_ref, joins_ref, score_ref):
    relayed = relayed_ref[...]
    inner = on_inner_chip()
    stays = relayed.astype(jnp.float32) * jnp.where(inner, 0.0, 1.0)
    joins_ref[...] = (relayed.astype(jnp.float32) * jnp.where(inner, 1.0, 0.0)).astype(jnp.bfloat16)
    own = own_ref[...].astype(jnp.float32) + swapped_ref[...].astype(jnp.float32) + stays
    sum_ref[...] = own
    head = head_ref[...]
    tile = score_tile(jnp.zeros(score_ref.shape, jnp.float32), 0, near_ref[...], head)
    score_ref[...] = score_tile(tile, 2, own, head)


def third_kernel(same_ref, swapped_ref, joins_ref, score_ref, head_ref, back_ref, out_score_ref):
    back = same_ref[...].astype(jnp.float32) + swapped_ref[...].astype(jnp.float32)
    back = (back + joins_ref[...].astype(jnp.float32)).astype(jnp.bfloat16)
    back_ref[...] = back
    out_score_ref[...] = score_tile(score_ref[...], 1, back, head_ref[...])


def both_kernel(score_ref, partner_ref, both_ref):
    both_ref[0] = score_ref[...]
    both_ref[1] = partner_ref[...]


def last_kernel(sum_ref, near_ref, third_ref, both_ref, from_near_ref, from_third_ref, mixed_ref, pair_ref):
    total = sum_ref[...] + near_ref[...].astype(jnp.float32) + third_ref[...].astype(jnp.float32)
    mixed_ref[...] = total.astype(jnp.bfloat16)
    own, partner = (from_near_ref[i, 0:1] + from_third_ref[i, 1:2] + both_ref[i, 2:3] for i in (0, 1))
    pair = jnp.abs(own - partner) + 0.5 * (own + partner)
    lane = lax.broadcasted_iota(jnp.int32, pair.shape, 1)
    for s in range(pair_ref.shape[0]):
        pair_ref[s] = jnp.sum(jnp.where(lane == s, pair, 0.0))


def local_call(kernel, name, out_shape, *xs, out_specs=None):
    return pl.pallas_call(
        kernel,
        out_shape=out_shape,
        in_specs=[VMEM] * len(xs),
        out_specs=out_specs or [VMEM] * len(out_shape),
        compiler_params=pltpu.CompilerParams(vmem_limit_bytes=16 * MIB),
        name=name,
    )(*map(near_memory, xs))


def send(x, route):
    return lax.ppermute(x, "expert", route)


def body(tokens, expert_ids, gate_fixed, scorer_id, direction_tags, w_gate, w_up, w_down, score_head):
    devices = lax.axis_size("expert")
    chips = devices // 2
    experts = w_gate.shape[0] * devices
    rows, width = tokens.shape
    x = pl.pallas_call(
        functools.partial(prep_kernel, experts),
        out_shape=pltpu.VMEM((rows, width + META), jnp.bfloat16),
        in_specs=[VMEM, VMEM, VMEM, SMEM, VMEM],
        out_specs=VMEM,
        name="prep",
    )(tokens, expert_ids.T, gate_fixed.T, scorer_id, direction_tags)
    weights = load(x, w_gate, w_up, w_down)

    def exchange(block, k):
        return send(block, [(d, d ^ (2 * k)) for d in range(devices)])

    def core_swap(block):
        return send(block, [(d, d ^ 1) for d in range(devices)])

    def pair(block):
        return block, core_swap(block)

    def partner_of(block):
        count = lax.axis_size("dp")
        return lax.ppermute(block, "dp", [(d, d ^ (count // 2)) for d in range(count)])

    def chip_sum(sums):
        same, other = sums
        return (same.astype(jnp.float32) + core_swap(other).astype(jnp.float32)).astype(jnp.bfloat16)

    def chip_route(*pairs):
        return [(2 * a + c, 2 * b + c) for a, b in pairs for c in (0, 1)]

    if chips == 4:
        far = exchange(x, 2)
        near = exchange(x, 1)
        x_pair = pair(x)
        far, near, x_pair, *weights = lax.optimization_barrier((far, near, x_pair, *weights))
        third = send(x_pair[0], chip_route((1, 2), (2, 1))) + send(far, chip_route((1, 0), (2, 3)))
        own_sums, near_sums, far_sums = ffn("experts_1", [x_pair, pair(near), pair(far)], experts, weights)
        far_back = chip_sum(far_sums)
        third_pair, far_back = lax.optimization_barrier((pair(third), far_back))
        relayed = send(far_back, chip_route((1, 3), (2, 0), (0, 1), (3, 2)))
        (third_sums,) = ffn("experts_2", [third_pair], experts, weights)
        near_back = chip_sum(near_sums)
        head = score_head.reshape(1, width)
        scores = (8, META)
        own_sum, joins, score = local_call(
            own_kernel,
            "own_sum",
            [
                pltpu.VMEM((rows, width), jnp.float32),
                pltpu.VMEM((rows, width), jnp.bfloat16),
                pltpu.VMEM(scores, jnp.float32),
            ],
            *(own_sums[0], core_swap(own_sums[1]), near_back, relayed, head),
        )
        third_same, third_other = third_sums
        third_other, joins = lax.optimization_barrier((third_other, joins))
        third_back, score = local_call(
            third_kernel,
            "third_back",
            [pltpu.VMEM((rows, width), jnp.bfloat16), pltpu.VMEM(scores, jnp.float32)],
            *(third_same, core_swap(third_other), joins, score, head),
        )
        near_back, third_back = lax.optimization_barrier((near_back, third_back))
        third = exchange(third_back, 3)
        near = exchange(near_back, 1)
        (both,) = local_call(
            both_kernel, "both_scores", [pltpu.VMEM((2, *scores), jnp.float32)], score, partner_of(score)
        )
        return local_call(
            last_kernel,
            "mixed",
            [
                jax.ShapeDtypeStruct((rows, width), jnp.bfloat16),
                jax.ShapeDtypeStruct((rows // SEQ_LEN,), jnp.float32),
            ],
            own_sum,
            near,
            third,
            both,
            exchange(both, 1),
            exchange(both, 3),
            out_specs=[VMEM, SMEM],
        )
    held = [x] + [exchange(x, k) for k in range(1, chips)]
    sums = ffn("experts", [pair(b) for b in held], experts, weights)
    parts = [chip_sum(sums[0])] + [exchange(chip_sum(sums[k]), k) for k in range(1, chips)]
    mixed, seq_score = pl.pallas_call(
        functools.partial(finish_kernel, len(parts)),
        out_shape=(
            jax.ShapeDtypeStruct((rows, width), jnp.bfloat16),
            jax.ShapeDtypeStruct((rows // SEQ_LEN,), jnp.float32),
        ),
        in_specs=[VMEM] * len(parts) + [VMEM],
        out_specs=(VMEM, SMEM),
        name="finish",
    )(*parts, score_head.reshape(1, width))
    partner = partner_of(seq_score)
    pair_score = jnp.abs(seq_score - partner) + 0.5 * (seq_score + partner)
    return mixed, pair_score


def solution(mesh):
    tokens, whole = P(("dp", "expert"), None), P()
    weights = P("expert", None, None)
    return jax.shard_map(
        body,
        mesh=mesh,
        in_specs=(tokens, tokens, tokens, P(("dp", "expert")), whole, weights, weights, weights, whole),
        out_specs=(tokens, P(("dp", "expert"))),
        check_vma=False,
    )
```

time: 85.7 us -> 62.9 us (0.73)
  waiting for transfers between devices: 35.7 us -> 18.4 us
  Pallas kernels: 17.6 us -> 23.2 us
  local copies, waits for them, and re-layouts: 4.97 us -> 0.01 us
  starting transfers between devices: 23.4 us -> 20 us
  other arithmetic: 2.84 us -> 0.2 us
    ppermute x14 -> x17, waiting for transfers between devices: 33.6 us -> 16.4 us  [send(): return lax.ppermute(x, 'expert', route)]
    pallas_call x3 -> x8, Pallas kernels: 17.6 us -> 23.2 us  [the longest x2 12 us: ffn(): pl.pallas_call(functools.partial(ffn_kernel, chips, experts), out_shape=[...]
    unnamed x26 -> x2, local copies, waits for them, and re-layouts: 4.21 us -> 0.01 us
    ppermute x14 -> x17, starting transfers between devices: 21.7 us -> 18.4 us  [send(): return lax.ppermute(x, 'expert', route)]
    convert_element_type x2, other arithmetic: 1.67 us -> 0.13 us  [chip_sum(): (same.astype(jnp.float32) + core_swap(other).astype(jnp.float32)).astype(...]
    add x1, other arithmetic: 1.17 us -> 0.07 us  [body(): send(x_pair[0], chip_route((1, 2), (2, 1)))]
  transfers between devices with their start and end apart: 15 -> 18, of which waited for: 8 -> 9; matrix products, arithmetic and copies ran while one was open for 0% -> 0% of each run, Pallas kernels for 0% -> 32%
where the time goes in v2:
time: 62.9 us; the launch traced here: 62.7 us
  Pallas kernels  23.2 us (37%)
  starting transfers between devices  20 us (32%)
  waiting for transfers between devices  18.4 us (29%)
  between operations  0.93 us (1%)
    ppermute x17, starting transfers between devices, send(): return lax.ppermute(x, 'expert', route)  18.4 us
    ppermute x17, waiting for transfers between devices, send(): return lax.ppermute(x, 'expert', route)  16.4 us
    pallas_call x2, Pallas kernels, ffn(): pl.pallas_call(functools.partial(ffn_kernel, chips, experts), out_shape=[...  12 us
    pallas_call x1, Pallas kernels, load(): pl.pallas_call(load_kernel, out_shape=[pltpu.VMEM(a.shape, a.dtype) for a...  8.34 us
    ppermute x1, waiting for transfers between devices, partner_of(): lax.ppermute(block, 'dp', [(d, d ^ count // 2) for d in range(count)])  2.09 us
    pallas_call x4, Pallas kernels, local_call(): pl.pallas_call(kernel, out_shape=out_shape, in_specs=[VMEM] * len(xs), ou...  1.65 us
    ppermute x1, starting transfers between devices, partner_of(): lax.ppermute(block, 'dp', [(d, d ^ count // 2) for d in range(count)])  1.52 us
  transfers between devices with their start and end apart: 18, of which 9 were waited for; matrix products, arithmetic and copies ran while one was open for 0% of the time, Pallas kernels for 32%

profile of v2, /device:TPU:0, one launch (start us, length us, event | category | flops | bytes accessed | tf_op | source)
XLA Modules:
  0.0 62.7 jit_solution(12466981182519309444)
XLA Ops:
  0.6 1.3 %prep.1.x_ref.refs_0_ = bf16[64,2176]{1,0:T(8,128)(2,1)S(1)} custom-call(bf16[64,2048]{1,0:T(8,128)(2,1)} %tok_ref.1, s32[8,64]{1,0:T(8,128)} %bitcast.5, s32[8,64]{1,0:T(8,128)} %bitcast.6, s32[4]{0:T(128)} %scorer_ref.1, bf16[2,2048]{1,0:T(2,128)(2,1)} %tags_ref.1), custom_call_target="tpu_custom_call" | custom-call | tf_op jit(solution)/shard_map/prep/pallas_call | solution.py:238
  1.9 4.1 %collective-permute-start = (bf16[64,2176]{1,0:T(8,128)(2,1)S(1)}, bf16[64,2176]{1,0:T(8,128)(2,1)S(1)}, u32[]{:S(2)}, u32[]{:S(2)}) collective-permute-start(bf16[64,2176]{1,0:T(8,128)(2,1)S(1)} %prep.1.x_ref.refs_0_), channel_id=1, source_target_pairs={{0,4},{1,5},{2,6},{3,7},{4,0},{5,1},{6,2},{7,3},{8,12},{9,13},{10,... | collective-permute-start | bytes 835592 | tf_op jit(solution)/shard_map/ppermute | solution.py:230
  6.0 1.6 %collective-permute-start.1 = (bf16[64,2176]{1,0:T(8,128)(2,1)S(1)}, bf16[64,2176]{1,0:T(8,128)(2,1)S(1)}, u32[]{:S(2)}, u32[]{:S(2)}) collective-permute-start(bf16[64,2176]{1,0:T(8,128)(2,1)S(1)} %prep.1.x_ref.refs_0_), channel_id=1, source_target_pairs={{0,2},{1,3},{2,0},{3,1},{4,6},{5,7},{6,4},{7,5},{8,10},{9,11},{10,... | collective-permute-start | bytes 835592 | tf_op jit(solution)/shard_map/ppermute | solution.py:230
  7.6 0.0 collective-permute-start.2
  7.6 8.3 %load_weights.1 = (bf16[4,2048,512]{2,1,0:T(8,128)(2,1)S(1)}, bf16[4,2048,512]{2,1,0:T(8,128)(2,1)S(1)}, bf16[4,512,2048]{2,1,0:T(8,128)(2,1)S(1)}) custom-call(bf16[64,2176]{1,0:T(8,128)(2,1)S(1)} %prep.1.x_ref.refs_0_, bf16[4,2048,512]{2,1,0:T(8,128)(2,1)} %refs_0_.1, bf16[4,2048,512]{2,1,0:T(8,128)(2,1)} %refs_1_.1, bf16[4,512,2048]{2,1,0:T(8,128)(2,1)} %refs_2_.1), custom_call_target="tpu_custom_call" | custom-call | bytes 25165824 | tf_op jit(solution)/shard_map/load_weights/pallas_call | solution.py:109
  15.9 2.8 %collective-permute-done.refs_4_ = bf16[64,2176]{1,0:T(8,128)(2,1)S(1)} collective-permute-done((bf16[64,2176]{1,0:T(8,128)(2,1)S(1)}, bf16[64,2176]{1,0:T(8,128)(2,1)S(1)}, u32[]{:S(2)}, u32[]{:S(2)}) %collective-permute-start) | collective-permute-done | bytes 278560 | tf_op jit(solution)/shard_map/ppermute | solution.py:230
  18.7 0.2 collective-permute-done.1.refs_2_
  18.9 0.0 collective-permute-done.2.refs_1_
  18.9 0.0 collective-permute-start.4
  18.9 0.5 collective-permute-start.3
  19.4 1.3 %collective-permute-start.8 = (bf16[64,2176]{1,0:T(8,128)(2,1)S(1)}, bf16[64,2176]{1,0:T(8,128)(2,1)S(1)}, u32[]{:S(2)}, u32[]{:S(2)}) collective-permute-start(bf16[64,2176]{1,0:T(8,128)(2,1)S(1)} %collective-permute-done.refs_4_), channel_id=1, source_target_pairs={{2,0},{3,1},{4,6},{5,7},{10,8},{11,9},{12,14},{13,15},{18,16},{19,... | collective-permute-start | bytes 835592 | tf_op jit(solution)/shard_map/ppermute | solution.py:230
  20.7 0.7 %collective-permute-start.7 = (bf16[64,2176]{1,0:T(8,128)(2,1)S(1)}, bf16[64,2176]{1,0:T(8,128)(2,1)S(1)}, u32[]{:S(2)}, u32[]{:S(2)}) collective-permute-start(bf16[64,2176]{1,0:T(8,128)(2,1)S(1)} %prep.1.x_ref.refs_0_), channel_id=1, source_target_pairs={{2,4},{3,5},{4,2},{5,3},{10,12},{11,13},{12,10},{13,11},{18,20},{1... | collective-permute-start | bytes 835592 | tf_op jit(solution)/shard_map/ppermute | solution.py:230
  21.4 0.0 collective-permute-done.4.refs_5_
  21.4 0.0 collective-permute-done.3.refs_3_
  21.4 6.4 %experts_1.1 = (bf16[64,2048]{1,0:T(8,128)(2,1)S(1)}, bf16[64,2048]{1,0:T(8,128)(2,1)S(1)}, bf16[64,2048]{1,0:T(8,128)(2,1)S(1)}, bf16[64,2048]{1,0:T(8,128)(2,1...) custom-call(bf16[64,2176]{1,0:T(8,128)(2,1)S(1)} %prep.1.x_ref.refs_0_, ...), custom_call_target="tpu_custom_call" | custom-call | flops 3623878656 | bytes 25165824 | tf_op jit(solution)/shard_map/experts_1/pallas_call | solution.py:133
  27.8 0.1 collective-permute-start.10
  27.9 2.0 %collective-permute-done.8 = bf16[64,2176]{1,0:T(8,128)(2,1)S(1)} collective-permute-done((bf16[64,2176]{1,0:T(8,128)(2,1)S(1)}, bf16[64,2176]{1,0:T(8,128)(2,1)S(1)}, u32[]{:S(2)}, u32[]{:S(2)}) %collective-permute-start.8) | collective-permute-done | bytes 278560 | tf_op jit(solution)/shard_map/ppermute | solution.py:230
  29.9 0.0 collective-permute-done.7
  29.9 0.1 add.10.refs_0_
  30.0 0.1 collective-permute-start.9
  30.0 0.5 collective-permute-start.6
  30.5 0.1 collective-permute-start.5
  30.6 0.0 collective-permute-done.10
  30.6 0.1 add_convert_fusion
  30.7 0.9 %collective-permute-done.9.refs_1_ = bf16[64,2176]{1,0:T(8,128)(2,1)S(1)} collective-permute-done((bf16[64,2176]{1,0:T(8,128)(2,1)S(1)}, bf16[64,2176]{1,0:T(8,128)(2,1)S(1)}, u32[]{:S(2)}, u32[]{:S(2)}) %collective-permute-start.9) | collective-permute-done | bytes 278560 | tf_op jit(solution)/shard_map/ppermute | solution.py:230
  31.6 4.5 %collective-permute-start.11 = (bf16[64,2048]{1,0:T(8,128)(2,1)S(1)}, bf16[64,2048]{1,0:T(8,128)(2,1)S(1)}, u32[]{:S(2)}, u32[]{:S(2)}) collective-permute-start(bf16[64,2048]{1,0:T(8,128)(2,1)S(1)} %add_convert_fusion), channel_id=1, source_target_pairs={{2,6},{3,7},{4,0},{5,1},{0,2},{1,3},{6,4},{7,5},{10,14},{11,15},{1... | collective-permute-start | bytes 786440 | tf_op jit(solution)/shard_map/ppermute | solution.py:230
  36.1 0.0 collective-permute-done.6
  36.1 0.1 add_convert_fusion.1.near_ref
  36.1 0.0 copy-start
  36.2 5.5 %experts_2.1 = (bf16[64,2048]{1,0:T(8,128)(2,1)S(1)}, bf16[64,2048]{1,0:T(8,128)(2,1)S(1)}) custom-call(bf16[64,2176]{1,0:T(8,128)(2,1)S(1)} %add.10.refs_0_, bf16[64,2176]{1,0:T(8,128)(2,1)S(1)} %collective-permute-done.9.refs_1_, bf16[4,2048,512]{2,1,0:T(8,128)(2,1)S(1)} %get-tuple-element.39.refs_6_.refs_2_, ...), custom_call_target="tpu_custom_call" | custom-call | flops 1207959552 | bytes 25165824 | tf_op jit(solution)/shard_map/experts_2/pallas_call | solution.py:133
  41.7 0.0 collective-permute-done.5.swapped_ref
  41.7 2.0 %collective-permute-done.11.relayed_ref = bf16[64,2048]{1,0:T(8,128)(2,1)S(1)} collective-permute-done((bf16[64,2048]{1,0:T(8,128)(2,1)S(1)}, bf16[64,2048]{1,0:T(8,128)(2,1)S(1)}, u32[]{:S(2)}, u32[]{:S(2)}) %collective-permute-start.11) | collective-permute-done | bytes 262176 | tf_op jit(solution)/shard_map/ppermute | solution.py:230
  43.7 0.0 copy-done
  43.7 0.4 own_sum.1
  44.1 0.1 collective-permute-start.12
  44.2 1.5 %collective-permute-done.12.swapped_ref = bf16[64,2048]{1,0:T(8,128)(2,1)S(1)} collective-permute-done((bf16[64,2048]{1,0:T(8,128)(2,1)S(1)}, bf16[64,2048]{1,0:T(8,128)(2,1)S(1)}, u32[]{:S(2)}, u32[]{:S(2)}) %collective-permute-start.12) | collective-permute-done | bytes 262176 | tf_op jit(solution)/shard_map/ppermute | solution.py:230
  45.7 0.3 third_back.1
  46.0 0.9 %collective-permute-start.13 = (bf16[64,2048]{1,0:T(8,128)(2,1)S(1)}, bf16[64,2048]{1,0:T(8,128)(2,1)S(1)}, u32[]{:S(2)}, u32[]{:S(2)}) collective-permute-start(bf16[64,2048]{1,0:T(8,128)(2,1)S(1)} %add_convert_fusion.1.near_ref), channel_id=1, source_target_pairs={{0,2},{1,3},{2,0},{3,1},{4,6},{5,7},{6,4},{7,5},{8,10},{9,11},{10,... | collective-permute-start | bytes 786440 | tf_op jit(solution)/shard_map/ppermute | solution.py:230
  47.0 2.4 %collective-permute-start.14 = (bf16[64,2048]{1,0:T(8,128)(2,1)S(1)}, bf16[64,2048]{1,0:T(8,128)(2,1)S(1)}, u32[]{:S(2)}, u32[]{:S(2)}) collective-permute-start(bf16[64,2048]{1,0:T(8,128)(2,1)S(1)} %get-tuple-element.60), channel_id=1, source_target_pairs={{0,6},{1,7},{2,4},{3,5},{4,2},{5,3},{6,0},{7,1},{8,14},{9,15},{10,... | collective-permute-start | bytes 786440 | tf_op jit(solution)/shard_map/ppermute | solution.py:230
  49.3 1.5 %collective-permute-start.15 = (f32[8,128]{1,0:T(8,128)S(1)}, f32[8,128]{1,0:T(8,128)S(1)}, u32[]{:S(2)}, u32[]{:S(2)}) collective-permute-start(f32[8,128]{1,0:T(8,128)S(1)} %get-tuple-element.61.score_ref), channel_id=1, source_target_pairs={{0,16},{8,24},{16,0},{24,8},{1,17},{9,25},{17,1},{25,9},{2,18},{10... | collective-permute-start | bytes 12296 | tf_op jit(solution)/shard_map/ppermute | solution.py:258
  50.8 2.1 %collective-permute-done.15.partner_ref = f32[8,128]{1,0:T(8,128)S(1)} collective-permute-done((f32[8,128]{1,0:T(8,128)S(1)}, f32[8,128]{1,0:T(8,128)S(1)}, u32[]{:S(2)}, u32[]{:S(2)}) %collective-permute-start.15) | collective-permute-done | bytes 4128 | tf_op jit(solution)/shard_map/ppermute | solution.py:258
  52.9 0.0 collective-permute-start.16
  52.9 1.7 %collective-permute-start.17 = (f32[2,8,128]{2,1,0:T(8,128)S(1)}, f32[2,8,128]{2,1,0:T(8,128)S(1)}, u32[]{:S(2)}, u32[]{:S(2)}) collective-permute-start(f32[2,8,128]{2,1,0:T(8,128)S(1)} %both_scores.1.both_ref), channel_id=1, source_target_pairs={{0,6},{1,7},{2,4},{3,5},{4,2},{5,3},{6,0},{7,1},{8,14},{9,15},{10,... | collective-permute-start | bytes 24584 | tf_op jit(solution)/shard_map/ppermute | solution.py:230
  54.7 4.1 %collective-permute-done.16.from_near_ref = f32[2,8,128]{2,1,0:T(8,128)S(1)} collective-permute-done((f32[2,8,128]{2,1,0:T(8,128)S(1)}, f32[2,8,128]{2,1,0:T(8,128)S(1)}, u32[]{:S(2)}, u32[]{:S(2)}) %collective-permute-start.16) | collective-permute-done | bytes 8224 | tf_op jit(solution)/shard_map/ppermute | solution.py:230
  58.8 2.9 %collective-permute-done.17.from_third_ref = f32[2,8,128]{2,1,0:T(8,128)S(1)} collective-permute-done((f32[2,8,128]{2,1,0:T(8,128)S(1)}, f32[2,8,128]{2,1,0:T(8,128)S(1)}, u32[]{:S(2)}, u32[]{:S(2)}) %collective-permute-start.17) | collective-permute-done | bytes 8224 | tf_op jit(solution)/shard_map/ppermute | solution.py:230
  61.7 0.0 collective-permute-done.13.near_ref
  61.7 0.0 collective-permute-done.14.third_ref
  61.7 0.9 %mixed.1 = (bf16[64,2048]{1,0:T(8,128)(2,1)}, f32[4]{0:T(128)}) custom-call(f32[64,2048]{1,0:T(8,128)S(1)} %get-tuple-element.49.sum_ref, bf16[64,2048]{1,0:T(8,128)(2,1)S(1)} %collective-permute-done.13.near_ref, bf16[64,2048]{1,0:T(8,128)(2,1)S(1)} %collective-permute-done.14.third_ref, f32[2,8,128]{2,1,0:T(8,128)S(1)} %both_scores.1.both_ref, ...), custom_call_target="tpu_custom_call" | custom-call | tf_op jit(solution)/shard_map/mixed/pallas_call | solution.py:219
  (1 shorter events, 0.0 us)
Async XLA Ops:
  1.9 16.8 %collective-permute-start = (bf16[64,2176]{1,0:T(8,128)(2,1)S(1)}, bf16[64,2176]{1,0:T(8,128)(2,1)S(1)}, u32[]{:S(2)}, u32[]{:S(2)}) collective-permute-start(bf16[64,2176]{1,0:T(8,128)(2,1)S(1)} %prep.1.x_ref.refs_0_), channel_id=1, source_target_pairs={{0,4},{1,5},{2,6},{3,7},{4,0},{5,1},{6,2},{7,3},{8,12},{9,13},{10,... | collective-permute-start | bytes 835592 | tf_op jit(solution)/shard_map/ppermute | solution.py:230
  6.0 12.9 %collective-permute-start.1 = (bf16[64,2176]{1,0:T(8,128)(2,1)S(1)}, bf16[64,2176]{1,0:T(8,128)(2,1)S(1)}, u32[]{:S(2)}, u32[]{:S(2)}) collective-permute-start(bf16[64,2176]{1,0:T(8,128)(2,1)S(1)} %prep.1.x_ref.refs_0_), channel_id=1, source_target_pairs={{0,2},{1,3},{2,0},{3,1},{4,6},{5,7},{6,4},{7,5},{8,10},{9,11},{10,... | collective-permute-start | bytes 835592 | tf_op jit(solution)/shard_map/ppermute | solution.py:230
  7.6 11.3 %collective-permute-start.2 = (bf16[64,2176]{1,0:T(8,128)(2,1)S(1)}, bf16[64,2176]{1,0:T(8,128)(2,1)S(1)}, u32[]{:S(2)}, u32[]{:S(2)}) collective-permute-start(bf16[64,2176]{1,0:T(8,128)(2,1)S(1)} %prep.1.x_ref.refs_0_), channel_id=1, source_target_pairs={{0,1},{1,0},{2,3},{3,2},{4,5},{5,4},{6,7},{7,6},{8,9},{9,8},{10,11... | collective-permute-start | bytes 835592 | tf_op jit(solution)/shard_map/ppermute | solution.py:230
  18.9 2.5 %collective-permute-start.4 = (bf16[64,2176]{1,0:T(8,128)(2,1)S(1)}, bf16[64,2176]{1,0:T(8,128)(2,1)S(1)}, u32[]{:S(2)}, u32[]{:S(2)}) collective-permute-start(bf16[64,2176]{1,0:T(8,128)(2,1)S(1)} %collective-permute-done.refs_4_), channel_id=1, source_target_pairs={{0,1},{1,0},{2,3},{3,2},{4,5},{5,4},{6,7},{7,6},{8,9},{9,8},{10,11... | collective-permute-start | bytes 835592 | tf_op jit(solution)/shard_map/ppermute | solution.py:230
  18.9 2.5 %collective-permute-start.3 = (bf16[64,2176]{1,0:T(8,128)(2,1)S(1)}, bf16[64,2176]{1,0:T(8,128)(2,1)S(1)}, u32[]{:S(2)}, u32[]{:S(2)}) collective-permute-start(bf16[64,2176]{1,0:T(8,128)(2,1)S(1)} %collective-permute-done.1.refs_2_), channel_id=1, source_target_pairs={{0,1},{1,0},{2,3},{3,2},{4,5},{5,4},{6,7},{7,6},{8,9},{9,8},{10,11... | collective-permute-start | bytes 835592 | tf_op jit(solution)/shard_map/ppermute | solution.py:230
  19.4 10.4 %collective-permute-start.8 = (bf16[64,2176]{1,0:T(8,128)(2,1)S(1)}, bf16[64,2176]{1,0:T(8,128)(2,1)S(1)}, u32[]{:S(2)}, u32[]{:S(2)}) collective-permute-start(bf16[64,2176]{1,0:T(8,128)(2,1)S(1)} %collective-permute-done.refs_4_), channel_id=1, source_target_pairs={{2,0},{3,1},{4,6},{5,7},{10,8},{11,9},{12,14},{13,15},{18,16},{19,... | collective-permute-start | bytes 835592 | tf_op jit(solution)/shard_map/ppermute | solution.py:230
  20.7 9.2 %collective-permute-start.7 = (bf16[64,2176]{1,0:T(8,128)(2,1)S(1)}, bf16[64,2176]{1,0:T(8,128)(2,1)S(1)}, u32[]{:S(2)}, u32[]{:S(2)}) collective-permute-start(bf16[64,2176]{1,0:T(8,128)(2,1)S(1)} %prep.1.x_ref.refs_0_), channel_id=1, source_target_pairs={{2,4},{3,5},{4,2},{5,3},{10,12},{11,13},{12,10},{13,11},{18,20},{1... | collective-permute-start | bytes 835592 | tf_op jit(solution)/shard_map/ppermute | solution.py:230
  27.8 2.8 %collective-permute-start.10 = (bf16[64,2048]{1,0:T(8,128)(2,1)S(1)}, bf16[64,2048]{1,0:T(8,128)(2,1)S(1)}, u32[]{:S(2)}, u32[]{:S(2)}) collective-permute-start(bf16[64,2048]{1,0:T(8,128)(2,1)S(1)} %get-tuple-element.47), channel_id=1, source_target_pairs={{0,1},{1,0},{2,3},{3,2},{4,5},{5,4},{6,7},{7,6},{8,9},{9,8},{10,11... | collective-permute-start | bytes 786440 | tf_op jit(solution)/shard_map/ppermute | solution.py:230
  30.0 1.6 %collective-permute-start.9 = (bf16[64,2176]{1,0:T(8,128)(2,1)S(1)}, bf16[64,2176]{1,0:T(8,128)(2,1)S(1)}, u32[]{:S(2)}, u32[]{:S(2)}) collective-permute-start(bf16[64,2176]{1,0:T(8,128)(2,1)S(1)} %add.10.refs_0_), channel_id=1, source_target_pairs={{0,1},{1,0},{2,3},{3,2},{4,5},{5,4},{6,7},{7,6},{8,9},{9,8},{10,11... | collective-permute-start | bytes 835592 | tf_op jit(solution)/shard_map/ppermute | solution.py:230
  30.0 6.0 %collective-permute-start.6 = (bf16[64,2048]{1,0:T(8,128)(2,1)S(1)}, bf16[64,2048]{1,0:T(8,128)(2,1)S(1)}, u32[]{:S(2)}, u32[]{:S(2)}) collective-permute-start(bf16[64,2048]{1,0:T(8,128)(2,1)S(1)} %get-tuple-element.45), channel_id=1, source_target_pairs={{0,1},{1,0},{2,3},{3,2},{4,5},{5,4},{6,7},{7,6},{8,9},{9,8},{10,11... | collective-permute-start | bytes 786440 | tf_op jit(solution)/shard_map/ppermute | solution.py:230
  30.5 11.2 %collective-permute-start.5 = (bf16[64,2048]{1,0:T(8,128)(2,1)S(1)}, bf16[64,2048]{1,0:T(8,128)(2,1)S(1)}, u32[]{:S(2)}, u32[]{:S(2)}) collective-permute-start(bf16[64,2048]{1,0:T(8,128)(2,1)S(1)} %get-tuple-element.43), channel_id=1, source_target_pairs={{0,1},{1,0},{2,3},{3,2},{4,5},{5,4},{6,7},{7,6},{8,9},{9,8},{10,11... | collective-permute-start | bytes 786440 | tf_op jit(solution)/shard_map/ppermute | solution.py:230
  31.6 12.1 %collective-permute-start.11 = (bf16[64,2048]{1,0:T(8,128)(2,1)S(1)}, bf16[64,2048]{1,0:T(8,128)(2,1)S(1)}, u32[]{:S(2)}, u32[]{:S(2)}) collective-permute-start(bf16[64,2048]{1,0:T(8,128)(2,1)S(1)} %add_convert_fusion), channel_id=1, source_target_pairs={{2,6},{3,7},{4,0},{5,1},{0,2},{1,3},{6,4},{7,5},{10,14},{11,15},{1... | collective-permute-start | bytes 786440 | tf_op jit(solution)/shard_map/ppermute | solution.py:230
  36.1 7.6 %copy-start = (f32[2048]{0:T(1024)S(1)}, f32[2048]{0:T(1024)}, u32[]{:S(2)}) copy-start(f32[2048]{0:T(1024)} %param.17) | copy-start | bytes 24580
  44.1 1.6 %collective-permute-start.12 = (bf16[64,2048]{1,0:T(8,128)(2,1)S(1)}, bf16[64,2048]{1,0:T(8,128)(2,1)S(1)}, u32[]{:S(2)}, u32[]{:S(2)}) collective-permute-start(bf16[64,2048]{1,0:T(8,128)(2,1)S(1)} %get-tuple-element.55), channel_id=1, source_target_pairs={{0,1},{1,0},{2,3},{3,2},{4,5},{5,4},{6,7},{7,6},{8,9},{9,8},{10,11... | collective-permute-start | bytes 786440 | tf_op jit(solution)/shard_map/ppermute | solution.py:230
  46.0 15.6 %collective-permute-start.13 = (bf16[64,2048]{1,0:T(8,128)(2,1)S(1)}, bf16[64,2048]{1,0:T(8,128)(2,1)S(1)}, u32[]{:S(2)}, u32[]{:S(2)}) collective-permute-start(bf16[64,2048]{1,0:T(8,128)(2,1)S(1)} %add_convert_fusion.1.near_ref), channel_id=1, source_target_pairs={{0,2},{1,3},{2,0},{3,1},{4,6},{5,7},{6,4},{7,5},{8,10},{9,11},{10,... | collective-permute-start | bytes 786440 | tf_op jit(solution)/shard_map/ppermute | solution.py:230
  47.0 14.7 %collective-permute-start.14 = (bf16[64,2048]{1,0:T(8,128)(2,1)S(1)}, bf16[64,2048]{1,0:T(8,128)(2,1)S(1)}, u32[]{:S(2)}, u32[]{:S(2)}) collective-permute-start(bf16[64,2048]{1,0:T(8,128)(2,1)S(1)} %get-tuple-element.60), channel_id=1, source_target_pairs={{0,6},{1,7},{2,4},{3,5},{4,2},{5,3},{6,0},{7,1},{8,14},{9,15},{10,... | collective-permute-start | bytes 786440 | tf_op jit(solution)/shard_map/ppermute | solution.py:230
  49.3 3.6 %collective-permute-start.15 = (f32[8,128]{1,0:T(8,128)S(1)}, f32[8,128]{1,0:T(8,128)S(1)}, u32[]{:S(2)}, u32[]{:S(2)}) collective-permute-start(f32[8,128]{1,0:T(8,128)S(1)} %get-tuple-element.61.score_ref), channel_id=1, source_target_pairs={{0,16},{8,24},{16,0},{24,8},{1,17},{9,25},{17,1},{25,9},{2,18},{10... | collective-permute-start | bytes 12296 | tf_op jit(solution)/shard_map/ppermute | solution.py:258
  52.9 5.8 %collective-permute-start.16 = (f32[2,8,128]{2,1,0:T(8,128)S(1)}, f32[2,8,128]{2,1,0:T(8,128)S(1)}, u32[]{:S(2)}, u32[]{:S(2)}) collective-permute-start(f32[2,8,128]{2,1,0:T(8,128)S(1)} %both_scores.1.both_ref), channel_id=1, source_target_pairs={{0,2},{1,3},{2,0},{3,1},{4,6},{5,7},{6,4},{7,5},{8,10},{9,11},{10,... | collective-permute-start | bytes 24584 | tf_op jit(solution)/shard_map/ppermute | solution.py:230
  52.9 8.7 %collective-permute-start.17 = (f32[2,8,128]{2,1,0:T(8,128)S(1)}, f32[2,8,128]{2,1,0:T(8,128)S(1)}, u32[]{:S(2)}, u32[]{:S(2)}) collective-permute-start(f32[2,8,128]{2,1,0:T(8,128)S(1)} %both_scores.1.both_ref), channel_id=1, source_target_pairs={{0,6},{1,7},{2,4},{3,5},{4,2},{5,3},{6,0},{7,1},{8,14},{9,15},{10,... | collective-permute-start | bytes 24584 | tf_op jit(solution)/shard_map/ppermute | solution.py:230

commit v3 on v2

--- a/solution.py
+++ b/solution.py
@@ -269,13 +269,15 @@
         near = exchange(x, 1)
         x_pair = pair(x)
         far, near, x_pair, *weights = lax.optimization_barrier((far, near, x_pair, *weights))
-        third = send(x_pair[0], chip_route((1, 2), (2, 1))) + send(far, chip_route((1, 0), (2, 3)))
+        third = exchange(far, 1)
         own_sums, near_sums, far_sums = ffn("experts_1", [x_pair, pair(near), pair(far)], experts, weights)
         far_back = chip_sum(far_sums)
-        third_pair, far_back = lax.optimization_barrier((pair(third), far_back))
         relayed = send(far_back, chip_route((1, 3), (2, 0), (0, 1), (3, 2)))
-        (third_sums,) = ffn("experts_2", [third_pair], experts, weights)
+        (third_sums,) = ffn("experts_2", [pair(third)], experts, weights)
+        third_same, third_other = third_sums
         near_back = chip_sum(near_sums)
+        third_other, near_back, relayed = lax.optimization_barrier((third_other, near_back, relayed))
+        near = exchange(near_back, 1)
         head = score_head.reshape(1, width)
         scores = (8, META)
         own_sum, joins, score = local_call(
@@ -288,17 +290,13 @@
             ],
             *(own_sums[0], core_swap(own_sums[1]), near_back, relayed, head),
         )
-        third_same, third_other = third_sums
-        third_other, joins = lax.optimization_barrier((third_other, joins))
         third_back, score = local_call(
             third_kernel,
             "third_back",
             [pltpu.VMEM((rows, width), jnp.bfloat16), pltpu.VMEM(scores, jnp.float32)],
             *(third_same, core_swap(third_other), joins, score, head),
         )
-        near_back, third_back = lax.optimization_barrier((near_back, third_back))
         third = exchange(third_back, 3)
-        near = exchange(near_back, 1)
         (both,) = local_call(
             both_kernel, "both_scores", [pltpu.VMEM((2, *scores), jnp.float32)], score, partner_of(score)
         )

time: 62.9 us -> 55.9 us (0.89)
  waiting for transfers between devices: 18.4 us -> 14.8 us
  starting transfers between devices: 20 us -> 16.7 us
    ppermute x17 -> x16, waiting for transfers between devices: 16.4 us -> 12.7 us  [send(): return lax.ppermute(x, 'expert', route)]
    ppermute x17 -> x16, starting transfers between devices: 18.4 us -> 15.2 us  [send(): return lax.ppermute(x, 'expert', route)]
  transfers between devices with their start and end apart: 18 -> 17, of which waited for: 9 -> 8; matrix products, arithmetic and copies ran while one was open for 0% -> 0% of each run, Pallas kernels for 32% -> 38%
where the time goes in v3:
time: 55.9 us; the launch traced here: 55.8 us
  Pallas kernels  23.2 us (42%)
  starting transfers between devices  16.7 us (30%)
  waiting for transfers between devices  14.8 us (26%)
  between operations  0.87 us (2%)
    ppermute x16, starting transfers between devices, send(): return lax.ppermute(x, 'expert', route)  15.2 us
    ppermute x16, waiting for transfers between devices, send(): return lax.ppermute(x, 'expert', route)  12.7 us
    pallas_call x2, Pallas kernels, ffn(): pl.pallas_call(functools.partial(ffn_kernel, chips, experts), out_shape=[...  12 us
    pallas_call x1, Pallas kernels, load(): pl.pallas_call(load_kernel, out_shape=[pltpu.VMEM(a.shape, a.dtype) for a...  8.34 us
    ppermute x1, waiting for transfers between devices, partner_of(): lax.ppermute(block, 'dp', [(d, d ^ count // 2) for d in range(count)])  2.08 us
    pallas_call x4, Pallas kernels, local_call(): pl.pallas_call(kernel, out_shape=out_shape, in_specs=[VMEM] * len(xs), ou...  1.64 us
    ppermute x1, starting transfers between devices, partner_of(): lax.ppermute(block, 'dp', [(d, d ^ count // 2) for d in range(count)])  1.53 us
    pallas_call x1, Pallas kernels, body(): pl.pallas_call(functools.partial(prep_kernel, experts), out_shape=pltpu.V...  1.26 us
  transfers between devices with their start and end apart: 17, of which 8 were waited for; matrix products, arithmetic and copies ran while one was open for 0% of the time, Pallas kernels for 38%

profile of v3, /device:TPU:0, one launch (start us, length us, event | category | flops | bytes accessed | tf_op | source)
XLA Modules:
  0.0 55.8 jit_solution(8934442032538196725)
XLA Ops:
  0.6 1.3 %prep.1.x_ref.refs_0_ = bf16[64,2176]{1,0:T(8,128)(2,1)S(1)} custom-call(bf16[64,2048]{1,0:T(8,128)(2,1)} %tok_ref.1, s32[8,64]{1,0:T(8,128)} %bitcast.5, s32[8,64]{1,0:T(8,128)} %bitcast.6, s32[4]{0:T(128)} %scorer_ref.1, bf16[2,2048]{1,0:T(2,128)(2,1)} %tags_ref.1), custom_call_target="tpu_custom_call" | custom-call | tf_op jit(solution)/shard_map/prep/pallas_call | solution.py:238
  1.9 4.1 %collective-permute-start = (bf16[64,2176]{1,0:T(8,128)(2,1)S(1)}, bf16[64,2176]{1,0:T(8,128)(2,1)S(1)}, u32[]{:S(2)}, u32[]{:S(2)}) collective-permute-start(bf16[64,2176]{1,0:T(8,128)(2,1)S(1)} %prep.1.x_ref.refs_0_), channel_id=1, source_target_pairs={{0,4},{1,5},{2,6},{3,7},{4,0},{5,1},{6,2},{7,3},{8,12},{9,13},{10,... | collective-permute-start | bytes 835592 | tf_op jit(solution)/shard_map/ppermute | solution.py:230
  6.0 1.6 %collective-permute-start.1 = (bf16[64,2176]{1,0:T(8,128)(2,1)S(1)}, bf16[64,2176]{1,0:T(8,128)(2,1)S(1)}, u32[]{:S(2)}, u32[]{:S(2)}) collective-permute-start(bf16[64,2176]{1,0:T(8,128)(2,1)S(1)} %prep.1.x_ref.refs_0_), channel_id=1, source_target_pairs={{0,2},{1,3},{2,0},{3,1},{4,6},{5,7},{6,4},{7,5},{8,10},{9,11},{10,... | collective-permute-start | bytes 835592 | tf_op jit(solution)/shard_map/ppermute | solution.py:230
  7.6 0.0 collective-permute-start.2
  7.6 8.3 %load_weights.1 = (bf16[4,2048,512]{2,1,0:T(8,128)(2,1)S(1)}, bf16[4,2048,512]{2,1,0:T(8,128)(2,1)S(1)}, bf16[4,512,2048]{2,1,0:T(8,128)(2,1)S(1)}) custom-call(bf16[64,2176]{1,0:T(8,128)(2,1)S(1)} %prep.1.x_ref.refs_0_, bf16[4,2048,512]{2,1,0:T(8,128)(2,1)} %refs_0_.1, bf16[4,2048,512]{2,1,0:T(8,128)(2,1)} %refs_1_.1, bf16[4,512,2048]{2,1,0:T(8,128)(2,1)} %refs_2_.1), custom_call_target="tpu_custom_call" | custom-call | bytes 25165824 | tf_op jit(solution)/shard_map/load_weights/pallas_call | solution.py:109
  15.9 2.8 %collective-permute-done.refs_4_ = bf16[64,2176]{1,0:T(8,128)(2,1)S(1)} collective-permute-done((bf16[64,2176]{1,0:T(8,128)(2,1)S(1)}, bf16[64,2176]{1,0:T(8,128)(2,1)S(1)}, u32[]{:S(2)}, u32[]{:S(2)}) %collective-permute-start) | collective-permute-done | bytes 278560 | tf_op jit(solution)/shard_map/ppermute | solution.py:230
  18.7 0.2 collective-permute-done.1.refs_2_
  18.9 0.0 collective-permute-done.2.refs_1_
  18.9 0.0 collective-permute-start.4
  18.9 0.5 collective-permute-start.3
  19.4 1.5 %collective-permute-start.6 = (bf16[64,2176]{1,0:T(8,128)(2,1)S(1)}, bf16[64,2176]{1,0:T(8,128)(2,1)S(1)}, u32[]{:S(2)}, u32[]{:S(2)}) collective-permute-start(bf16[64,2176]{1,0:T(8,128)(2,1)S(1)} %collective-permute-done.refs_4_), channel_id=1, source_target_pairs={{0,2},{1,3},{2,0},{3,1},{4,6},{5,7},{6,4},{7,5},{8,10},{9,11},{10,... | collective-permute-start | bytes 835592 | tf_op jit(solution)/shard_map/ppermute | solution.py:230
  20.9 0.0 collective-permute-done.4.refs_5_
  20.9 0.0 collective-permute-done.3.refs_3_
  20.9 6.4 %experts_1.1 = (bf16[64,2048]{1,0:T(8,128)(2,1)S(1)}, bf16[64,2048]{1,0:T(8,128)(2,1)S(1)}, bf16[64,2048]{1,0:T(8,128)(2,1)S(1)}, bf16[64,2048]{1,0:T(8,128)(2,1...) custom-call(bf16[64,2176]{1,0:T(8,128)(2,1)S(1)} %prep.1.x_ref.refs_0_, ...), custom_call_target="tpu_custom_call" | custom-call | flops 3623878656 | bytes 25165824 | tf_op jit(solution)/shard_map/experts_1/pallas_call | solution.py:133
  27.3 0.2 collective-permute-start.9
  27.5 0.4 collective-permute-start.8
  27.9 0.1 collective-permute-start.5
  28.0 0.0 collective-permute-done.6.refs_0_
  28.0 0.4 collective-permute-start.7
  28.4 0.5 collective-permute-done.9
  28.9 0.1 add_convert_fusion
  29.0 1.6 %collective-permute-start.10 = (bf16[64,2048]{1,0:T(8,128)(2,1)S(1)}, bf16[64,2048]{1,0:T(8,128)(2,1)S(1)}, u32[]{:S(2)}, u32[]{:S(2)}) collective-permute-start(bf16[64,2048]{1,0:T(8,128)(2,1)S(1)} %add_convert_fusion), channel_id=1, source_target_pairs={{2,6},{3,7},{4,0},{5,1},{0,2},{1,3},{6,4},{7,5},{10,14},{11,15},{1... | collective-permute-start | bytes 786440 | tf_op jit(solution)/shard_map/ppermute | solution.py:230
  30.7 0.0 collective-permute-done.8
  30.7 0.1 add_convert_fusion.1.near_ref
  30.7 0.0 copy-start
  30.7 0.0 collective-permute-done.7.refs_1_
  30.7 5.5 %experts_2.1 = (bf16[64,2048]{1,0:T(8,128)(2,1)S(1)}, bf16[64,2048]{1,0:T(8,128)(2,1)S(1)}) custom-call(bf16[64,2176]{1,0:T(8,128)(2,1)S(1)} %collective-permute-done.6.refs_0_, bf16[64,2176]{1,0:T(8,128)(2,1)S(1)} %collective-permute-done.7.refs_1_, bf16[4,2048,512]{2,1,0:T(8,128)(2,1)S(1)} %get-tuple-element.35.refs_6_.refs_2_, ...), custom_call_target="tpu_custom_call" | custom-call | flops 1207959552 | bytes 25165824 | tf_op jit(solution)/shard_map/experts_2/pallas_call | solution.py:133
  36.3 2.2 %collective-permute-done.10.relayed_ref = bf16[64,2048]{1,0:T(8,128)(2,1)S(1)} collective-permute-done((bf16[64,2048]{1,0:T(8,128)(2,1)S(1)}, bf16[64,2048]{1,0:T(8,128)(2,1)S(1)}, u32[]{:S(2)}, u32[]{:S(2)}) %collective-permute-start.10) | collective-permute-done | bytes 262176 | tf_op jit(solution)/shard_map/ppermute | solution.py:230
  38.5 0.0 collective-permute-start.12
  38.5 0.5 collective-permute-start.11
  39.0 0.0 collective-permute-done.5.swapped_ref
  39.0 0.0 copy-done
  39.0 0.4 own_sum.1
  39.4 0.6 %collective-permute-done.12.swapped_ref = bf16[64,2048]{1,0:T(8,128)(2,1)S(1)} collective-permute-done((bf16[64,2048]{1,0:T(8,128)(2,1)S(1)}, bf16[64,2048]{1,0:T(8,128)(2,1)S(1)}, u32[]{:S(2)}, u32[]{:S(2)}) %collective-permute-start.12) | collective-permute-done | bytes 262176 | tf_op jit(solution)/shard_map/ppermute | solution.py:230
  40.0 0.3 third_back.1
  40.3 3.3 %collective-permute-start.13 = (bf16[64,2048]{1,0:T(8,128)(2,1)S(1)}, bf16[64,2048]{1,0:T(8,128)(2,1)S(1)}, u32[]{:S(2)}, u32[]{:S(2)}) collective-permute-start(bf16[64,2048]{1,0:T(8,128)(2,1)S(1)} %get-tuple-element.52), channel_id=1, source_target_pairs={{0,6},{1,7},{2,4},{3,5},{4,2},{5,3},{6,0},{7,1},{8,14},{9,15},{10,... | collective-permute-start | bytes 786440 | tf_op jit(solution)/shard_map/ppermute | solution.py:230
  43.6 1.5 %collective-permute-start.14 = (f32[8,128]{1,0:T(8,128)S(1)}, f32[8,128]{1,0:T(8,128)S(1)}, u32[]{:S(2)}, u32[]{:S(2)}) collective-permute-start(f32[8,128]{1,0:T(8,128)S(1)} %get-tuple-element.53.score_ref), channel_id=1, source_target_pairs={{0,16},{8,24},{16,0},{24,8},{1,17},{9,25},{17,1},{25,9},{2,18},{10... | collective-permute-start | bytes 12296 | tf_op jit(solution)/shard_map/ppermute | solution.py:258
  45.1 2.1 %collective-permute-done.14.partner_ref = f32[8,128]{1,0:T(8,128)S(1)} collective-permute-done((f32[8,128]{1,0:T(8,128)S(1)}, f32[8,128]{1,0:T(8,128)S(1)}, u32[]{:S(2)}, u32[]{:S(2)}) %collective-permute-start.14) | collective-permute-done | bytes 4128 | tf_op jit(solution)/shard_map/ppermute | solution.py:258
  47.2 0.0 collective-permute-start.15
  47.2 1.0 %collective-permute-start.16 = (f32[2,8,128]{2,1,0:T(8,128)S(1)}, f32[2,8,128]{2,1,0:T(8,128)S(1)}, u32[]{:S(2)}, u32[]{:S(2)}) collective-permute-start(f32[2,8,128]{2,1,0:T(8,128)S(1)} %both_scores.1.both_ref), channel_id=1, source_target_pairs={{0,6},{1,7},{2,4},{3,5},{4,2},{5,3},{6,0},{7,1},{8,14},{9,15},{10,... | collective-permute-start | bytes 24584 | tf_op jit(solution)/shard_map/ppermute | solution.py:230
  48.2 0.0 collective-permute-done.11.near_ref
  48.2 6.3 %collective-permute-done.15.from_near_ref = f32[2,8,128]{2,1,0:T(8,128)S(1)} collective-permute-done((f32[2,8,128]{2,1,0:T(8,128)S(1)}, f32[2,8,128]{2,1,0:T(8,128)S(1)}, u32[]{:S(2)}, u32[]{:S(2)}) %collective-permute-start.15) | collective-permute-done | bytes 8224 | tf_op jit(solution)/shard_map/ppermute | solution.py:230
  54.5 0.2 collective-permute-done.16.from_third_ref
  54.7 0.0 collective-permute-done.13.third_ref
  54.7 0.9 %mixed.1 = (bf16[64,2048]{1,0:T(8,128)(2,1)}, f32[4]{0:T(128)}) custom-call(f32[64,2048]{1,0:T(8,128)S(1)} %get-tuple-element.47.sum_ref, bf16[64,2048]{1,0:T(8,128)(2,1)S(1)} %collective-permute-done.11.near_ref, bf16[64,2048]{1,0:T(8,128)(2,1)S(1)} %collective-permute-done.13.third_ref, f32[2,8,128]{2,1,0:T(8,128)S(1)} %both_scores.1.both_ref, ...), custom_call_target="tpu_custom_call" | custom-call | tf_op jit(solution)/shard_map/mixed/pallas_call | solution.py:219
  (1 shorter events, 0.0 us)
Async XLA Ops:
  1.9 16.8 %collective-permute-start = (bf16[64,2176]{1,0:T(8,128)(2,1)S(1)}, bf16[64,2176]{1,0:T(8,128)(2,1)S(1)}, u32[]{:S(2)}, u32[]{:S(2)}) collective-permute-start(bf16[64,2176]{1,0:T(8,128)(2,1)S(1)} %prep.1.x_ref.refs_0_), channel_id=1, source_target_pairs={{0,4},{1,5},{2,6},{3,7},{4,0},{5,1},{6,2},{7,3},{8,12},{9,13},{10,... | collective-permute-start | bytes 835592 | tf_op jit(solution)/shard_map/ppermute | solution.py:230
  6.0 12.9 %collective-permute-start.1 = (bf16[64,2176]{1,0:T(8,128)(2,1)S(1)}, bf16[64,2176]{1,0:T(8,128)(2,1)S(1)}, u32[]{:S(2)}, u32[]{:S(2)}) collective-permute-start(bf16[64,2176]{1,0:T(8,128)(2,1)S(1)} %prep.1.x_ref.refs_0_), channel_id=1, source_target_pairs={{0,2},{1,3},{2,0},{3,1},{4,6},{5,7},{6,4},{7,5},{8,10},{9,11},{10,... | collective-permute-start | bytes 835592 | tf_op jit(solution)/shard_map/ppermute | solution.py:230
  7.6 11.3 %collective-permute-start.2 = (bf16[64,2176]{1,0:T(8,128)(2,1)S(1)}, bf16[64,2176]{1,0:T(8,128)(2,1)S(1)}, u32[]{:S(2)}, u32[]{:S(2)}) collective-permute-start(bf16[64,2176]{1,0:T(8,128)(2,1)S(1)} %prep.1.x_ref.refs_0_), channel_id=1, source_target_pairs={{0,1},{1,0},{2,3},{3,2},{4,5},{5,4},{6,7},{7,6},{8,9},{9,8},{10,11... | collective-permute-start | bytes 835592 | tf_op jit(solution)/shard_map/ppermute | solution.py:230
  18.9 2.0 %collective-permute-start.4 = (bf16[64,2176]{1,0:T(8,128)(2,1)S(1)}, bf16[64,2176]{1,0:T(8,128)(2,1)S(1)}, u32[]{:S(2)}, u32[]{:S(2)}) collective-permute-start(bf16[64,2176]{1,0:T(8,128)(2,1)S(1)} %collective-permute-done.refs_4_), channel_id=1, source_target_pairs={{0,1},{1,0},{2,3},{3,2},{4,5},{5,4},{6,7},{7,6},{8,9},{9,8},{10,11... | collective-permute-start | bytes 835592 | tf_op jit(solution)/shard_map/ppermute | solution.py:230
  18.9 2.0 %collective-permute-start.3 = (bf16[64,2176]{1,0:T(8,128)(2,1)S(1)}, bf16[64,2176]{1,0:T(8,128)(2,1)S(1)}, u32[]{:S(2)}, u32[]{:S(2)}) collective-permute-start(bf16[64,2176]{1,0:T(8,128)(2,1)S(1)} %collective-permute-done.1.refs_2_), channel_id=1, source_target_pairs={{0,1},{1,0},{2,3},{3,2},{4,5},{5,4},{6,7},{7,6},{8,9},{9,8},{10,11... | collective-permute-start | bytes 835592 | tf_op jit(solution)/shard_map/ppermute | solution.py:230
  19.4 8.6 %collective-permute-start.6 = (bf16[64,2176]{1,0:T(8,128)(2,1)S(1)}, bf16[64,2176]{1,0:T(8,128)(2,1)S(1)}, u32[]{:S(2)}, u32[]{:S(2)}) collective-permute-start(bf16[64,2176]{1,0:T(8,128)(2,1)S(1)} %collective-permute-done.refs_4_), channel_id=1, source_target_pairs={{0,2},{1,3},{2,0},{3,1},{4,6},{5,7},{6,4},{7,5},{8,10},{9,11},{10,... | collective-permute-start | bytes 835592 | tf_op jit(solution)/shard_map/ppermute | solution.py:230
  27.3 1.6 %collective-permute-start.9 = (bf16[64,2048]{1,0:T(8,128)(2,1)S(1)}, bf16[64,2048]{1,0:T(8,128)(2,1)S(1)}, u32[]{:S(2)}, u32[]{:S(2)}) collective-permute-start(bf16[64,2048]{1,0:T(8,128)(2,1)S(1)} %get-tuple-element.44), channel_id=1, source_target_pairs={{0,1},{1,0},{2,3},{3,2},{4,5},{5,4},{6,7},{7,6},{8,9},{9,8},{10,11... | collective-permute-start | bytes 786440 | tf_op jit(solution)/shard_map/ppermute | solution.py:230
  27.5 3.2 %collective-permute-start.8 = (bf16[64,2048]{1,0:T(8,128)(2,1)S(1)}, bf16[64,2048]{1,0:T(8,128)(2,1)S(1)}, u32[]{:S(2)}, u32[]{:S(2)}) collective-permute-start(bf16[64,2048]{1,0:T(8,128)(2,1)S(1)} %get-tuple-element.42), channel_id=1, source_target_pairs={{0,1},{1,0},{2,3},{3,2},{4,5},{5,4},{6,7},{7,6},{8,9},{9,8},{10,11... | collective-permute-start | bytes 786440 | tf_op jit(solution)/shard_map/ppermute | solution.py:230
  27.9 11.1 %collective-permute-start.5 = (bf16[64,2048]{1,0:T(8,128)(2,1)S(1)}, bf16[64,2048]{1,0:T(8,128)(2,1)S(1)}, u32[]{:S(2)}, u32[]{:S(2)}) collective-permute-start(bf16[64,2048]{1,0:T(8,128)(2,1)S(1)} %get-tuple-element.39), channel_id=1, source_target_pairs={{0,1},{1,0},{2,3},{3,2},{4,5},{5,4},{6,7},{7,6},{8,9},{9,8},{10,11... | collective-permute-start | bytes 786440 | tf_op jit(solution)/shard_map/ppermute | solution.py:230
  28.0 2.7 %collective-permute-start.7 = (bf16[64,2176]{1,0:T(8,128)(2,1)S(1)}, bf16[64,2176]{1,0:T(8,128)(2,1)S(1)}, u32[]{:S(2)}, u32[]{:S(2)}) collective-permute-start(bf16[64,2176]{1,0:T(8,128)(2,1)S(1)} %collective-permute-done.6.refs_0_), channel_id=1, source_target_pairs={{0,1},{1,0},{2,3},{3,2},{4,5},{5,4},{6,7},{7,6},{8,9},{9,8},{10,11... | collective-permute-start | bytes 835592 | tf_op jit(solution)/shard_map/ppermute | solution.py:230
  29.0 9.5 %collective-permute-start.10 = (bf16[64,2048]{1,0:T(8,128)(2,1)S(1)}, bf16[64,2048]{1,0:T(8,128)(2,1)S(1)}, u32[]{:S(2)}, u32[]{:S(2)}) collective-permute-start(bf16[64,2048]{1,0:T(8,128)(2,1)S(1)} %add_convert_fusion), channel_id=1, source_target_pairs={{2,6},{3,7},{4,0},{5,1},{0,2},{1,3},{6,4},{7,5},{10,14},{11,15},{1... | collective-permute-start | bytes 786440 | tf_op jit(solution)/shard_map/ppermute | solution.py:230
  30.7 8.3 %copy-start = (f32[2048]{0:T(1024)S(1)}, f32[2048]{0:T(1024)}, u32[]{:S(2)}) copy-start(f32[2048]{0:T(1024)} %param.17) | copy-start | bytes 24580
  38.5 1.5 %collective-permute-start.12 = (bf16[64,2048]{1,0:T(8,128)(2,1)S(1)}, bf16[64,2048]{1,0:T(8,128)(2,1)S(1)}, u32[]{:S(2)}, u32[]{:S(2)}) collective-permute-start(bf16[64,2048]{1,0:T(8,128)(2,1)S(1)} %get-tuple-element.49), channel_id=1, source_target_pairs={{0,1},{1,0},{2,3},{3,2},{4,5},{5,4},{6,7},{7,6},{8,9},{9,8},{10,11... | collective-permute-start | bytes 786440 | tf_op jit(solution)/shard_map/ppermute | solution.py:230
  38.5 9.7 %collective-permute-start.11 = (bf16[64,2048]{1,0:T(8,128)(2,1)S(1)}, bf16[64,2048]{1,0:T(8,128)(2,1)S(1)}, u32[]{:S(2)}, u32[]{:S(2)}) collective-permute-start(bf16[64,2048]{1,0:T(8,128)(2,1)S(1)} %add_convert_fusion.1.near_ref), channel_id=1, source_target_pairs={{0,2},{1,3},{2,0},{3,1},{4,6},{5,7},{6,4},{7,5},{8,10},{9,11},{10,... | collective-permute-start | bytes 786440 | tf_op jit(solution)/shard_map/ppermute | solution.py:230
  40.3 14.4 %collective-permute-start.13 = (bf16[64,2048]{1,0:T(8,128)(2,1)S(1)}, bf16[64,2048]{1,0:T(8,128)(2,1)S(1)}, u32[]{:S(2)}, u32[]{:S(2)}) collective-permute-start(bf16[64,2048]{1,0:T(8,128)(2,1)S(1)} %get-tuple-element.52), channel_id=1, source_target_pairs={{0,6},{1,7},{2,4},{3,5},{4,2},{5,3},{6,0},{7,1},{8,14},{9,15},{10,... | collective-permute-start | bytes 786440 | tf_op jit(solution)/shard_map/ppermute | solution.py:230
  43.6 3.6 %collective-permute-start.14 = (f32[8,128]{1,0:T(8,128)S(1)}, f32[8,128]{1,0:T(8,128)S(1)}, u32[]{:S(2)}, u32[]{:S(2)}) collective-permute-start(f32[8,128]{1,0:T(8,128)S(1)} %get-tuple-element.53.score_ref), channel_id=1, source_target_pairs={{0,16},{8,24},{16,0},{24,8},{1,17},{9,25},{17,1},{25,9},{2,18},{10... | collective-permute-start | bytes 12296 | tf_op jit(solution)/shard_map/ppermute | solution.py:258
  47.2 7.3 %collective-permute-start.15 = (f32[2,8,128]{2,1,0:T(8,128)S(1)}, f32[2,8,128]{2,1,0:T(8,128)S(1)}, u32[]{:S(2)}, u32[]{:S(2)}) collective-permute-start(f32[2,8,128]{2,1,0:T(8,128)S(1)} %both_scores.1.both_ref), channel_id=1, source_target_pairs={{0,2},{1,3},{2,0},{3,1},{4,6},{5,7},{6,4},{7,5},{8,10},{9,11},{10,... | collective-permute-start | bytes 24584 | tf_op jit(solution)/shard_map/ppermute | solution.py:230
  47.2 7.4 %collective-permute-start.16 = (f32[2,8,128]{2,1,0:T(8,128)S(1)}, f32[2,8,128]{2,1,0:T(8,128)S(1)}, u32[]{:S(2)}, u32[]{:S(2)}) collective-permute-start(f32[2,8,128]{2,1,0:T(8,128)S(1)} %both_scores.1.both_ref), channel_id=1, source_target_pairs={{0,6},{1,7},{2,4},{3,5},{4,2},{5,3},{6,0},{7,1},{8,14},{9,15},{10,... | collective-permute-start | bytes 24584 | tf_op jit(solution)/shard_map/ppermute | solution.py:230

commit v4 on v3

--- a/solution.py
+++ b/solution.py
@@ -181,23 +181,20 @@
     return tile
 
 
-def own_kernel(own_ref, swapped_ref, near_ref, relayed_ref, head_ref, sum_ref, joins_ref, score_ref):
-    relayed = relayed_ref[...]
-    inner = on_inner_chip()
-    stays = relayed.astype(jnp.float32) * jnp.where(inner, 0.0, 1.0)
-    joins_ref[...] = (relayed.astype(jnp.float32) * jnp.where(inner, 1.0, 0.0)).astype(jnp.bfloat16)
+def third_kernel(sum_ref, relayed_ref, back_ref):
+    joins = relayed_ref[...].astype(jnp.float32) * jnp.where(on_inner_chip(), 1.0, 0.0)
+    back_ref[...] = (sum_ref[...] + joins).astype(jnp.bfloat16)
+
+
+def own_kernel(own_ref, swapped_ref, relayed_ref, near_ref, third_ref, head_ref, sum_ref, score_ref):
+    stays = relayed_ref[...].astype(jnp.float32) * jnp.where(on_inner_chip(), 0.0, 1.0)
     own = own_ref[...].astype(jnp.float32) + swapped_ref[...].astype(jnp.float32) + stays
     sum_ref[...] = own
     head = head_ref[...]
-    tile = score_tile(jnp.zeros(score_ref.shape, jnp.float32), 0, near_ref[...], head)
-    score_ref[...] = score_tile(tile, 2, own, head)
-
-
-def third_kernel(same_ref, swapped_ref, joins_ref, score_ref, head_ref, back_ref, out_score_ref):
-    back = same_ref[...].astype(jnp.float32) + swapped_ref[...].astype(jnp.float32)
-    back = (back + joins_ref[...].astype(jnp.float32)).astype(jnp.bfloat16)
-    back_ref[...] = back
-    out_score_ref[...] = score_tile(score_ref[...], 1, back, head_ref[...])
+    tile = jnp.zeros(score_ref.shape, jnp.float32)
+    for row, value in enumerate((near_ref[...], third_ref[...], own)):
+        tile = score_tile(tile, row, value, head)
+    score_ref[...] = tile
 
 
 def both_kernel(score_ref, partner_ref, both_ref):
@@ -257,9 +254,9 @@
         count = lax.axis_size("dp")
         return lax.ppermute(block, "dp", [(d, d ^ (count // 2)) for d in range(count)])
 
-    def chip_sum(sums):
+    def chip_sum(sums, dtype=jnp.bfloat16):
         same, other = sums
-        return (same.astype(jnp.float32) + core_swap(other).astype(jnp.float32)).astype(jnp.bfloat16)
+        return (same.astype(jnp.float32) + core_swap(other).astype(jnp.float32)).astype(dtype)
 
     def chip_route(*pairs):
         return [(2 * a + c, 2 * b + c) for a, b in pairs for c in (0, 1)]
@@ -267,36 +264,26 @@
     if chips == 4:
         far = exchange(x, 2)
         near = exchange(x, 1)
-        x_pair = pair(x)
-        far, near, x_pair, *weights = lax.optimization_barrier((far, near, x_pair, *weights))
+        near, far, x, *weights = lax.optimization_barrier((near, far, x, *weights))
         third = exchange(far, 1)
-        own_sums, near_sums, far_sums = ffn("experts_1", [x_pair, pair(near), pair(far)], experts, weights)
+        far_sums, near_sums = ffn("experts_far_near", [pair(far), pair(near)], experts, weights)
         far_back = chip_sum(far_sums)
         relayed = send(far_back, chip_route((1, 3), (2, 0), (0, 1), (3, 2)))
-        (third_sums,) = ffn("experts_2", [pair(third)], experts, weights)
-        third_same, third_other = third_sums
+        third_sums, own_sums = ffn("experts_third_own", [pair(third), pair(x)], experts, weights)
         near_back = chip_sum(near_sums)
-        third_other, near_back, relayed = lax.optimization_barrier((third_other, near_back, relayed))
+        third_same, near_back = lax.optimization_barrier((third_sums[0], near_back))
         near = exchange(near_back, 1)
-        head = score_head.reshape(1, width)
+        (third_back,) = local_call(
+            third_kernel, "third_back", [pltpu.VMEM((rows, width), jnp.bfloat16)], chip_sum((third_same, third_sums[1]), jnp.float32), relayed
+        )
+        third = exchange(third_back, 3)
         scores = (8, META)
-        own_sum, joins, score = local_call(
+        own_sum, score = local_call(
             own_kernel,
             "own_sum",
-            [
-                pltpu.VMEM((rows, width), jnp.float32),
-                pltpu.VMEM((rows, width), jnp.bfloat16),
-                pltpu.VMEM(scores, jnp.float32),
-            ],
-            *(own_sums[0], core_swap(own_sums[1]), near_back, relayed, head),
+            [pltpu.VMEM((rows, width), jnp.float32), pltpu.VMEM(scores, jnp.float32)],
+            *(own_sums[0], core_swap(own_sums[1]), relayed, near_back, third_back, score_head.reshape(1, width)),
         )
-        third_back, score = local_call(
-            third_kernel,
-            "third_back",
-            [pltpu.VMEM((rows, width), jnp.bfloat16), pltpu.VMEM(scores, jnp.float32)],
-            *(third_same, core_swap(third_other), joins, score, head),
-        )
-        third = exchange(third_back, 3)
         (both,) = local_call(
             both_kernel, "both_scores", [pltpu.VMEM((2, *scores), jnp.float32)], score, partner_of(score)
         )

time: 55.9 us -> 53.4 us (0.955)
  waiting for transfers between devices: 14.8 us -> 11.4 us
  starting transfers between devices: 16.7 us -> 18 us
    ppermute x16, waiting for transfers between devices: 12.7 us -> 9.34 us  [send(): return lax.ppermute(x, 'expert', route)]
    ppermute x16, starting transfers between devices: 15.2 us -> 16.4 us  [send(): return lax.ppermute(x, 'expert', route)]
  transfers between devices with their start and end apart: 17 -> 17, of which waited for: 8 -> 6; matrix products, arithmetic and copies ran while one was open for 0% -> 0% of each run, Pallas kernels for 38% -> 39%
where the time goes in v4:
time: 53.4 us; the launch traced here: 53.3 us
  Pallas kernels  22.9 us (43%)
  starting transfers between devices  18 us (34%)
  waiting for transfers between devices  11.4 us (21%)
  between operations  0.73 us (1%)
    ppermute x16, starting transfers between devices, send(): return lax.ppermute(x, 'expert', route)  16.4 us
    pallas_call x2, Pallas kernels, ffn(): pl.pallas_call(functools.partial(ffn_kernel, chips, experts), out_shape=[...  11.9 us
    ppermute x16, waiting for transfers between devices, send(): return lax.ppermute(x, 'expert', route)  9.34 us
    pallas_call x1, Pallas kernels, load(): pl.pallas_call(load_kernel, out_shape=[pltpu.VMEM(a.shape, a.dtype) for a...  8.34 us
    ppermute x1, waiting for transfers between devices, partner_of(): lax.ppermute(block, 'dp', [(d, d ^ count // 2) for d in range(count)])  2.07 us
    ppermute x1, starting transfers between devices, partner_of(): lax.ppermute(block, 'dp', [(d, d ^ count // 2) for d in range(count)])  1.6 us
    pallas_call x4, Pallas kernels, local_call(): pl.pallas_call(kernel, out_shape=out_shape, in_specs=[VMEM] * len(xs), ou...  1.43 us
    pallas_call x1, Pallas kernels, body(): pl.pallas_call(functools.partial(prep_kernel, experts), out_shape=pltpu.V...  1.26 us
  transfers between devices with their start and end apart: 17, of which 6 were waited for; matrix products, arithmetic and copies ran while one was open for 0% of the time, Pallas kernels for 39%

profile of v4, /device:TPU:0, one launch (start us, length us, event | category | flops | bytes accessed | tf_op | source)
XLA Modules:
  0.0 53.3 jit_solution(5616530221087821667)
XLA Ops:
  0.6 1.3 %prep.1.x_ref.refs_2_ = bf16[64,2176]{1,0:T(8,128)(2,1)S(1)} custom-call(bf16[64,2048]{1,0:T(8,128)(2,1)} %tok_ref.1, s32[8,64]{1,0:T(8,128)} %bitcast.4, s32[8,64]{1,0:T(8,128)} %bitcast.5, s32[4]{0:T(128)} %scorer_ref.1, bf16[2,2048]{1,0:T(2,128)(2,1)} %tags_ref.1), custom_call_target="tpu_custom_call" | custom-call | tf_op jit(solution)/shard_map/prep/pallas_call | solution.py:235
  1.9 4.1 %collective-permute-start.1 = (bf16[64,2176]{1,0:T(8,128)(2,1)S(1)}, bf16[64,2176]{1,0:T(8,128)(2,1)S(1)}, u32[]{:S(2)}, u32[]{:S(2)}) collective-permute-start(bf16[64,2176]{1,0:T(8,128)(2,1)S(1)} %prep.1.x_ref.refs_2_), channel_id=1, source_target_pairs={{0,4},{1,5},{2,6},{3,7},{4,0},{5,1},{6,2},{7,3},{8,12},{9,13},{10,... | collective-permute-start | bytes 835592 | tf_op jit(solution)/shard_map/ppermute | solution.py:227
  6.0 1.6 %collective-permute-start = (bf16[64,2176]{1,0:T(8,128)(2,1)S(1)}, bf16[64,2176]{1,0:T(8,128)(2,1)S(1)}, u32[]{:S(2)}, u32[]{:S(2)}) collective-permute-start(bf16[64,2176]{1,0:T(8,128)(2,1)S(1)} %prep.1.x_ref.refs_2_), channel_id=1, source_target_pairs={{0,2},{1,3},{2,0},{3,1},{4,6},{5,7},{6,4},{7,5},{8,10},{9,11},{10,... | collective-permute-start | bytes 835592 | tf_op jit(solution)/shard_map/ppermute | solution.py:227
  7.6 8.3 %load_weights.1 = (bf16[4,2048,512]{2,1,0:T(8,128)(2,1)S(1)}, bf16[4,2048,512]{2,1,0:T(8,128)(2,1)S(1)}, bf16[4,512,2048]{2,1,0:T(8,128)(2,1)S(1)}) custom-call(bf16[64,2176]{1,0:T(8,128)(2,1)S(1)} %prep.1.x_ref.refs_2_, bf16[4,2048,512]{2,1,0:T(8,128)(2,1)} %refs_0_.1, bf16[4,2048,512]{2,1,0:T(8,128)(2,1)} %refs_1_.1, bf16[4,512,2048]{2,1,0:T(8,128)(2,1)} %refs_2_.1), custom_call_target="tpu_custom_call" | custom-call | bytes 25165824 | tf_op jit(solution)/shard_map/load_weights/pallas_call | solution.py:109
  15.9 2.8 %collective-permute-done.1.refs_0_ = bf16[64,2176]{1,0:T(8,128)(2,1)S(1)} collective-permute-done((bf16[64,2176]{1,0:T(8,128)(2,1)S(1)}, bf16[64,2176]{1,0:T(8,128)(2,1)S(1)}, u32[]{:S(2)}, u32[]{:S(2)}) %collective-permute-start.1) | collective-permute-done | bytes 278560 | tf_op jit(solution)/shard_map/ppermute | solution.py:227
  18.7 0.2 collective-permute-done.refs_2_
  18.9 0.0 collective-permute-start.7
  18.9 0.5 collective-permute-start.6
  19.4 1.5 %collective-permute-start.2 = (bf16[64,2176]{1,0:T(8,128)(2,1)S(1)}, bf16[64,2176]{1,0:T(8,128)(2,1)S(1)}, u32[]{:S(2)}, u32[]{:S(2)}) collective-permute-start(bf16[64,2176]{1,0:T(8,128)(2,1)S(1)} %collective-permute-done.1.refs_0_), channel_id=1, source_target_pairs={{0,2},{1,3},{2,0},{3,1},{4,6},{5,7},{6,4},{7,5},{8,10},{9,11},{10,... | collective-permute-start | bytes 835592 | tf_op jit(solution)/shard_map/ppermute | solution.py:227
  20.9 0.0 collective-permute-done.7.refs_3_
  20.9 0.0 collective-permute-done.6.refs_1_
  20.9 5.9 %experts_far_near.1 = (bf16[64,2048]{1,0:T(8,128)(2,1)S(1)}, bf16[64,2048]{1,0:T(8,128)(2,1)S(1)}, bf16[64,2048]{1,0:T(8,128)(2,1)S(1)}, bf16[64,2048]{1,0:T(8,128)(2,1)S(1)}) custom-call(bf16[64,2176]{1,0:T(8,128)(2,1)S(1)} %collective-permute-done.1.refs_0_, bf16[64,2176]{1,0:T(8,128)(2,1)S(1)} %collective-permute-done.6.refs_1_, ...), custom_call_target="tpu_custom_call" | custom-call | flops 2415919104 | bytes 25165824 | tf_op jit(solution)/shard_map/experts_far_near/pallas_call | solution.py:133
  26.9 0.2 collective-permute-start.8
  27.0 0.4 collective-permute-start.4
  27.4 0.1 collective-permute-start.10
  27.5 0.5 collective-permute-done.2.refs_0_
  28.0 0.0 collective-permute-start.3
  28.0 0.5 collective-permute-done.8
  28.5 0.1 add_convert_fusion.1
  28.5 0.0 copy-start
  28.5 1.5 %collective-permute-start.9 = (bf16[64,2048]{1,0:T(8,128)(2,1)S(1)}, bf16[64,2048]{1,0:T(8,128)(2,1)S(1)}, u32[]{:S(2)}, u32[]{:S(2)}) collective-permute-start(bf16[64,2048]{1,0:T(8,128)(2,1)S(1)} %add_convert_fusion.1), channel_id=1, source_target_pairs={{2,6},{3,7},{4,0},{5,1},{0,2},{1,3},{6,4},{7,5},{10,14},{11,15},{1... | collective-permute-start | bytes 786440 | tf_op jit(solution)/shard_map/ppermute | solution.py:227
  30.1 0.0 collective-permute-done.4.refs_3_
  30.1 0.0 collective-permute-done.3.refs_1_
  30.1 5.9 %experts_third_own.1 = (bf16[64,2048]{1,0:T(8,128)(2,1)S(1)}, bf16[64,2048]{1,0:T(8,128)(2,1)S(1)}, bf16[64,2048]{1,0:T(8,128)(2,1)S(1)}, bf16[64,2048]{1,0:T(8,128)(2,1)S(1)}) custom-call(bf16[64,2176]{1,0:T(8,128)(2,1)S(1)} %collective-permute-done.2.refs_0_, bf16[64,2176]{1,0:T(8,128)(2,1)S(1)} %collective-permute-done.3.refs_1_, ...), custom_call_target="tpu_custom_call" | custom-call | flops 2415919104 | bytes 25165824 | tf_op jit(solution)/shard_map/experts_third_own/pallas_call | solution.py:133
  36.0 0.1 collective-permute-start.11
  36.1 0.0 collective-permute-done.10
  36.1 0.1 add_convert_fusion.near_ref
  36.2 2.4 %collective-permute-start.12 = (bf16[64,2048]{1,0:T(8,128)(2,1)S(1)}, bf16[64,2048]{1,0:T(8,128)(2,1)S(1)}, u32[]{:S(2)}, u32[]{:S(2)}) collective-permute-start(bf16[64,2048]{1,0:T(8,128)(2,1)S(1)} %add_convert_fusion.near_ref), channel_id=1, source_target_pairs={{0,2},{1,3},{2,0},{3,1},{4,6},{5,7},{6,4},{7,5},{8,10},{9,11},{10,... | collective-permute-start | bytes 786440 | tf_op jit(solution)/shard_map/ppermute | solution.py:227
  38.6 0.2 collective-permute-start.5
  38.8 0.0 collective-permute-done.11
  38.8 0.1 convert_add_fusion.sum_ref
  38.9 0.0 collective-permute-done.9.relayed_ref
  38.9 0.1 third_back.1.third_ref
  38.9 2.3 %collective-permute-start.13 = (bf16[64,2048]{1,0:T(8,128)(2,1)S(1)}, bf16[64,2048]{1,0:T(8,128)(2,1)S(1)}, u32[]{:S(2)}, u32[]{:S(2)}) collective-permute-start(bf16[64,2048]{1,0:T(8,128)(2,1)S(1)} %third_back.1.third_ref), channel_id=1, source_target_pairs={{0,6},{1,7},{2,4},{3,5},{4,2},{5,3},{6,0},{7,1},{8,14},{9,15},{10,... | collective-permute-start | bytes 786440 | tf_op jit(solution)/shard_map/ppermute | solution.py:227
  41.2 0.0 collective-permute-done.5.swapped_ref
  41.2 0.0 copy-done
  41.2 0.4 own_sum.1
  41.6 1.6 %collective-permute-start.14 = (f32[8,128]{1,0:T(8,128)S(1)}, f32[8,128]{1,0:T(8,128)S(1)}, u32[]{:S(2)}, u32[]{:S(2)}) collective-permute-start(f32[8,128]{1,0:T(8,128)S(1)} %get-tuple-element.43.score_ref), channel_id=1, source_target_pairs={{0,16},{8,24},{16,0},{24,8},{1,17},{9,25},{17,1},{25,9},{2,18},{10... | collective-permute-start | bytes 12296 | tf_op jit(solution)/shard_map/ppermute | solution.py:255
  43.2 2.1 %collective-permute-done.14.partner_ref = f32[8,128]{1,0:T(8,128)S(1)} collective-permute-done((f32[8,128]{1,0:T(8,128)S(1)}, f32[8,128]{1,0:T(8,128)S(1)}, u32[]{:S(2)}, u32[]{:S(2)}) %collective-permute-start.14) | collective-permute-done | bytes 4128 | tf_op jit(solution)/shard_map/ppermute | solution.py:255
  45.3 1.6 %collective-permute-start.16 = (f32[2,8,128]{2,1,0:T(8,128)S(1)}, f32[2,8,128]{2,1,0:T(8,128)S(1)}, u32[]{:S(2)}, u32[]{:S(2)}) collective-permute-start(f32[2,8,128]{2,1,0:T(8,128)S(1)} %both_scores.1.both_ref), channel_id=1, source_target_pairs={{0,6},{1,7},{2,4},{3,5},{4,2},{5,3},{6,0},{7,1},{8,14},{9,15},{10,... | collective-permute-start | bytes 24584 | tf_op jit(solution)/shard_map/ppermute | solution.py:227
  46.9 0.0 collective-permute-start.15
  46.9 0.0 collective-permute-done.12.near_ref
  47.0 5.4 %collective-permute-done.16.from_third_ref = f32[2,8,128]{2,1,0:T(8,128)S(1)} collective-permute-done((f32[2,8,128]{2,1,0:T(8,128)S(1)}, f32[2,8,128]{2,1,0:T(8,128)S(1)}, u32[]{:S(2)}, u32[]{:S(2)}) %collective-permute-start.16) | collective-permute-done | bytes 8224 | tf_op jit(solution)/shard_map/ppermute | solution.py:227
  52.3 0.0 collective-permute-done.15.from_near_ref
  52.3 0.0 collective-permute-done.13.third_ref
  52.3 0.9 %mixed.1 = (bf16[64,2048]{1,0:T(8,128)(2,1)}, f32[4]{0:T(128)}) custom-call(f32[64,2048]{1,0:T(8,128)S(1)} %get-tuple-element.42.sum_ref, bf16[64,2048]{1,0:T(8,128)(2,1)S(1)} %collective-permute-done.12.near_ref, bf16[64,2048]{1,0:T(8,128)(2,1)S(1)} %collective-permute-done.13.third_ref, f32[2,8,128]{2,1,0:T(8,128)S(1)} %both_scores.1.both_ref, ...), custom_call_target="tpu_custom_call" | custom-call | tf_op jit(solution)/shard_map/mixed/pallas_call | solution.py:216
  (1 shorter events, 0.0 us)
Async XLA Ops:
  1.9 16.8 %collective-permute-start.1 = (bf16[64,2176]{1,0:T(8,128)(2,1)S(1)}, bf16[64,2176]{1,0:T(8,128)(2,1)S(1)}, u32[]{:S(2)}, u32[]{:S(2)}) collective-permute-start(bf16[64,2176]{1,0:T(8,128)(2,1)S(1)} %prep.1.x_ref.refs_2_), channel_id=1, source_target_pairs={{0,4},{1,5},{2,6},{3,7},{4,0},{5,1},{6,2},{7,3},{8,12},{9,13},{10,... | collective-permute-start | bytes 835592 | tf_op jit(solution)/shard_map/ppermute | solution.py:227
  6.0 12.9 %collective-permute-start = (bf16[64,2176]{1,0:T(8,128)(2,1)S(1)}, bf16[64,2176]{1,0:T(8,128)(2,1)S(1)}, u32[]{:S(2)}, u32[]{:S(2)}) collective-permute-start(bf16[64,2176]{1,0:T(8,128)(2,1)S(1)} %prep.1.x_ref.refs_2_), channel_id=1, source_target_pairs={{0,2},{1,3},{2,0},{3,1},{4,6},{5,7},{6,4},{7,5},{8,10},{9,11},{10,... | collective-permute-start | bytes 835592 | tf_op jit(solution)/shard_map/ppermute | solution.py:227
  18.9 2.0 %collective-permute-start.7 = (bf16[64,2176]{1,0:T(8,128)(2,1)S(1)}, bf16[64,2176]{1,0:T(8,128)(2,1)S(1)}, u32[]{:S(2)}, u32[]{:S(2)}) collective-permute-start(bf16[64,2176]{1,0:T(8,128)(2,1)S(1)} %collective-permute-done.refs_2_), channel_id=1, source_target_pairs={{0,1},{1,0},{2,3},{3,2},{4,5},{5,4},{6,7},{7,6},{8,9},{9,8},{10,11... | collective-permute-start | bytes 835592 | tf_op jit(solution)/shard_map/ppermute | solution.py:227
  18.9 2.0 %collective-permute-start.6 = (bf16[64,2176]{1,0:T(8,128)(2,1)S(1)}, bf16[64,2176]{1,0:T(8,128)(2,1)S(1)}, u32[]{:S(2)}, u32[]{:S(2)}) collective-permute-start(bf16[64,2176]{1,0:T(8,128)(2,1)S(1)} %collective-permute-done.1.refs_0_), channel_id=1, source_target_pairs={{0,1},{1,0},{2,3},{3,2},{4,5},{5,4},{6,7},{7,6},{8,9},{9,8},{10,11... | collective-permute-start | bytes 835592 | tf_op jit(solution)/shard_map/ppermute | solution.py:227
  19.4 8.6 %collective-permute-start.2 = (bf16[64,2176]{1,0:T(8,128)(2,1)S(1)}, bf16[64,2176]{1,0:T(8,128)(2,1)S(1)}, u32[]{:S(2)}, u32[]{:S(2)}) collective-permute-start(bf16[64,2176]{1,0:T(8,128)(2,1)S(1)} %collective-permute-done.1.refs_0_), channel_id=1, source_target_pairs={{0,2},{1,3},{2,0},{3,1},{4,6},{5,7},{6,4},{7,5},{8,10},{9,11},{10,... | collective-permute-start | bytes 835592 | tf_op jit(solution)/shard_map/ppermute | solution.py:227
  26.9 1.6 %collective-permute-start.8 = (bf16[64,2048]{1,0:T(8,128)(2,1)S(1)}, bf16[64,2048]{1,0:T(8,128)(2,1)S(1)}, u32[]{:S(2)}, u32[]{:S(2)}) collective-permute-start(bf16[64,2048]{1,0:T(8,128)(2,1)S(1)} %get-tuple-element.35), channel_id=1, source_target_pairs={{0,1},{1,0},{2,3},{3,2},{4,5},{5,4},{6,7},{7,6},{8,9},{9,8},{10,11... | collective-permute-start | bytes 786440 | tf_op jit(solution)/shard_map/ppermute | solution.py:227
  27.0 3.0 %collective-permute-start.4 = (bf16[64,2176]{1,0:T(8,128)(2,1)S(1)}, bf16[64,2176]{1,0:T(8,128)(2,1)S(1)}, u32[]{:S(2)}, u32[]{:S(2)}) collective-permute-start(bf16[64,2176]{1,0:T(8,128)(2,1)S(1)} %prep.1.x_ref.refs_2_), channel_id=1, source_target_pairs={{0,1},{1,0},{2,3},{3,2},{4,5},{5,4},{6,7},{7,6},{8,9},{9,8},{10,11... | collective-permute-start | bytes 835592 | tf_op jit(solution)/shard_map/ppermute | solution.py:227
  27.4 8.7 %collective-permute-start.10 = (bf16[64,2048]{1,0:T(8,128)(2,1)S(1)}, bf16[64,2048]{1,0:T(8,128)(2,1)S(1)}, u32[]{:S(2)}, u32[]{:S(2)}) collective-permute-start(bf16[64,2048]{1,0:T(8,128)(2,1)S(1)} %get-tuple-element.38), channel_id=1, source_target_pairs={{0,1},{1,0},{2,3},{3,2},{4,5},{5,4},{6,7},{7,6},{8,9},{9,8},{10,11... | collective-permute-start | bytes 786440 | tf_op jit(solution)/shard_map/ppermute | solution.py:227
  28.0 2.1 %collective-permute-start.3 = (bf16[64,2176]{1,0:T(8,128)(2,1)S(1)}, bf16[64,2176]{1,0:T(8,128)(2,1)S(1)}, u32[]{:S(2)}, u32[]{:S(2)}) collective-permute-start(bf16[64,2176]{1,0:T(8,128)(2,1)S(1)} %collective-permute-done.2.refs_0_), channel_id=1, source_target_pairs={{0,1},{1,0},{2,3},{3,2},{4,5},{5,4},{6,7},{7,6},{8,9},{9,8},{10,11... | collective-permute-start | bytes 835592 | tf_op jit(solution)/shard_map/ppermute | solution.py:227
  28.5 12.7 %copy-start = (f32[2048]{0:T(1024)S(1)}, f32[2048]{0:T(1024)}, u32[]{:S(2)}) copy-start(f32[2048]{0:T(1024)} %param.17) | copy-start | bytes 24580
  28.5 10.3 %collective-permute-start.9 = (bf16[64,2048]{1,0:T(8,128)(2,1)S(1)}, bf16[64,2048]{1,0:T(8,128)(2,1)S(1)}, u32[]{:S(2)}, u32[]{:S(2)}) collective-permute-start(bf16[64,2048]{1,0:T(8,128)(2,1)S(1)} %add_convert_fusion.1), channel_id=1, source_target_pairs={{2,6},{3,7},{4,0},{5,1},{0,2},{1,3},{6,4},{7,5},{10,14},{11,15},{1... | collective-permute-start | bytes 786440 | tf_op jit(solution)/shard_map/ppermute | solution.py:227
  36.0 2.8 %collective-permute-start.11 = (bf16[64,2048]{1,0:T(8,128)(2,1)S(1)}, bf16[64,2048]{1,0:T(8,128)(2,1)S(1)}, u32[]{:S(2)}, u32[]{:S(2)}) collective-permute-start(bf16[64,2048]{1,0:T(8,128)(2,1)S(1)} %get-tuple-element.41), channel_id=1, source_target_pairs={{0,1},{1,0},{2,3},{3,2},{4,5},{5,4},{6,7},{7,6},{8,9},{9,8},{10,11... | collective-permute-start | bytes 786440 | tf_op jit(solution)/shard_map/ppermute | solution.py:227
  36.2 10.8 %collective-permute-start.12 = (bf16[64,2048]{1,0:T(8,128)(2,1)S(1)}, bf16[64,2048]{1,0:T(8,128)(2,1)S(1)}, u32[]{:S(2)}, u32[]{:S(2)}) collective-permute-start(bf16[64,2048]{1,0:T(8,128)(2,1)S(1)} %add_convert_fusion.near_ref), channel_id=1, source_target_pairs={{0,2},{1,3},{2,0},{3,1},{4,6},{5,7},{6,4},{7,5},{8,10},{9,11},{10,... | collective-permute-start | bytes 786440 | tf_op jit(solution)/shard_map/ppermute | solution.py:227
  38.6 2.6 %collective-permute-start.5 = (bf16[64,2048]{1,0:T(8,128)(2,1)S(1)}, bf16[64,2048]{1,0:T(8,128)(2,1)S(1)}, u32[]{:S(2)}, u32[]{:S(2)}) collective-permute-start(bf16[64,2048]{1,0:T(8,128)(2,1)S(1)} %get-tuple-element.32), channel_id=1, source_target_pairs={{0,1},{1,0},{2,3},{3,2},{4,5},{5,4},{6,7},{7,6},{8,9},{9,8},{10,11... | collective-permute-start | bytes 786440 | tf_op jit(solution)/shard_map/ppermute | solution.py:227
  38.9 13.4 %collective-permute-start.13 = (bf16[64,2048]{1,0:T(8,128)(2,1)S(1)}, bf16[64,2048]{1,0:T(8,128)(2,1)S(1)}, u32[]{:S(2)}, u32[]{:S(2)}) collective-permute-start(bf16[64,2048]{1,0:T(8,128)(2,1)S(1)} %third_back.1.third_ref), channel_id=1, source_target_pairs={{0,6},{1,7},{2,4},{3,5},{4,2},{5,3},{6,0},{7,1},{8,14},{9,15},{10,... | collective-permute-start | bytes 786440 | tf_op jit(solution)/shard_map/ppermute | solution.py:227
  41.6 3.7 %collective-permute-start.14 = (f32[8,128]{1,0:T(8,128)S(1)}, f32[8,128]{1,0:T(8,128)S(1)}, u32[]{:S(2)}, u32[]{:S(2)}) collective-permute-start(f32[8,128]{1,0:T(8,128)S(1)} %get-tuple-element.43.score_ref), channel_id=1, source_target_pairs={{0,16},{8,24},{16,0},{24,8},{1,17},{9,25},{17,1},{25,9},{2,18},{10... | collective-permute-start | bytes 12296 | tf_op jit(solution)/shard_map/ppermute | solution.py:255
  45.3 7.0 %collective-permute-start.16 = (f32[2,8,128]{2,1,0:T(8,128)S(1)}, f32[2,8,128]{2,1,0:T(8,128)S(1)}, u32[]{:S(2)}, u32[]{:S(2)}) collective-permute-start(f32[2,8,128]{2,1,0:T(8,128)S(1)} %both_scores.1.both_ref), channel_id=1, source_target_pairs={{0,6},{1,7},{2,4},{3,5},{4,2},{5,3},{6,0},{7,1},{8,14},{9,15},{10,... | collective-permute-start | bytes 24584 | tf_op jit(solution)/shard_map/ppermute | solution.py:227
  46.9 5.4 %collective-permute-start.15 = (f32[2,8,128]{2,1,0:T(8,128)S(1)}, f32[2,8,128]{2,1,0:T(8,128)S(1)}, u32[]{:S(2)}, u32[]{:S(2)}) collective-permute-start(f32[2,8,128]{2,1,0:T(8,128)S(1)} %both_scores.1.both_ref), channel_id=1, source_target_pairs={{0,2},{1,3},{2,0},{3,1},{4,6},{5,7},{6,4},{7,5},{8,10},{9,11},{10,... | collective-permute-start | bytes 24584 | tf_op jit(solution)/shard_map/ppermute | solution.py:227

commit v5 on v4

--- a/solution.py
+++ b/solution.py
@@ -55,12 +55,49 @@
     return hit.astype(jnp.float32).astype(jnp.bfloat16)
 
 
-def ffn_kernel(chips, experts, *refs):
+def hidden_rows(x, weight, w_gate, w_up):
+    gate = jnp.dot(x, w_gate, preferred_element_type=jnp.float32)
+    up = jnp.dot(x, w_up, preferred_element_type=jnp.float32)
+    return (gate / (1.0 + jnp.exp(-gate)) * up * weight).astype(jnp.bfloat16)
+
+
+def expert_weight(meta, expert, experts):
+    lane = lax.broadcasted_iota(jnp.int32, meta.shape, 1)
+    mine = (lane == expert) | (lane == expert + experts)
+    return jnp.sum(jnp.where(mine, meta, 0.0), axis=1, keepdims=True)
+
+
+def all_rows_kernel(experts, *refs):
+    x_refs, (wg, wu, wd), out_refs, (x_ref,) = refs[:2], refs[2:5], refs[5:7], refs[7:]
+    per_device, width, ff = wg.shape
+    rows = x_refs[0].shape[0]
+    first = lax.axis_index("expert") * per_device
+    for i, ref in enumerate(x_refs):
+        x_ref[i * rows : (i + 1) * rows, :] = ref[...]
+    meta = x_ref[:, width:].astype(jnp.float32)
+
+    def hidden_of(e):
+        return hidden_rows(x_ref[:, 0:width], expert_weight(meta, first + e, experts), wg[e], wu[e])
+
+    out = 0.0
+    hidden = hidden_of(0)
+    for e in range(1, per_device):
+        following = hidden_of(e)
+        out = out + jnp.dot(hidden, wd[e - 1], preferred_element_type=jnp.float32)
+        hidden = following
+    out = out + jnp.dot(hidden, wd[per_device - 1], preferred_element_type=jnp.float32)
+    for i, ref in enumerate(out_refs):
+        ref[...] = out[i * rows : (i + 1) * rows].astype(jnp.bfloat16)
+
+
+def picked_rows_kernel(chips, experts, *refs):
     x_refs, (wg, wu, wd), refs = refs[: 2 * chips], refs[2 * chips : 2 * chips + 3], refs[2 * chips + 3 :]
     out_refs, (g_ref, pick_ref, o_ref) = refs[: 2 * chips], refs[2 * chips :]
     per_device, width, ff = wg.shape
     room = 2 * MOST
     first = lax.axis_index("expert") * per_device
+    if g_ref.shape[1] > chips * room:
+        g_ref[:, chips * room :, :] = jnp.zeros_like(g_ref[:, chips * room :, :])
     for k in range(chips):
         x = jnp.concatenate([x_refs[2 * k][...], x_refs[2 * k + 1][...]], axis=0)
         pick = pick_rows(x[:, width:].astype(jnp.float32), first, per_device, experts)
@@ -69,18 +106,22 @@
         picked = picked.astype(jnp.bfloat16)
         for e in range(per_device):
             g_ref[e, k * room : (k + 1) * room, :] = picked[e * room : (e + 1) * room, :]
-    lane = lax.broadcasted_iota(jnp.int32, (chips * room, META), 1)
-    for e in range(per_device):
-        x = g_ref[e, :, 0:width]
+
+    def hidden_of(e):
         meta = g_ref[e, :, width:].astype(jnp.float32)
-        mine = (lane == first + e) | (lane == first + e + experts)
-        weight = jnp.sum(jnp.where(mine, meta, 0.0), axis=1, keepdims=True)
-        gate = jnp.dot(x, wg[e], preferred_element_type=jnp.float32)
-        up = jnp.dot(x, wu[e], preferred_element_type=jnp.float32)
-        hidden = (gate / (1.0 + jnp.exp(-gate)) * up * weight).astype(jnp.bfloat16)
+        return hidden_rows(g_ref[e, :, 0:width], expert_weight(meta, first + e, experts), wg[e], wu[e])
+
+    def leave(e, hidden):
         out = jnp.dot(hidden, wd[e], preferred_element_type=jnp.float32).astype(jnp.bfloat16)
         for k in range(chips):
             o_ref[k, e * room : (e + 1) * room, :] = out[k * room : (k + 1) * room, :]
+
+    hidden = hidden_of(0)
+    for e in range(1, per_device):
+        following = hidden_of(e)
+        leave(e - 1, hidden)
+        hidden = following
+    leave(per_device - 1, hidden)
     for k in range(chips):
         rows = jnp.dot(pick_ref[k], o_ref[k], preferred_element_type=jnp.float32).astype(jnp.bfloat16)
         half = rows.shape[0] // 2
@@ -130,19 +171,27 @@
     rows = xs[0].shape[0]
     chips = len(sources)
     room = 2 * MOST
+    if chips == 1:
+        met = 2 * rows
+        kernel = functools.partial(all_rows_kernel, experts)
+        scratch = [pltpu.VMEM((met, width + META), jnp.bfloat16)]
+    else:
+        met = -(-chips * room // META) * META
+        kernel = functools.partial(picked_rows_kernel, chips, experts)
+        scratch = [
+            pltpu.VMEM((per_device, met, width + META), jnp.bfloat16),
+            pltpu.VMEM((chips, 2 * rows, per_device * room), jnp.bfloat16),
+            pltpu.VMEM((chips, per_device * room, width), jnp.bfloat16),
+        ]
     outs = pl.pallas_call(
-        functools.partial(ffn_kernel, chips, experts),
+        kernel,
         out_shape=[pltpu.VMEM((rows, width), jnp.bfloat16)] * (2 * chips),
         in_specs=[VMEM] * (len(xs) + 3),
         out_specs=[VMEM] * (2 * chips),
-        scratch_shapes=[
-            pltpu.VMEM((per_device, chips * room, width + META), jnp.bfloat16),
-            pltpu.VMEM((chips, 2 * rows, per_device * room), jnp.bfloat16),
-            pltpu.VMEM((chips, per_device * room, width), jnp.bfloat16),
-        ],
+        scratch_shapes=scratch,
         compiler_params=pltpu.CompilerParams(vmem_limit_bytes=16 * MIB),
         cost_estimate=pl.CostEstimate(
-            flops=6 * per_device * chips * room * width * ff,
+            flops=6 * per_device * met * width * ff,
             bytes_accessed=6 * per_device * width * ff,
             transcendentals=0,
         ),

time: 53.4 us -> 52 us (0.974)
  Pallas kernels: 22.9 us -> 20.8 us
  waiting for transfers between devices: 11.4 us -> 12.1 us
    pallas_call x2, Pallas kernels: 11.9 us -> 9.75 us  [ffn(): pl.pallas_call(kernel, out_shape=[pltpu.VMEM((rows, width), jnp.bfloat16)...]
    ppermute x16, waiting for transfers between devices: 9.34 us -> 10.1 us  [send(): return lax.ppermute(x, 'expert', route)]
  transfers between devices with their start and end apart: 17 -> 17, of which waited for: 6 -> 6; matrix products, arithmetic and copies ran while one was open for 0% -> 0% of each run, Pallas kernels for 39% -> 36%
where the time goes in v5:
time: 52 us; the launch traced here: 51.9 us
  Pallas kernels  20.8 us (40%)
  starting transfers between devices  18.1 us (35%)
  waiting for transfers between devices  12.1 us (23%)
  between operations  0.71 us (1%)
    ppermute x16, starting transfers between devices, send(): return lax.ppermute(x, 'expert', route)  16.5 us
    ppermute x16, waiting for transfers between devices, send(): return lax.ppermute(x, 'expert', route)  10.1 us
    pallas_call x2, Pallas kernels, ffn(): pl.pallas_call(kernel, out_shape=[pltpu.VMEM((rows, width), jnp.bfloat16)...  9.75 us
    pallas_call x1, Pallas kernels, load(): pl.pallas_call(load_kernel, out_shape=[pltpu.VMEM(a.shape, a.dtype) for a...  8.34 us
    ppermute x1, waiting for transfers between devices, partner_of(): lax.ppermute(block, 'dp', [(d, d ^ count // 2) for d in range(count)])  2.09 us
    ppermute x1, starting transfers between devices, partner_of(): lax.ppermute(block, 'dp', [(d, d ^ count // 2) for d in range(count)])  1.58 us
    pallas_call x4, Pallas kernels, local_call(): pl.pallas_call(kernel, out_shape=out_shape, in_specs=[VMEM] * len(xs), ou...  1.42 us
    pallas_call x1, Pallas kernels, body(): pl.pallas_call(functools.partial(prep_kernel, experts), out_shape=pltpu.V...  1.26 us
  transfers between devices with their start and end apart: 17, of which 6 were waited for; matrix products, arithmetic and copies ran while one was open for 0% of the time, Pallas kernels for 36%

profile of v5, /device:TPU:0, one launch (start us, length us, event | category | flops | bytes accessed | tf_op | source)
XLA Modules:
  0.0 51.9 jit_solution(2693928494620520524)
XLA Ops:
  0.6 1.3 %prep.1.x_ref.refs_2_ = bf16[64,2176]{1,0:T(8,128)(2,1)S(1)} custom-call(bf16[64,2048]{1,0:T(8,128)(2,1)} %tok_ref.1, s32[8,64]{1,0:T(8,128)} %bitcast.4, s32[8,64]{1,0:T(8,128)} %bitcast.5, s32[4]{0:T(128)} %scorer_ref.1, bf16[2,2048]{1,0:T(2,128)(2,1)} %tags_ref.1), custom_call_target="tpu_custom_call" | custom-call | tf_op jit(solution)/shard_map/prep/pallas_call | solution.py:284
  1.9 4.1 %collective-permute-start.1 = (bf16[64,2176]{1,0:T(8,128)(2,1)S(1)}, bf16[64,2176]{1,0:T(8,128)(2,1)S(1)}, u32[]{:S(2)}, u32[]{:S(2)}) collective-permute-start(bf16[64,2176]{1,0:T(8,128)(2,1)S(1)} %prep.1.x_ref.refs_2_), channel_id=1, source_target_pairs={{0,4},{1,5},{2,6},{3,7},{4,0},{5,1},{6,2},{7,3},{8,12},{9,13},{10,... | collective-permute-start | bytes 835592 | tf_op jit(solution)/shard_map/ppermute | solution.py:276
  6.0 1.6 %collective-permute-start = (bf16[64,2176]{1,0:T(8,128)(2,1)S(1)}, bf16[64,2176]{1,0:T(8,128)(2,1)S(1)}, u32[]{:S(2)}, u32[]{:S(2)}) collective-permute-start(bf16[64,2176]{1,0:T(8,128)(2,1)S(1)} %prep.1.x_ref.refs_2_), channel_id=1, source_target_pairs={{0,2},{1,3},{2,0},{3,1},{4,6},{5,7},{6,4},{7,5},{8,10},{9,11},{10,... | collective-permute-start | bytes 835592 | tf_op jit(solution)/shard_map/ppermute | solution.py:276
  7.6 8.3 %load_weights.1 = (bf16[4,2048,512]{2,1,0:T(8,128)(2,1)S(1)}, bf16[4,2048,512]{2,1,0:T(8,128)(2,1)S(1)}, bf16[4,512,2048]{2,1,0:T(8,128)(2,1)S(1)}) custom-call(bf16[64,2176]{1,0:T(8,128)(2,1)S(1)} %prep.1.x_ref.refs_2_, bf16[4,2048,512]{2,1,0:T(8,128)(2,1)} %refs_0_.1, bf16[4,2048,512]{2,1,0:T(8,128)(2,1)} %refs_1_.1, bf16[4,512,2048]{2,1,0:T(8,128)(2,1)} %refs_2_.1), custom_call_target="tpu_custom_call" | custom-call | bytes 25165824 | tf_op jit(solution)/shard_map/load_weights/pallas_call | solution.py:150
  15.9 2.8 %collective-permute-done.1.refs_0_ = bf16[64,2176]{1,0:T(8,128)(2,1)S(1)} collective-permute-done((bf16[64,2176]{1,0:T(8,128)(2,1)S(1)}, bf16[64,2176]{1,0:T(8,128)(2,1)S(1)}, u32[]{:S(2)}, u32[]{:S(2)}) %collective-permute-start.1) | collective-permute-done | bytes 278560 | tf_op jit(solution)/shard_map/ppermute | solution.py:276
  18.7 0.2 collective-permute-done.refs_2_
  18.9 0.0 collective-permute-start.7
  18.9 0.5 collective-permute-start.6
  19.4 1.5 %collective-permute-start.2 = (bf16[64,2176]{1,0:T(8,128)(2,1)S(1)}, bf16[64,2176]{1,0:T(8,128)(2,1)S(1)}, u32[]{:S(2)}, u32[]{:S(2)}) collective-permute-start(bf16[64,2176]{1,0:T(8,128)(2,1)S(1)} %collective-permute-done.1.refs_0_), channel_id=1, source_target_pairs={{0,2},{1,3},{2,0},{3,1},{4,6},{5,7},{6,4},{7,5},{8,10},{9,11},{10,... | collective-permute-start | bytes 835592 | tf_op jit(solution)/shard_map/ppermute | solution.py:276
  20.9 0.0 collective-permute-done.7.refs_3_
  20.9 0.0 collective-permute-done.6.refs_1_
  20.9 4.9 %experts_far_near.1 = (bf16[64,2048]{1,0:T(8,128)(2,1)S(1)}, bf16[64,2048]{1,0:T(8,128)(2,1)S(1)}, bf16[64,2048]{1,0:T(8,128)(2,1)S(1)}, bf16[64,2048]{1,0:T(8,128)(2,1)S(1)}) custom-call(bf16[64,2176]{1,0:T(8,128)(2,1)S(1)} %collective-permute-done.1.refs_0_, bf16[64,2176]{1,0:T(8,128)(2,1)S(1)} %collective-permute-done.6.refs_1_, ...), custom_call_target="tpu_custom_call" | custom-call | flops 3221225472 | bytes 25165824 | tf_op jit(solution)/shard_map/experts_far_near/pallas_call | solution.py:186
  25.8 0.2 collective-permute-start.8
  26.0 0.4 collective-permute-start.4
  26.4 0.1 collective-permute-start.10
  26.5 1.5 %collective-permute-done.2.refs_0_ = bf16[64,2176]{1,0:T(8,128)(2,1)S(1)} collective-permute-done((bf16[64,2176]{1,0:T(8,128)(2,1)S(1)}, bf16[64,2176]{1,0:T(8,128)(2,1)S(1)}, u32[]{:S(2)}, u32[]{:S(2)}) %collective-permute-start.2) | collective-permute-done | bytes 278560 | tf_op jit(solution)/shard_map/ppermute | solution.py:276
  28.0 0.0 collective-permute-start.3
  28.0 0.0 collective-permute-done.8
  28.0 0.1 add_convert_fusion.1
  28.1 0.0 copy-start
  28.1 1.5 %collective-permute-start.9 = (bf16[64,2048]{1,0:T(8,128)(2,1)S(1)}, bf16[64,2048]{1,0:T(8,128)(2,1)S(1)}, u32[]{:S(2)}, u32[]{:S(2)}) collective-permute-start(bf16[64,2048]{1,0:T(8,128)(2,1)S(1)} %add_convert_fusion.1), channel_id=1, source_target_pairs={{2,6},{3,7},{4,0},{5,1},{0,2},{1,3},{6,4},{7,5},{10,14},{11,15},{1... | collective-permute-start | bytes 786440 | tf_op jit(solution)/shard_map/ppermute | solution.py:276
  29.6 0.0 collective-permute-done.4.refs_3_
  29.6 0.0 collective-permute-done.3.refs_1_
  29.6 4.9 %experts_third_own.1 = (bf16[64,2048]{1,0:T(8,128)(2,1)S(1)}, bf16[64,2048]{1,0:T(8,128)(2,1)S(1)}, bf16[64,2048]{1,0:T(8,128)(2,1)S(1)}, bf16[64,2048]{1,0:T(8,128)(2,1)S(1)}) custom-call(bf16[64,2176]{1,0:T(8,128)(2,1)S(1)} %collective-permute-done.2.refs_0_, bf16[64,2176]{1,0:T(8,128)(2,1)S(1)} %collective-permute-done.3.refs_1_, ...), custom_call_target="tpu_custom_call" | custom-call | flops 3221225472 | bytes 25165824 | tf_op jit(solution)/shard_map/experts_third_own/pallas_call | solution.py:186
  34.5 0.3 collective-permute-start.11
  34.8 0.0 collective-permute-done.10
  34.8 0.1 add_convert_fusion.near_ref
  34.9 2.4 %collective-permute-start.12 = (bf16[64,2048]{1,0:T(8,128)(2,1)S(1)}, bf16[64,2048]{1,0:T(8,128)(2,1)S(1)}, u32[]{:S(2)}, u32[]{:S(2)}) collective-permute-start(bf16[64,2048]{1,0:T(8,128)(2,1)S(1)} %add_convert_fusion.near_ref), channel_id=1, source_target_pairs={{0,2},{1,3},{2,0},{3,1},{4,6},{5,7},{6,4},{7,5},{8,10},{9,11},{10,... | collective-permute-start | bytes 786440 | tf_op jit(solution)/shard_map/ppermute | solution.py:276
  37.3 0.0 collective-permute-start.5
  37.3 0.0 collective-permute-done.11
  37.3 0.1 convert_add_fusion.sum_ref
  37.3 0.4 collective-permute-done.9.relayed_ref
  37.8 0.1 third_back.1.third_ref
  37.8 3.3 %collective-permute-start.13 = (bf16[64,2048]{1,0:T(8,128)(2,1)S(1)}, bf16[64,2048]{1,0:T(8,128)(2,1)S(1)}, u32[]{:S(2)}, u32[]{:S(2)}) collective-permute-start(bf16[64,2048]{1,0:T(8,128)(2,1)S(1)} %third_back.1.third_ref), channel_id=1, source_target_pairs={{0,6},{1,7},{2,4},{3,5},{4,2},{5,3},{6,0},{7,1},{8,14},{9,15},{10,... | collective-permute-start | bytes 786440 | tf_op jit(solution)/shard_map/ppermute | solution.py:276
  41.2 0.0 collective-permute-done.5.swapped_ref
  41.2 0.0 copy-done
  41.2 0.4 own_sum.1
  41.6 1.6 %collective-permute-start.14 = (f32[8,128]{1,0:T(8,128)S(1)}, f32[8,128]{1,0:T(8,128)S(1)}, u32[]{:S(2)}, u32[]{:S(2)}) collective-permute-start(f32[8,128]{1,0:T(8,128)S(1)} %get-tuple-element.43.score_ref), channel_id=1, source_target_pairs={{0,16},{8,24},{16,0},{24,8},{1,17},{9,25},{17,1},{25,9},{2,18},{10... | collective-permute-start | bytes 12296 | tf_op jit(solution)/shard_map/ppermute | solution.py:304
  43.2 2.1 %collective-permute-done.14.partner_ref = f32[8,128]{1,0:T(8,128)S(1)} collective-permute-done((f32[8,128]{1,0:T(8,128)S(1)}, f32[8,128]{1,0:T(8,128)S(1)}, u32[]{:S(2)}, u32[]{:S(2)}) %collective-permute-start.14) | collective-permute-done | bytes 4128 | tf_op jit(solution)/shard_map/ppermute | solution.py:304
  45.3 0.6 %collective-permute-start.16 = (f32[2,8,128]{2,1,0:T(8,128)S(1)}, f32[2,8,128]{2,1,0:T(8,128)S(1)}, u32[]{:S(2)}, u32[]{:S(2)}) collective-permute-start(f32[2,8,128]{2,1,0:T(8,128)S(1)} %both_scores.1.both_ref), channel_id=1, source_target_pairs={{0,6},{1,7},{2,4},{3,5},{4,2},{5,3},{6,0},{7,1},{8,14},{9,15},{10,... | collective-permute-start | bytes 24584 | tf_op jit(solution)/shard_map/ppermute | solution.py:276
  45.8 0.0 collective-permute-start.15
  45.8 0.0 collective-permute-done.12.near_ref
  45.8 5.1 %collective-permute-done.16.from_third_ref = f32[2,8,128]{2,1,0:T(8,128)S(1)} collective-permute-done((f32[2,8,128]{2,1,0:T(8,128)S(1)}, f32[2,8,128]{2,1,0:T(8,128)S(1)}, u32[]{:S(2)}, u32[]{:S(2)}) %collective-permute-start.16) | collective-permute-done | bytes 8224 | tf_op jit(solution)/shard_map/ppermute | solution.py:276
  50.9 0.0 collective-permute-done.15.from_near_ref
  51.0 0.0 collective-permute-done.13.third_ref
  51.0 0.9 %mixed.1 = (bf16[64,2048]{1,0:T(8,128)(2,1)}, f32[4]{0:T(128)}) custom-call(f32[64,2048]{1,0:T(8,128)S(1)} %get-tuple-element.42.sum_ref, bf16[64,2048]{1,0:T(8,128)(2,1)S(1)} %collective-permute-done.12.near_ref, bf16[64,2048]{1,0:T(8,128)(2,1)S(1)} %collective-permute-done.13.third_ref, f32[2,8,128]{2,1,0:T(8,128)S(1)} %both_scores.1.both_ref, ...), custom_call_target="tpu_custom_call" | custom-call | tf_op jit(solution)/shard_map/mixed/pallas_call | solution.py:265
  (1 shorter events, 0.0 us)
Async XLA Ops:
  1.9 16.8 %collective-permute-start.1 = (bf16[64,2176]{1,0:T(8,128)(2,1)S(1)}, bf16[64,2176]{1,0:T(8,128)(2,1)S(1)}, u32[]{:S(2)}, u32[]{:S(2)}) collective-permute-start(bf16[64,2176]{1,0:T(8,128)(2,1)S(1)} %prep.1.x_ref.refs_2_), channel_id=1, source_target_pairs={{0,4},{1,5},{2,6},{3,7},{4,0},{5,1},{6,2},{7,3},{8,12},{9,13},{10,... | collective-permute-start | bytes 835592 | tf_op jit(solution)/shard_map/ppermute | solution.py:276
  6.0 12.9 %collective-permute-start = (bf16[64,2176]{1,0:T(8,128)(2,1)S(1)}, bf16[64,2176]{1,0:T(8,128)(2,1)S(1)}, u32[]{:S(2)}, u32[]{:S(2)}) collective-permute-start(bf16[64,2176]{1,0:T(8,128)(2,1)S(1)} %prep.1.x_ref.refs_2_), channel_id=1, source_target_pairs={{0,2},{1,3},{2,0},{3,1},{4,6},{5,7},{6,4},{7,5},{8,10},{9,11},{10,... | collective-permute-start | bytes 835592 | tf_op jit(solution)/shard_map/ppermute | solution.py:276
  18.9 2.0 %collective-permute-start.7 = (bf16[64,2176]{1,0:T(8,128)(2,1)S(1)}, bf16[64,2176]{1,0:T(8,128)(2,1)S(1)}, u32[]{:S(2)}, u32[]{:S(2)}) collective-permute-start(bf16[64,2176]{1,0:T(8,128)(2,1)S(1)} %collective-permute-done.refs_2_), channel_id=1, source_target_pairs={{0,1},{1,0},{2,3},{3,2},{4,5},{5,4},{6,7},{7,6},{8,9},{9,8},{10,11... | collective-permute-start | bytes 835592 | tf_op jit(solution)/shard_map/ppermute | solution.py:276
  18.9 2.0 %collective-permute-start.6 = (bf16[64,2176]{1,0:T(8,128)(2,1)S(1)}, bf16[64,2176]{1,0:T(8,128)(2,1)S(1)}, u32[]{:S(2)}, u32[]{:S(2)}) collective-permute-start(bf16[64,2176]{1,0:T(8,128)(2,1)S(1)} %collective-permute-done.1.refs_0_), channel_id=1, source_target_pairs={{0,1},{1,0},{2,3},{3,2},{4,5},{5,4},{6,7},{7,6},{8,9},{9,8},{10,11... | collective-permute-start | bytes 835592 | tf_op jit(solution)/shard_map/ppermute | solution.py:276
  19.4 8.6 %collective-permute-start.2 = (bf16[64,2176]{1,0:T(8,128)(2,1)S(1)}, bf16[64,2176]{1,0:T(8,128)(2,1)S(1)}, u32[]{:S(2)}, u32[]{:S(2)}) collective-permute-start(bf16[64,2176]{1,0:T(8,128)(2,1)S(1)} %collective-permute-done.1.refs_0_), channel_id=1, source_target_pairs={{0,2},{1,3},{2,0},{3,1},{4,6},{5,7},{6,4},{7,5},{8,10},{9,11},{10,... | collective-permute-start | bytes 835592 | tf_op jit(solution)/shard_map/ppermute | solution.py:276
  25.8 2.2 %collective-permute-start.8 = (bf16[64,2048]{1,0:T(8,128)(2,1)S(1)}, bf16[64,2048]{1,0:T(8,128)(2,1)S(1)}, u32[]{:S(2)}, u32[]{:S(2)}) collective-permute-start(bf16[64,2048]{1,0:T(8,128)(2,1)S(1)} %get-tuple-element.35), channel_id=1, source_target_pairs={{0,1},{1,0},{2,3},{3,2},{4,5},{5,4},{6,7},{7,6},{8,9},{9,8},{10,11... | collective-permute-start | bytes 786440 | tf_op jit(solution)/shard_map/ppermute | solution.py:276
  26.0 3.7 %collective-permute-start.4 = (bf16[64,2176]{1,0:T(8,128)(2,1)S(1)}, bf16[64,2176]{1,0:T(8,128)(2,1)S(1)}, u32[]{:S(2)}, u32[]{:S(2)}) collective-permute-start(bf16[64,2176]{1,0:T(8,128)(2,1)S(1)} %prep.1.x_ref.refs_2_), channel_id=1, source_target_pairs={{0,1},{1,0},{2,3},{3,2},{4,5},{5,4},{6,7},{7,6},{8,9},{9,8},{10,11... | collective-permute-start | bytes 835592 | tf_op jit(solution)/shard_map/ppermute | solution.py:276
  26.4 8.4 %collective-permute-start.10 = (bf16[64,2048]{1,0:T(8,128)(2,1)S(1)}, bf16[64,2048]{1,0:T(8,128)(2,1)S(1)}, u32[]{:S(2)}, u32[]{:S(2)}) collective-permute-start(bf16[64,2048]{1,0:T(8,128)(2,1)S(1)} %get-tuple-element.38), channel_id=1, source_target_pairs={{0,1},{1,0},{2,3},{3,2},{4,5},{5,4},{6,7},{7,6},{8,9},{9,8},{10,11... | collective-permute-start | bytes 786440 | tf_op jit(solution)/shard_map/ppermute | solution.py:276
  28.0 1.6 %collective-permute-start.3 = (bf16[64,2176]{1,0:T(8,128)(2,1)S(1)}, bf16[64,2176]{1,0:T(8,128)(2,1)S(1)}, u32[]{:S(2)}, u32[]{:S(2)}) collective-permute-start(bf16[64,2176]{1,0:T(8,128)(2,1)S(1)} %collective-permute-done.2.refs_0_), channel_id=1, source_target_pairs={{0,1},{1,0},{2,3},{3,2},{4,5},{5,4},{6,7},{7,6},{8,9},{9,8},{10,11... | collective-permute-start | bytes 835592 | tf_op jit(solution)/shard_map/ppermute | solution.py:276
  28.1 13.1 %copy-start = (f32[2048]{0:T(1024)S(1)}, f32[2048]{0:T(1024)}, u32[]{:S(2)}) copy-start(f32[2048]{0:T(1024)} %param.17) | copy-start | bytes 24580
  28.1 9.7 %collective-permute-start.9 = (bf16[64,2048]{1,0:T(8,128)(2,1)S(1)}, bf16[64,2048]{1,0:T(8,128)(2,1)S(1)}, u32[]{:S(2)}, u32[]{:S(2)}) collective-permute-start(bf16[64,2048]{1,0:T(8,128)(2,1)S(1)} %add_convert_fusion.1), channel_id=1, source_target_pairs={{2,6},{3,7},{4,0},{5,1},{0,2},{1,3},{6,4},{7,5},{10,14},{11,15},{1... | collective-permute-start | bytes 786440 | tf_op jit(solution)/shard_map/ppermute | solution.py:276
  34.5 2.8 %collective-permute-start.11 = (bf16[64,2048]{1,0:T(8,128)(2,1)S(1)}, bf16[64,2048]{1,0:T(8,128)(2,1)S(1)}, u32[]{:S(2)}, u32[]{:S(2)}) collective-permute-start(bf16[64,2048]{1,0:T(8,128)(2,1)S(1)} %get-tuple-element.41), channel_id=1, source_target_pairs={{0,1},{1,0},{2,3},{3,2},{4,5},{5,4},{6,7},{7,6},{8,9},{9,8},{10,11... | collective-permute-start | bytes 786440 | tf_op jit(solution)/shard_map/ppermute | solution.py:276
  34.9 11.0 %collective-permute-start.12 = (bf16[64,2048]{1,0:T(8,128)(2,1)S(1)}, bf16[64,2048]{1,0:T(8,128)(2,1)S(1)}, u32[]{:S(2)}, u32[]{:S(2)}) collective-permute-start(bf16[64,2048]{1,0:T(8,128)(2,1)S(1)} %add_convert_fusion.near_ref), channel_id=1, source_target_pairs={{0,2},{1,3},{2,0},{3,1},{4,6},{5,7},{6,4},{7,5},{8,10},{9,11},{10,... | collective-permute-start | bytes 786440 | tf_op jit(solution)/shard_map/ppermute | solution.py:276
  37.3 3.9 %collective-permute-start.5 = (bf16[64,2048]{1,0:T(8,128)(2,1)S(1)}, bf16[64,2048]{1,0:T(8,128)(2,1)S(1)}, u32[]{:S(2)}, u32[]{:S(2)}) collective-permute-start(bf16[64,2048]{1,0:T(8,128)(2,1)S(1)} %get-tuple-element.32), channel_id=1, source_target_pairs={{0,1},{1,0},{2,3},{3,2},{4,5},{5,4},{6,7},{7,6},{8,9},{9,8},{10,11... | collective-permute-start | bytes 786440 | tf_op jit(solution)/shard_map/ppermute | solution.py:276
  37.8 13.1 %collective-permute-start.13 = (bf16[64,2048]{1,0:T(8,128)(2,1)S(1)}, bf16[64,2048]{1,0:T(8,128)(2,1)S(1)}, u32[]{:S(2)}, u32[]{:S(2)}) collective-permute-start(bf16[64,2048]{1,0:T(8,128)(2,1)S(1)} %third_back.1.third_ref), channel_id=1, source_target_pairs={{0,6},{1,7},{2,4},{3,5},{4,2},{5,3},{6,0},{7,1},{8,14},{9,15},{10,... | collective-permute-start | bytes 786440 | tf_op jit(solution)/shard_map/ppermute | solution.py:276
  41.6 3.7 %collective-permute-start.14 = (f32[8,128]{1,0:T(8,128)S(1)}, f32[8,128]{1,0:T(8,128)S(1)}, u32[]{:S(2)}, u32[]{:S(2)}) collective-permute-start(f32[8,128]{1,0:T(8,128)S(1)} %get-tuple-element.43.score_ref), channel_id=1, source_target_pairs={{0,16},{8,24},{16,0},{24,8},{1,17},{9,25},{17,1},{25,9},{2,18},{10... | collective-permute-start | bytes 12296 | tf_op jit(solution)/shard_map/ppermute | solution.py:304
  45.3 5.7 %collective-permute-start.16 = (f32[2,8,128]{2,1,0:T(8,128)S(1)}, f32[2,8,128]{2,1,0:T(8,128)S(1)}, u32[]{:S(2)}, u32[]{:S(2)}) collective-permute-start(f32[2,8,128]{2,1,0:T(8,128)S(1)} %both_scores.1.both_ref), channel_id=1, source_target_pairs={{0,6},{1,7},{2,4},{3,5},{4,2},{5,3},{6,0},{7,1},{8,14},{9,15},{10,... | collective-permute-start | bytes 24584 | tf_op jit(solution)/shard_map/ppermute | solution.py:276
  45.8 5.1 %collective-permute-start.15 = (f32[2,8,128]{2,1,0:T(8,128)S(1)}, f32[2,8,128]{2,1,0:T(8,128)S(1)}, u32[]{:S(2)}, u32[]{:S(2)}) collective-permute-start(f32[2,8,128]{2,1,0:T(8,128)S(1)} %both_scores.1.both_ref), channel_id=1, source_target_pairs={{0,2},{1,3},{2,0},{3,1},{4,6},{5,7},{6,4},{7,5},{8,10},{9,11},{10,... | collective-permute-start | bytes 24584 | tf_op jit(solution)/shard_map/ppermute | solution.py:276

commit v6 on v5

--- a/solution.py
+++ b/solution.py
@@ -217,11 +217,6 @@
     return [jnp.sum(scored[at : at + SEQ_LEN, :]) for at in range(0, rows.shape[0], SEQ_LEN)]
 
 
-def on_inner_chip():
-    chip = lax.axis_index("expert") // 2
-    return (chip == 1) | (chip == 2)
-
-
 def score_tile(tile, row, rows, head):
     at = lax.broadcasted_iota(jnp.int32, tile.shape, 0)
     lane = lax.broadcasted_iota(jnp.int32, tile.shape, 1)
@@ -231,13 +226,11 @@
 
 
 def third_kernel(sum_ref, relayed_ref, back_ref):
-    joins = relayed_ref[...].astype(jnp.float32) * jnp.where(on_inner_chip(), 1.0, 0.0)
-    back_ref[...] = (sum_ref[...] + joins).astype(jnp.bfloat16)
-
-
-def own_kernel(own_ref, swapped_ref, relayed_ref, near_ref, third_ref, head_ref, sum_ref, score_ref):
-    stays = relayed_ref[...].astype(jnp.float32) * jnp.where(on_inner_chip(), 0.0, 1.0)
-    own = own_ref[...].astype(jnp.float32) + swapped_ref[...].astype(jnp.float32) + stays
+    back_ref[...] = (sum_ref[...] + relayed_ref[...].astype(jnp.float32)).astype(jnp.bfloat16)
+
+
+def own_kernel(own_ref, swapped_ref, near_ref, third_ref, head_ref, sum_ref, score_ref):
+    own = own_ref[...].astype(jnp.float32) + swapped_ref[...].astype(jnp.float32)
     sum_ref[...] = own
     head = head_ref[...]
     tile = jnp.zeros(score_ref.shape, jnp.float32)
@@ -307,18 +300,16 @@
         same, other = sums
         return (same.astype(jnp.float32) + core_swap(other).astype(jnp.float32)).astype(dtype)
 
-    def chip_route(*pairs):
-        return [(2 * a + c, 2 * b + c) for a, b in pairs for c in (0, 1)]
-
     if chips == 4:
         far = exchange(x, 2)
         near = exchange(x, 1)
-        near, far, x, *weights = lax.optimization_barrier((near, far, x, *weights))
+        (own_sums,) = ffn("experts_own", [pair(x)], experts, weights)
+        near, far, own_sums, *weights = lax.optimization_barrier((near, far, own_sums, *weights))
         third = exchange(far, 1)
         far_sums, near_sums = ffn("experts_far_near", [pair(far), pair(near)], experts, weights)
         far_back = chip_sum(far_sums)
-        relayed = send(far_back, chip_route((1, 3), (2, 0), (0, 1), (3, 2)))
-        third_sums, own_sums = ffn("experts_third_own", [pair(third), pair(x)], experts, weights)
+        relayed = exchange(far_back, 1)
+        (third_sums,) = ffn("experts_third", [pair(third)], experts, weights)
         near_back = chip_sum(near_sums)
         third_same, near_back = lax.optimization_barrier((third_sums[0], near_back))
         near = exchange(near_back, 1)
@@ -331,7 +322,7 @@
             own_kernel,
             "own_sum",
             [pltpu.VMEM((rows, width), jnp.float32), pltpu.VMEM(scores, jnp.float32)],
-            *(own_sums[0], core_swap(own_sums[1]), relayed, near_back, third_back, score_head.reshape(1, width)),
+            *(own_sums[0], core_swap(own_sums[1]), near_back, third_back, score_head.reshape(1, width)),
         )
         (both,) = local_call(
             both_kernel, "both_scores", [pltpu.VMEM((2, *scores), jnp.float32)], score, partner_of(score)

time: 52 us -> 52 us (level)
  Pallas kernels: 20.8 us -> 22.7 us
  waiting for transfers between devices: 12.1 us -> 11 us
  starting transfers between devices: 18.1 us -> 17.1 us
    pallas_call x2 -> x3, Pallas kernels: 9.75 us -> 11.8 us  [ffn(): pl.pallas_call(kernel, out_shape=[pltpu.VMEM((rows, width), jnp.bfloat16)...]
    ppermute x16, waiting for transfers between devices: 10.1 us -> 8.95 us  [send(): return lax.ppermute(x, 'expert', route)]
    ppermute x16, starting transfers between devices: 16.5 us -> 15.5 us  [send(): return lax.ppermute(x, 'expert', route)]
  transfers between devices with their start and end apart: 17 -> 17, of which waited for: 6 -> 5; matrix products, arithmetic and copies ran while one was open for 0% -> 0% of each run, Pallas kernels for 36% -> 40%
where the time goes in v6:
time: 52 us; the launch traced here: 51.8 us
  Pallas kernels  22.7 us (44%)
  starting transfers between devices  17.1 us (33%)
  waiting for transfers between devices  11 us (21%)
  between operations  0.73 us (1%)
    ppermute x16, starting transfers between devices, send(): return lax.ppermute(x, 'expert', route)  15.5 us
    pallas_call x3, Pallas kernels, ffn(): pl.pallas_call(kernel, out_shape=[pltpu.VMEM((rows, width), jnp.bfloat16)...  11.8 us
    ppermute x16, waiting for transfers between devices, send(): return lax.ppermute(x, 'expert', route)  8.95 us
    pallas_call x1, Pallas kernels, load(): pl.pallas_call(load_kernel, out_shape=[pltpu.VMEM(a.shape, a.dtype) for a...  8.34 us
    ppermute x1, waiting for transfers between devices, partner_of(): lax.ppermute(block, 'dp', [(d, d ^ count // 2) for d in range(count)])  2.09 us
    ppermute x1, starting transfers between devices, partner_of(): lax.ppermute(block, 'dp', [(d, d ^ count // 2) for d in range(count)])  1.58 us
    pallas_call x4, Pallas kernels, local_call(): pl.pallas_call(kernel, out_shape=out_shape, in_specs=[VMEM] * len(xs), ou...  1.34 us
    pallas_call x1, Pallas kernels, body(): pl.pallas_call(functools.partial(prep_kernel, experts), out_shape=pltpu.V...  1.26 us
  transfers between devices with their start and end apart: 17, of which 5 were waited for; matrix products, arithmetic and copies ran while one was open for 0% of the time, Pallas kernels for 40%

profile of v6, /device:TPU:0, one launch (start us, length us, event | category | flops | bytes accessed | tf_op | source)
XLA Modules:
  0.0 51.8 jit_solution(10862258981196021156)
XLA Ops:
  0.6 1.3 %prep.1.x_ref.refs_0_ = bf16[64,2176]{1,0:T(8,128)(2,1)S(1)} custom-call(bf16[64,2048]{1,0:T(8,128)(2,1)} %tok_ref.1, s32[8,64]{1,0:T(8,128)} %bitcast.4, s32[8,64]{1,0:T(8,128)} %bitcast.5, s32[4]{0:T(128)} %scorer_ref.1, bf16[2,2048]{1,0:T(2,128)(2,1)} %tags_ref.1), custom_call_target="tpu_custom_call" | custom-call | tf_op jit(solution)/shard_map/prep/pallas_call | solution.py:277
  1.9 0.5 collective-permute-start.2
  2.4 3.7 %collective-permute-start.1 = (bf16[64,2176]{1,0:T(8,128)(2,1)S(1)}, bf16[64,2176]{1,0:T(8,128)(2,1)S(1)}, u32[]{:S(2)}, u32[]{:S(2)}) collective-permute-start(bf16[64,2176]{1,0:T(8,128)(2,1)S(1)} %prep.1.x_ref.refs_0_), channel_id=1, source_target_pairs={{0,4},{1,5},{2,6},{3,7},{4,0},{5,1},{6,2},{7,3},{8,12},{9,13},{10,... | collective-permute-start | bytes 835592 | tf_op jit(solution)/shard_map/ppermute | solution.py:269
  6.1 1.6 %collective-permute-start = (bf16[64,2176]{1,0:T(8,128)(2,1)S(1)}, bf16[64,2176]{1,0:T(8,128)(2,1)S(1)}, u32[]{:S(2)}, u32[]{:S(2)}) collective-permute-start(bf16[64,2176]{1,0:T(8,128)(2,1)S(1)} %prep.1.x_ref.refs_0_), channel_id=1, source_target_pairs={{0,2},{1,3},{2,0},{3,1},{4,6},{5,7},{6,4},{7,5},{8,10},{9,11},{10,... | collective-permute-start | bytes 835592 | tf_op jit(solution)/shard_map/ppermute | solution.py:269
  7.7 8.3 %load_weights.1 = (bf16[4,2048,512]{2,1,0:T(8,128)(2,1)S(1)}, bf16[4,2048,512]{2,1,0:T(8,128)(2,1)S(1)}, bf16[4,512,2048]{2,1,0:T(8,128)(2,1)S(1)}) custom-call(bf16[64,2176]{1,0:T(8,128)(2,1)S(1)} %prep.1.x_ref.refs_0_, bf16[4,2048,512]{2,1,0:T(8,128)(2,1)} %refs_0_.1, bf16[4,2048,512]{2,1,0:T(8,128)(2,1)} %refs_1_.1, bf16[4,512,2048]{2,1,0:T(8,128)(2,1)} %refs_2_.1), custom_call_target="tpu_custom_call" | custom-call | bytes 25165824 | tf_op jit(solution)/shard_map/load_weights/pallas_call | solution.py:150
  16.0 0.0 collective-permute-done.2.refs_1_
  16.0 3.5 %experts_own.1 = (bf16[64,2048]{1,0:T(8,128)(2,1)S(1)}, bf16[64,2048]{1,0:T(8,128)(2,1)S(1)}) custom-call(bf16[64,2176]{1,0:T(8,128)(2,1)S(1)} %prep.1.x_ref.refs_0_, bf16[64,2176]{1,0:T(8,128)(2,1)S(1)} %collective-permute-done.2.refs_1_, bf16[4,2048,512]{2,1,0:T(8,128)(2,1)S(1)} %get-tuple-element.32.refs_2_.refs_4_, ...), custom_call_target="tpu_custom_call" | custom-call | flops 3221225472 | bytes 25165824 | tf_op jit(solution)/shard_map/experts_own/pallas_call | solution.py:186
  19.5 0.0 collective-permute-done.1.refs_0_
  19.5 0.1 collective-permute-done.refs_2_
  19.6 0.0 collective-permute-start.7
  19.6 0.5 collective-permute-start.6
  20.1 1.5 %collective-permute-start.4 = (bf16[64,2176]{1,0:T(8,128)(2,1)S(1)}, bf16[64,2176]{1,0:T(8,128)(2,1)S(1)}, u32[]{:S(2)}, u32[]{:S(2)}) collective-permute-start(bf16[64,2176]{1,0:T(8,128)(2,1)S(1)} %collective-permute-done.1.refs_0_), channel_id=1, source_target_pairs={{0,2},{1,3},{2,0},{3,1},{4,6},{5,7},{6,4},{7,5},{8,10},{9,11},{10,... | collective-permute-start | bytes 835592 | tf_op jit(solution)/shard_map/ppermute | solution.py:269
  21.6 0.0 collective-permute-done.7.refs_3_
  21.6 0.0 collective-permute-done.6.refs_1_
  21.6 4.9 %experts_far_near.1 = (bf16[64,2048]{1,0:T(8,128)(2,1)S(1)}, bf16[64,2048]{1,0:T(8,128)(2,1)S(1)}, bf16[64,2048]{1,0:T(8,128)(2,1)S(1)}, bf16[64,2048]{1,0:T(8,128)(2,1)S(1)}) custom-call(bf16[64,2176]{1,0:T(8,128)(2,1)S(1)} %collective-permute-done.1.refs_0_, bf16[64,2176]{1,0:T(8,128)(2,1)S(1)} %collective-permute-done.6.refs_1_, ...), custom_call_target="tpu_custom_call" | custom-call | flops 3221225472 | bytes 25165824 | tf_op jit(solution)/shard_map/experts_far_near/pallas_call | solution.py:186
  26.5 0.1 collective-permute-start.10
  26.6 0.4 collective-permute-start.3
  27.1 0.1 collective-permute-start.8
  27.1 1.6 %collective-permute-done.4.refs_0_ = bf16[64,2176]{1,0:T(8,128)(2,1)S(1)} collective-permute-done((bf16[64,2176]{1,0:T(8,128)(2,1)S(1)}, bf16[64,2176]{1,0:T(8,128)(2,1)S(1)}, u32[]{:S(2)}, u32[]{:S(2)}) %collective-permute-start.4) | collective-permute-done | bytes 278560 | tf_op jit(solution)/shard_map/ppermute | solution.py:269
  28.7 0.0 collective-permute-start.5
  28.7 0.0 collective-permute-done.10
  28.7 0.1 add_convert_fusion
  28.8 0.0 copy-start
  28.8 1.5 %collective-permute-start.11 = (bf16[64,2048]{1,0:T(8,128)(2,1)S(1)}, bf16[64,2048]{1,0:T(8,128)(2,1)S(1)}, u32[]{:S(2)}, u32[]{:S(2)}) collective-permute-start(bf16[64,2048]{1,0:T(8,128)(2,1)S(1)} %add_convert_fusion), channel_id=1, source_target_pairs={{0,2},{1,3},{2,0},{3,1},{4,6},{5,7},{6,4},{7,5},{8,10},{9,11},{10,... | collective-permute-start | bytes 786440 | tf_op jit(solution)/shard_map/ppermute | solution.py:269
  30.3 0.0 collective-permute-done.5.refs_1_
  30.3 3.5 %experts_third.1 = (bf16[64,2048]{1,0:T(8,128)(2,1)S(1)}, bf16[64,2048]{1,0:T(8,128)(2,1)S(1)}) custom-call(bf16[64,2176]{1,0:T(8,128)(2,1)S(1)} %collective-permute-done.4.refs_0_, bf16[64,2176]{1,0:T(8,128)(2,1)S(1)} %collective-permute-done.5.refs_1_, bf16[4,2048,512]{2,1,0:T(8,128)(2,1)S(1)} %get-tuple-element.32.refs_2_.refs_4_, ...), custom_call_target="tpu_custom_call" | custom-call | flops 3221225472 | bytes 25165824 | tf_op jit(solution)/shard_map/experts_third/pallas_call | solution.py:186
  33.8 0.3 collective-permute-start.9
  34.1 0.0 collective-permute-done.8
  34.1 0.1 add_convert_fusion.1.near_ref
  34.2 1.4 %collective-permute-start.12 = (bf16[64,2048]{1,0:T(8,128)(2,1)S(1)}, bf16[64,2048]{1,0:T(8,128)(2,1)S(1)}, u32[]{:S(2)}, u32[]{:S(2)}) collective-permute-start(bf16[64,2048]{1,0:T(8,128)(2,1)S(1)} %add_convert_fusion.1.near_ref), channel_id=1, source_target_pairs={{0,2},{1,3},{2,0},{3,1},{4,6},{5,7},{6,4},{7,5},{8,10},{9,11},{10,... | collective-permute-start | bytes 786440 | tf_op jit(solution)/shard_map/ppermute | solution.py:269
  35.6 0.0 collective-permute-done.9
  35.6 0.1 convert_add_fusion.sum_ref
  35.6 2.4 %collective-permute-done.11.relayed_ref = bf16[64,2048]{1,0:T(8,128)(2,1)S(1)} collective-permute-done((bf16[64,2048]{1,0:T(8,128)(2,1)S(1)}, bf16[64,2048]{1,0:T(8,128)(2,1)S(1)}, u32[]{:S(2)}, u32[]{:S(2)}) %collective-permute-start.11) | collective-permute-done | bytes 262176 | tf_op jit(solution)/shard_map/ppermute | solution.py:269
  38.0 3.3 %collective-permute-start.13 = (bf16[64,2048]{1,0:T(8,128)(2,1)S(1)}, bf16[64,2048]{1,0:T(8,128)(2,1)S(1)}, u32[]{:S(2)}, u32[]{:S(2)}) collective-permute-start(bf16[64,2048]{1,0:T(8,128)(2,1)S(1)} %third_back.1.third_ref), channel_id=1, source_target_pairs={{0,6},{1,7},{2,4},{3,5},{4,2},{5,3},{6,0},{7,1},{8,14},{9,15},{10,... | collective-permute-start | bytes 786440 | tf_op jit(solution)/shard_map/ppermute | solution.py:269
  41.4 0.0 collective-permute-done.3.swapped_ref
  41.4 0.0 copy-done
  41.4 0.4 own_sum.1
  41.7 1.6 %collective-permute-start.14 = (f32[8,128]{1,0:T(8,128)S(1)}, f32[8,128]{1,0:T(8,128)S(1)}, u32[]{:S(2)}, u32[]{:S(2)}) collective-permute-start(f32[8,128]{1,0:T(8,128)S(1)} %get-tuple-element.45.score_ref), channel_id=1, source_target_pairs={{0,16},{8,24},{16,0},{24,8},{1,17},{9,25},{17,1},{25,9},{2,18},{10... | collective-permute-start | bytes 12296 | tf_op jit(solution)/shard_map/ppermute | solution.py:297
  43.3 2.1 %collective-permute-done.14.partner_ref = f32[8,128]{1,0:T(8,128)S(1)} collective-permute-done((f32[8,128]{1,0:T(8,128)S(1)}, f32[8,128]{1,0:T(8,128)S(1)}, u32[]{:S(2)}, u32[]{:S(2)}) %collective-permute-start.14) | collective-permute-done | bytes 4128 | tf_op jit(solution)/shard_map/ppermute | solution.py:297
  45.4 0.6 %collective-permute-start.16 = (f32[2,8,128]{2,1,0:T(8,128)S(1)}, f32[2,8,128]{2,1,0:T(8,128)S(1)}, u32[]{:S(2)}, u32[]{:S(2)}) collective-permute-start(f32[2,8,128]{2,1,0:T(8,128)S(1)} %both_scores.1.both_ref), channel_id=1, source_target_pairs={{0,6},{1,7},{2,4},{3,5},{4,2},{5,3},{6,0},{7,1},{8,14},{9,15},{10,... | collective-permute-start | bytes 24584 | tf_op jit(solution)/shard_map/ppermute | solution.py:269
  46.0 0.0 collective-permute-start.15
  46.0 0.0 collective-permute-done.12.near_ref
  46.0 4.9 %collective-permute-done.16.from_third_ref = f32[2,8,128]{2,1,0:T(8,128)S(1)} collective-permute-done((f32[2,8,128]{2,1,0:T(8,128)S(1)}, f32[2,8,128]{2,1,0:T(8,128)S(1)}, u32[]{:S(2)}, u32[]{:S(2)}) %collective-permute-start.16) | collective-permute-done | bytes 8224 | tf_op jit(solution)/shard_map/ppermute | solution.py:269
  50.9 0.0 collective-permute-done.15.from_near_ref
  50.9 0.0 collective-permute-done.13.third_ref
  50.9 0.9 %mixed.1 = (bf16[64,2048]{1,0:T(8,128)(2,1)}, f32[4]{0:T(128)}) custom-call(f32[64,2048]{1,0:T(8,128)S(1)} %get-tuple-element.44.sum_ref, bf16[64,2048]{1,0:T(8,128)(2,1)S(1)} %collective-permute-done.12.near_ref, bf16[64,2048]{1,0:T(8,128)(2,1)S(1)} %collective-permute-done.13.third_ref, f32[2,8,128]{2,1,0:T(8,128)S(1)} %both_scores.1.both_ref, ...), custom_call_target="tpu_custom_call" | custom-call | tf_op jit(solution)/shard_map/mixed/pallas_call | solution.py:258
  (2 shorter events, 0.0 us)
Async XLA Ops:
  1.9 14.1 %collective-permute-start.2 = (bf16[64,2176]{1,0:T(8,128)(2,1)S(1)}, bf16[64,2176]{1,0:T(8,128)(2,1)S(1)}, u32[]{:S(2)}, u32[]{:S(2)}) collective-permute-start(bf16[64,2176]{1,0:T(8,128)(2,1)S(1)} %prep.1.x_ref.refs_0_), channel_id=1, source_target_pairs={{0,1},{1,0},{2,3},{3,2},{4,5},{5,4},{6,7},{7,6},{8,9},{9,8},{10,11... | collective-permute-start | bytes 835592 | tf_op jit(solution)/shard_map/ppermute | solution.py:269
  2.4 17.1 %collective-permute-start.1 = (bf16[64,2176]{1,0:T(8,128)(2,1)S(1)}, bf16[64,2176]{1,0:T(8,128)(2,1)S(1)}, u32[]{:S(2)}, u32[]{:S(2)}) collective-permute-start(bf16[64,2176]{1,0:T(8,128)(2,1)S(1)} %prep.1.x_ref.refs_0_), channel_id=1, source_target_pairs={{0,4},{1,5},{2,6},{3,7},{4,0},{5,1},{6,2},{7,3},{8,12},{9,13},{10,... | collective-permute-start | bytes 835592 | tf_op jit(solution)/shard_map/ppermute | solution.py:269
  6.1 13.5 %collective-permute-start = (bf16[64,2176]{1,0:T(8,128)(2,1)S(1)}, bf16[64,2176]{1,0:T(8,128)(2,1)S(1)}, u32[]{:S(2)}, u32[]{:S(2)}) collective-permute-start(bf16[64,2176]{1,0:T(8,128)(2,1)S(1)} %prep.1.x_ref.refs_0_), channel_id=1, source_target_pairs={{0,2},{1,3},{2,0},{3,1},{4,6},{5,7},{6,4},{7,5},{8,10},{9,11},{10,... | collective-permute-start | bytes 835592 | tf_op jit(solution)/shard_map/ppermute | solution.py:269
  19.6 2.0 %collective-permute-start.7 = (bf16[64,2176]{1,0:T(8,128)(2,1)S(1)}, bf16[64,2176]{1,0:T(8,128)(2,1)S(1)}, u32[]{:S(2)}, u32[]{:S(2)}) collective-permute-start(bf16[64,2176]{1,0:T(8,128)(2,1)S(1)} %collective-permute-done.refs_2_), channel_id=1, source_target_pairs={{0,1},{1,0},{2,3},{3,2},{4,5},{5,4},{6,7},{7,6},{8,9},{9,8},{10,11... | collective-permute-start | bytes 835592 | tf_op jit(solution)/shard_map/ppermute | solution.py:269
  19.6 2.0 %collective-permute-start.6 = (bf16[64,2176]{1,0:T(8,128)(2,1)S(1)}, bf16[64,2176]{1,0:T(8,128)(2,1)S(1)}, u32[]{:S(2)}, u32[]{:S(2)}) collective-permute-start(bf16[64,2176]{1,0:T(8,128)(2,1)S(1)} %collective-permute-done.1.refs_0_), channel_id=1, source_target_pairs={{0,1},{1,0},{2,3},{3,2},{4,5},{5,4},{6,7},{7,6},{8,9},{9,8},{10,11... | collective-permute-start | bytes 835592 | tf_op jit(solution)/shard_map/ppermute | solution.py:269
  20.1 8.6 %collective-permute-start.4 = (bf16[64,2176]{1,0:T(8,128)(2,1)S(1)}, bf16[64,2176]{1,0:T(8,128)(2,1)S(1)}, u32[]{:S(2)}, u32[]{:S(2)}) collective-permute-start(bf16[64,2176]{1,0:T(8,128)(2,1)S(1)} %collective-permute-done.1.refs_0_), channel_id=1, source_target_pairs={{0,2},{1,3},{2,0},{3,1},{4,6},{5,7},{6,4},{7,5},{8,10},{9,11},{10,... | collective-permute-start | bytes 835592 | tf_op jit(solution)/shard_map/ppermute | solution.py:269
  26.5 2.2 %collective-permute-start.10 = (bf16[64,2048]{1,0:T(8,128)(2,1)S(1)}, bf16[64,2048]{1,0:T(8,128)(2,1)S(1)}, u32[]{:S(2)}, u32[]{:S(2)}) collective-permute-start(bf16[64,2048]{1,0:T(8,128)(2,1)S(1)} %get-tuple-element.43), channel_id=1, source_target_pairs={{0,1},{1,0},{2,3},{3,2},{4,5},{5,4},{6,7},{7,6},{8,9},{9,8},{10,11... | collective-permute-start | bytes 786440 | tf_op jit(solution)/shard_map/ppermute | solution.py:269
  26.6 14.7 %collective-permute-start.3 = (bf16[64,2048]{1,0:T(8,128)(2,1)S(1)}, bf16[64,2048]{1,0:T(8,128)(2,1)S(1)}, u32[]{:S(2)}, u32[]{:S(2)}) collective-permute-start(bf16[64,2048]{1,0:T(8,128)(2,1)S(1)} %get-tuple-element.30), channel_id=1, source_target_pairs={{0,1},{1,0},{2,3},{3,2},{4,5},{5,4},{6,7},{7,6},{8,9},{9,8},{10,11... | collective-permute-start | bytes 786440 | tf_op jit(solution)/shard_map/ppermute | solution.py:269
  27.1 7.0 %collective-permute-start.8 = (bf16[64,2048]{1,0:T(8,128)(2,1)S(1)}, bf16[64,2048]{1,0:T(8,128)(2,1)S(1)}, u32[]{:S(2)}, u32[]{:S(2)}) collective-permute-start(bf16[64,2048]{1,0:T(8,128)(2,1)S(1)} %get-tuple-element.38), channel_id=1, source_target_pairs={{0,1},{1,0},{2,3},{3,2},{4,5},{5,4},{6,7},{7,6},{8,9},{9,8},{10,11... | collective-permute-start | bytes 786440 | tf_op jit(solution)/shard_map/ppermute | solution.py:269
  28.7 1.6 %collective-permute-start.5 = (bf16[64,2176]{1,0:T(8,128)(2,1)S(1)}, bf16[64,2176]{1,0:T(8,128)(2,1)S(1)}, u32[]{:S(2)}, u32[]{:S(2)}) collective-permute-start(bf16[64,2176]{1,0:T(8,128)(2,1)S(1)} %collective-permute-done.4.refs_0_), channel_id=1, source_target_pairs={{0,1},{1,0},{2,3},{3,2},{4,5},{5,4},{6,7},{7,6},{8,9},{9,8},{10,11... | collective-permute-start | bytes 835592 | tf_op jit(solution)/shard_map/ppermute | solution.py:269
  28.8 12.6 %copy-start = (f32[2048]{0:T(1024)S(1)}, f32[2048]{0:T(1024)}, u32[]{:S(2)}) copy-start(f32[2048]{0:T(1024)} %param.17) | copy-start | bytes 24580
  28.8 9.2 %collective-permute-start.11 = (bf16[64,2048]{1,0:T(8,128)(2,1)S(1)}, bf16[64,2048]{1,0:T(8,128)(2,1)S(1)}, u32[]{:S(2)}, u32[]{:S(2)}) collective-permute-start(bf16[64,2048]{1,0:T(8,128)(2,1)S(1)} %add_convert_fusion), channel_id=1, source_target_pairs={{0,2},{1,3},{2,0},{3,1},{4,6},{5,7},{6,4},{7,5},{8,10},{9,11},{10,... | collective-permute-start | bytes 786440 | tf_op jit(solution)/shard_map/ppermute | solution.py:269
  33.8 1.8 %collective-permute-start.9 = (bf16[64,2048]{1,0:T(8,128)(2,1)S(1)}, bf16[64,2048]{1,0:T(8,128)(2,1)S(1)}, u32[]{:S(2)}, u32[]{:S(2)}) collective-permute-start(bf16[64,2048]{1,0:T(8,128)(2,1)S(1)} %get-tuple-element.41), channel_id=1, source_target_pairs={{0,1},{1,0},{2,3},{3,2},{4,5},{5,4},{6,7},{7,6},{8,9},{9,8},{10,11... | collective-permute-start | bytes 786440 | tf_op jit(solution)/shard_map/ppermute | solution.py:269
  34.2 11.8 %collective-permute-start.12 = (bf16[64,2048]{1,0:T(8,128)(2,1)S(1)}, bf16[64,2048]{1,0:T(8,128)(2,1)S(1)}, u32[]{:S(2)}, u32[]{:S(2)}) collective-permute-start(bf16[64,2048]{1,0:T(8,128)(2,1)S(1)} %add_convert_fusion.1.near_ref), channel_id=1, source_target_pairs={{0,2},{1,3},{2,0},{3,1},{4,6},{5,7},{6,4},{7,5},{8,10},{9,11},{10,... | collective-permute-start | bytes 786440 | tf_op jit(solution)/shard_map/ppermute | solution.py:269
  38.0 12.8 %collective-permute-start.13 = (bf16[64,2048]{1,0:T(8,128)(2,1)S(1)}, bf16[64,2048]{1,0:T(8,128)(2,1)S(1)}, u32[]{:S(2)}, u32[]{:S(2)}) collective-permute-start(bf16[64,2048]{1,0:T(8,128)(2,1)S(1)} %third_back.1.third_ref), channel_id=1, source_target_pairs={{0,6},{1,7},{2,4},{3,5},{4,2},{5,3},{6,0},{7,1},{8,14},{9,15},{10,... | collective-permute-start | bytes 786440 | tf_op jit(solution)/shard_map/ppermute | solution.py:269
  41.7 3.7 %collective-permute-start.14 = (f32[8,128]{1,0:T(8,128)S(1)}, f32[8,128]{1,0:T(8,128)S(1)}, u32[]{:S(2)}, u32[]{:S(2)}) collective-permute-start(f32[8,128]{1,0:T(8,128)S(1)} %get-tuple-element.45.score_ref), channel_id=1, source_target_pairs={{0,16},{8,24},{16,0},{24,8},{1,17},{9,25},{17,1},{25,9},{2,18},{10... | collective-permute-start | bytes 12296 | tf_op jit(solution)/shard_map/ppermute | solution.py:297
  45.4 5.5 %collective-permute-start.16 = (f32[2,8,128]{2,1,0:T(8,128)S(1)}, f32[2,8,128]{2,1,0:T(8,128)S(1)}, u32[]{:S(2)}, u32[]{:S(2)}) collective-permute-start(f32[2,8,128]{2,1,0:T(8,128)S(1)} %both_scores.1.both_ref), channel_id=1, source_target_pairs={{0,6},{1,7},{2,4},{3,5},{4,2},{5,3},{6,0},{7,1},{8,14},{9,15},{10,... | collective-permute-start | bytes 24584 | tf_op jit(solution)/shard_map/ppermute | solution.py:269
  46.0 4.9 %collective-permute-start.15 = (f32[2,8,128]{2,1,0:T(8,128)S(1)}, f32[2,8,128]{2,1,0:T(8,128)S(1)}, u32[]{:S(2)}, u32[]{:S(2)}) collective-permute-start(f32[2,8,128]{2,1,0:T(8,128)S(1)} %both_scores.1.both_ref), channel_id=1, source_target_pairs={{0,2},{1,3},{2,0},{3,1},{4,6},{5,7},{6,4},{7,5},{8,10},{9,11},{10,... | collective-permute-start | bytes 24584 | tf_op jit(solution)/shard_map/ppermute | solution.py:269

commit v7 on v6

--- a/solution.py
+++ b/solution.py
@@ -176,7 +176,7 @@
         kernel = functools.partial(all_rows_kernel, experts)
         scratch = [pltpu.VMEM((met, width + META), jnp.bfloat16)]
     else:
-        met = -(-chips * room // META) * META
+        met = max(META, -(-chips * room // 32) * 32)
         kernel = functools.partial(picked_rows_kernel, chips, experts)
         scratch = [
             pltpu.VMEM((per_device, met, width + META), jnp.bfloat16),
@@ -303,10 +303,10 @@
     if chips == 4:
         far = exchange(x, 2)
         near = exchange(x, 1)
-        (own_sums,) = ffn("experts_own", [pair(x)], experts, weights)
-        near, far, own_sums, *weights = lax.optimization_barrier((near, far, own_sums, *weights))
+        x_pair = pair(x)
+        far, near, x_pair, *weights = lax.optimization_barrier((far, near, x_pair, *weights))
         third = exchange(far, 1)
-        far_sums, near_sums = ffn("experts_far_near", [pair(far), pair(near)], experts, weights)
+        far_sums, near_sums, own_sums = ffn("experts_first", [pair(far), pair(near), x_pair], experts, weights)
         far_back = chip_sum(far_sums)
         relayed = exchange(far_back, 1)
         (third_sums,) = ffn("experts_third", [pair(third)], experts, weights)

time: 52 us -> 52 us (level)
  Pallas kernels: 22.7 us -> 20.8 us
  waiting for transfers between devices: 11 us -> 12.2 us
  starting transfers between devices: 17.1 us -> 17.9 us
    pallas_call x3 -> x2, Pallas kernels: 11.8 us -> 9.88 us  [ffn(): pl.pallas_call(kernel, out_shape=[pltpu.VMEM((rows, width), jnp.bfloat16)...]
    ppermute x16, waiting for transfers between devices: 8.95 us -> 10 us  [send(): return lax.ppermute(x, 'expert', route)]
    ppermute x16, starting transfers between devices: 15.5 us -> 16.4 us  [send(): return lax.ppermute(x, 'expert', route)]
  transfers between devices with their start and end apart: 17 -> 17, of which waited for: 5 -> 7; matrix products, arithmetic and copies ran while one was open for 0% -> 0% of each run, Pallas kernels for 40% -> 36%
where the time goes in v7:
time: 52 us; the launch traced here: 51.8 us
  Pallas kernels  20.8 us (40%)
  starting transfers between devices  17.9 us (34%)
  waiting for transfers between devices  12.2 us (23%)
  between operations  0.73 us (1%)
    ppermute x16, starting transfers between devices, send(): return lax.ppermute(x, 'expert', route)  16.4 us
    ppermute x16, waiting for transfers between devices, send(): return lax.ppermute(x, 'expert', route)  10 us
    pallas_call x2, Pallas kernels, ffn(): pl.pallas_call(kernel, out_shape=[pltpu.VMEM((rows, width), jnp.bfloat16)...  9.88 us
    pallas_call x1, Pallas kernels, load(): pl.pallas_call(load_kernel, out_shape=[pltpu.VMEM(a.shape, a.dtype) for a...  8.34 us
    ppermute x1, waiting for transfers between devices, partner_of(): lax.ppermute(block, 'dp', [(d, d ^ count // 2) for d in range(count)])  2.12 us
    ppermute x1, starting transfers between devices, partner_of(): lax.ppermute(block, 'dp', [(d, d ^ count // 2) for d in range(count)])  1.55 us
    pallas_call x4, Pallas kernels, local_call(): pl.pallas_call(kernel, out_shape=out_shape, in_specs=[VMEM] * len(xs), ou...  1.34 us
    pallas_call x1, Pallas kernels, body(): pl.pallas_call(functools.partial(prep_kernel, experts), out_shape=pltpu.V...  1.26 us
  transfers between devices with their start and end apart: 17, of which 7 were waited for; matrix products, arithmetic and copies ran while one was open for 0% of the time, Pallas kernels for 36%

profile of v7, /device:TPU:0, one launch (start us, length us, event | category | flops | bytes accessed | tf_op | source)
XLA Modules:
  0.0 51.8 jit_solution(16025607471722956606)
XLA Ops:
  0.6 1.3 %prep.1.x_ref.refs_4_ = bf16[64,2176]{1,0:T(8,128)(2,1)S(1)} custom-call(bf16[64,2048]{1,0:T(8,128)(2,1)} %tok_ref.1, s32[8,64]{1,0:T(8,128)} %bitcast.4, s32[8,64]{1,0:T(8,128)} %bitcast.5, s32[4]{0:T(128)} %scorer_ref.1, bf16[2,2048]{1,0:T(2,128)(2,1)} %tags_ref.1), custom_call_target="tpu_custom_call" | custom-call | tf_op jit(solution)/shard_map/prep/pallas_call | solution.py:277
  1.9 4.1 %collective-permute-start = (bf16[64,2176]{1,0:T(8,128)(2,1)S(1)}, bf16[64,2176]{1,0:T(8,128)(2,1)S(1)}, u32[]{:S(2)}, u32[]{:S(2)}) collective-permute-start(bf16[64,2176]{1,0:T(8,128)(2,1)S(1)} %prep.1.x_ref.refs_4_), channel_id=1, source_target_pairs={{0,4},{1,5},{2,6},{3,7},{4,0},{5,1},{6,2},{7,3},{8,12},{9,13},{10,... | collective-permute-start | bytes 835592 | tf_op jit(solution)/shard_map/ppermute | solution.py:269
  6.0 1.6 %collective-permute-start.1 = (bf16[64,2176]{1,0:T(8,128)(2,1)S(1)}, bf16[64,2176]{1,0:T(8,128)(2,1)S(1)}, u32[]{:S(2)}, u32[]{:S(2)}) collective-permute-start(bf16[64,2176]{1,0:T(8,128)(2,1)S(1)} %prep.1.x_ref.refs_4_), channel_id=1, source_target_pairs={{0,2},{1,3},{2,0},{3,1},{4,6},{5,7},{6,4},{7,5},{8,10},{9,11},{10,... | collective-permute-start | bytes 835592 | tf_op jit(solution)/shard_map/ppermute | solution.py:269
  7.6 0.0 collective-permute-start.2
  7.6 8.3 %load_weights.1 = (bf16[4,2048,512]{2,1,0:T(8,128)(2,1)S(1)}, bf16[4,2048,512]{2,1,0:T(8,128)(2,1)S(1)}, bf16[4,512,2048]{2,1,0:T(8,128)(2,1)S(1)}) custom-call(bf16[64,2176]{1,0:T(8,128)(2,1)S(1)} %prep.1.x_ref.refs_4_, bf16[4,2048,512]{2,1,0:T(8,128)(2,1)} %refs_0_.1, bf16[4,2048,512]{2,1,0:T(8,128)(2,1)} %refs_1_.1, bf16[4,512,2048]{2,1,0:T(8,128)(2,1)} %refs_2_.1), custom_call_target="tpu_custom_call" | custom-call | bytes 25165824 | tf_op jit(solution)/shard_map/load_weights/pallas_call | solution.py:150
  15.9 2.8 %collective-permute-done.refs_0_ = bf16[64,2176]{1,0:T(8,128)(2,1)S(1)} collective-permute-done((bf16[64,2176]{1,0:T(8,128)(2,1)S(1)}, bf16[64,2176]{1,0:T(8,128)(2,1)S(1)}, u32[]{:S(2)}, u32[]{:S(2)}) %collective-permute-start) | collective-permute-done | bytes 278560 | tf_op jit(solution)/shard_map/ppermute | solution.py:269
  18.7 0.2 collective-permute-done.1.refs_2_
  18.9 0.0 collective-permute-done.2.refs_5_
  18.9 0.0 collective-permute-start.3
  18.9 0.5 collective-permute-start.4
  19.4 1.5 %collective-permute-start.6 = (bf16[64,2176]{1,0:T(8,128)(2,1)S(1)}, bf16[64,2176]{1,0:T(8,128)(2,1)S(1)}, u32[]{:S(2)}, u32[]{:S(2)}) collective-permute-start(bf16[64,2176]{1,0:T(8,128)(2,1)S(1)} %collective-permute-done.refs_0_), channel_id=1, source_target_pairs={{0,2},{1,3},{2,0},{3,1},{4,6},{5,7},{6,4},{7,5},{8,10},{9,11},{10,... | collective-permute-start | bytes 835592 | tf_op jit(solution)/shard_map/ppermute | solution.py:269
  20.9 0.0 collective-permute-done.3.refs_1_
  20.9 0.0 collective-permute-done.4.refs_3_
  20.9 6.4 %experts_first.1 = (bf16[64,2048]{1,0:T(8,128)(2,1)S(1)}, bf16[64,2048]{1,0:T(8,128)(2,1)S(1)}, bf16[64,2048]{1,0:T(8,128)(2,1)S(1)}, bf16[64,2048]{1,0:T(8,128)...) custom-call(bf16[64,2176]{1,0:T(8,128)(2,1)S(1)} %collective-permute-done.refs_0_, ...), custom_call_target="tpu_custom_call" | custom-call | flops 4026531840 | bytes 25165824 | tf_op jit(solution)/shard_map/experts_first/pallas_call | solution.py:186
  27.3 0.2 collective-permute-start.10
  27.5 0.4 collective-permute-start.8
  27.9 0.1 collective-permute-start.5
  28.0 0.0 collective-permute-done.6.refs_0_
  28.0 0.4 collective-permute-start.7
  28.4 0.5 collective-permute-done.10
  28.9 0.1 add_convert_fusion
  29.0 0.0 copy-start
  29.0 1.5 %collective-permute-start.11 = (bf16[64,2048]{1,0:T(8,128)(2,1)S(1)}, bf16[64,2048]{1,0:T(8,128)(2,1)S(1)}, u32[]{:S(2)}, u32[]{:S(2)}) collective-permute-start(bf16[64,2048]{1,0:T(8,128)(2,1)S(1)} %add_convert_fusion), channel_id=1, source_target_pairs={{0,2},{1,3},{2,0},{3,1},{4,6},{5,7},{6,4},{7,5},{8,10},{9,11},{10,... | collective-permute-start | bytes 786440 | tf_op jit(solution)/shard_map/ppermute | solution.py:269
  30.5 0.0 collective-permute-done.7.refs_1_
  30.5 3.5 %experts_third.1 = (bf16[64,2048]{1,0:T(8,128)(2,1)S(1)}, bf16[64,2048]{1,0:T(8,128)(2,1)S(1)}) custom-call(bf16[64,2176]{1,0:T(8,128)(2,1)S(1)} %collective-permute-done.6.refs_0_, bf16[64,2176]{1,0:T(8,128)(2,1)S(1)} %collective-permute-done.7.refs_1_, bf16[4,2048,512]{2,1,0:T(8,128)(2,1)S(1)} %get-tuple-element.31.refs_6_.refs_2_, ...), custom_call_target="tpu_custom_call" | custom-call | flops 3221225472 | bytes 25165824 | tf_op jit(solution)/shard_map/experts_third/pallas_call | solution.py:186
  34.0 0.1 collective-permute-start.9
  34.1 0.0 collective-permute-done.8
  34.1 0.1 add_convert_fusion.1.near_ref
  34.1 1.2 %collective-permute-start.12 = (bf16[64,2048]{1,0:T(8,128)(2,1)S(1)}, bf16[64,2048]{1,0:T(8,128)(2,1)S(1)}, u32[]{:S(2)}, u32[]{:S(2)}) collective-permute-start(bf16[64,2048]{1,0:T(8,128)(2,1)S(1)} %add_convert_fusion.1.near_ref), channel_id=1, source_target_pairs={{0,2},{1,3},{2,0},{3,1},{4,6},{5,7},{6,4},{7,5},{8,10},{9,11},{10,... | collective-permute-start | bytes 786440 | tf_op jit(solution)/shard_map/ppermute | solution.py:269
  35.4 0.2 collective-permute-done.9
  35.6 0.1 convert_add_fusion.sum_ref
  35.6 1.9 %collective-permute-done.11.relayed_ref = bf16[64,2048]{1,0:T(8,128)(2,1)S(1)} collective-permute-done((bf16[64,2048]{1,0:T(8,128)(2,1)S(1)}, bf16[64,2048]{1,0:T(8,128)(2,1)S(1)}, u32[]{:S(2)}, u32[]{:S(2)}) %collective-permute-start.11) | collective-permute-done | bytes 262176 | tf_op jit(solution)/shard_map/ppermute | solution.py:269
  37.6 3.7 %collective-permute-start.13 = (bf16[64,2048]{1,0:T(8,128)(2,1)S(1)}, bf16[64,2048]{1,0:T(8,128)(2,1)S(1)}, u32[]{:S(2)}, u32[]{:S(2)}) collective-permute-start(bf16[64,2048]{1,0:T(8,128)(2,1)S(1)} %third_back.1.third_ref), channel_id=1, source_target_pairs={{0,6},{1,7},{2,4},{3,5},{4,2},{5,3},{6,0},{7,1},{8,14},{9,15},{10,... | collective-permute-start | bytes 786440 | tf_op jit(solution)/shard_map/ppermute | solution.py:269
  41.3 0.0 collective-permute-done.5.swapped_ref
  41.3 0.0 copy-done
  41.3 0.4 own_sum.1
  41.6 1.6 %collective-permute-start.14 = (f32[8,128]{1,0:T(8,128)S(1)}, f32[8,128]{1,0:T(8,128)S(1)}, u32[]{:S(2)}, u32[]{:S(2)}) collective-permute-start(f32[8,128]{1,0:T(8,128)S(1)} %get-tuple-element.45.score_ref), channel_id=1, source_target_pairs={{0,16},{8,24},{16,0},{24,8},{1,17},{9,25},{17,1},{25,9},{2,18},{10... | collective-permute-start | bytes 12296 | tf_op jit(solution)/shard_map/ppermute | solution.py:297
  43.2 2.1 %collective-permute-done.14.partner_ref = f32[8,128]{1,0:T(8,128)S(1)} collective-permute-done((f32[8,128]{1,0:T(8,128)S(1)}, f32[8,128]{1,0:T(8,128)S(1)}, u32[]{:S(2)}, u32[]{:S(2)}) %collective-permute-start.14) | collective-permute-done | bytes 4128 | tf_op jit(solution)/shard_map/ppermute | solution.py:297
  45.3 0.0 collective-permute-start.15
  45.3 1.2 %collective-permute-start.16 = (f32[2,8,128]{2,1,0:T(8,128)S(1)}, f32[2,8,128]{2,1,0:T(8,128)S(1)}, u32[]{:S(2)}, u32[]{:S(2)}) collective-permute-start(f32[2,8,128]{2,1,0:T(8,128)S(1)} %both_scores.1.both_ref), channel_id=1, source_target_pairs={{0,6},{1,7},{2,4},{3,5},{4,2},{5,3},{6,0},{7,1},{8,14},{9,15},{10,... | collective-permute-start | bytes 24584 | tf_op jit(solution)/shard_map/ppermute | solution.py:269
  46.5 0.0 collective-permute-done.12.near_ref
  46.5 4.4 %collective-permute-done.15.from_near_ref = f32[2,8,128]{2,1,0:T(8,128)S(1)} collective-permute-done((f32[2,8,128]{2,1,0:T(8,128)S(1)}, f32[2,8,128]{2,1,0:T(8,128)S(1)}, u32[]{:S(2)}, u32[]{:S(2)}) %collective-permute-start.15) | collective-permute-done | bytes 8224 | tf_op jit(solution)/shard_map/ppermute | solution.py:269
  50.9 0.0 collective-permute-done.16.from_third_ref
  50.9 0.0 collective-permute-done.13.third_ref
  50.9 0.9 %mixed.1 = (bf16[64,2048]{1,0:T(8,128)(2,1)}, f32[4]{0:T(128)}) custom-call(f32[64,2048]{1,0:T(8,128)S(1)} %get-tuple-element.44.sum_ref, bf16[64,2048]{1,0:T(8,128)(2,1)S(1)} %collective-permute-done.12.near_ref, bf16[64,2048]{1,0:T(8,128)(2,1)S(1)} %collective-permute-done.13.third_ref, f32[2,8,128]{2,1,0:T(8,128)S(1)} %both_scores.1.both_ref, ...), custom_call_target="tpu_custom_call" | custom-call | tf_op jit(solution)/shard_map/mixed/pallas_call | solution.py:258
  (2 shorter events, 0.0 us)
Async XLA Ops:
  1.9 16.8 %collective-permute-start = (bf16[64,2176]{1,0:T(8,128)(2,1)S(1)}, bf16[64,2176]{1,0:T(8,128)(2,1)S(1)}, u32[]{:S(2)}, u32[]{:S(2)}) collective-permute-start(bf16[64,2176]{1,0:T(8,128)(2,1)S(1)} %prep.1.x_ref.refs_4_), channel_id=1, source_target_pairs={{0,4},{1,5},{2,6},{3,7},{4,0},{5,1},{6,2},{7,3},{8,12},{9,13},{10,... | collective-permute-start | bytes 835592 | tf_op jit(solution)/shard_map/ppermute | solution.py:269
  6.0 12.9 %collective-permute-start.1 = (bf16[64,2176]{1,0:T(8,128)(2,1)S(1)}, bf16[64,2176]{1,0:T(8,128)(2,1)S(1)}, u32[]{:S(2)}, u32[]{:S(2)}) collective-permute-start(bf16[64,2176]{1,0:T(8,128)(2,1)S(1)} %prep.1.x_ref.refs_4_), channel_id=1, source_target_pairs={{0,2},{1,3},{2,0},{3,1},{4,6},{5,7},{6,4},{7,5},{8,10},{9,11},{10,... | collective-permute-start | bytes 835592 | tf_op jit(solution)/shard_map/ppermute | solution.py:269
  7.6 11.3 %collective-permute-start.2 = (bf16[64,2176]{1,0:T(8,128)(2,1)S(1)}, bf16[64,2176]{1,0:T(8,128)(2,1)S(1)}, u32[]{:S(2)}, u32[]{:S(2)}) collective-permute-start(bf16[64,2176]{1,0:T(8,128)(2,1)S(1)} %prep.1.x_ref.refs_4_), channel_id=1, source_target_pairs={{0,1},{1,0},{2,3},{3,2},{4,5},{5,4},{6,7},{7,6},{8,9},{9,8},{10,11... | collective-permute-start | bytes 835592 | tf_op jit(solution)/shard_map/ppermute | solution.py:269
  18.9 2.0 %collective-permute-start.3 = (bf16[64,2176]{1,0:T(8,128)(2,1)S(1)}, bf16[64,2176]{1,0:T(8,128)(2,1)S(1)}, u32[]{:S(2)}, u32[]{:S(2)}) collective-permute-start(bf16[64,2176]{1,0:T(8,128)(2,1)S(1)} %collective-permute-done.refs_0_), channel_id=1, source_target_pairs={{0,1},{1,0},{2,3},{3,2},{4,5},{5,4},{6,7},{7,6},{8,9},{9,8},{10,11... | collective-permute-start | bytes 835592 | tf_op jit(solution)/shard_map/ppermute | solution.py:269
  18.9 2.0 %collective-permute-start.4 = (bf16[64,2176]{1,0:T(8,128)(2,1)S(1)}, bf16[64,2176]{1,0:T(8,128)(2,1)S(1)}, u32[]{:S(2)}, u32[]{:S(2)}) collective-permute-start(bf16[64,2176]{1,0:T(8,128)(2,1)S(1)} %collective-permute-done.1.refs_2_), channel_id=1, source_target_pairs={{0,1},{1,0},{2,3},{3,2},{4,5},{5,4},{6,7},{7,6},{8,9},{9,8},{10,11... | collective-permute-start | bytes 835592 | tf_op jit(solution)/shard_map/ppermute | solution.py:269
  19.4 8.6 %collective-permute-start.6 = (bf16[64,2176]{1,0:T(8,128)(2,1)S(1)}, bf16[64,2176]{1,0:T(8,128)(2,1)S(1)}, u32[]{:S(2)}, u32[]{:S(2)}) collective-permute-start(bf16[64,2176]{1,0:T(8,128)(2,1)S(1)} %collective-permute-done.refs_0_), channel_id=1, source_target_pairs={{0,2},{1,3},{2,0},{3,1},{4,6},{5,7},{6,4},{7,5},{8,10},{9,11},{10,... | collective-permute-start | bytes 835592 | tf_op jit(solution)/shard_map/ppermute | solution.py:269
  27.3 1.6 %collective-permute-start.10 = (bf16[64,2048]{1,0:T(8,128)(2,1)S(1)}, bf16[64,2048]{1,0:T(8,128)(2,1)S(1)}, u32[]{:S(2)}, u32[]{:S(2)}) collective-permute-start(bf16[64,2048]{1,0:T(8,128)(2,1)S(1)} %get-tuple-element.43), channel_id=1, source_target_pairs={{0,1},{1,0},{2,3},{3,2},{4,5},{5,4},{6,7},{7,6},{8,9},{9,8},{10,11... | collective-permute-start | bytes 786440 | tf_op jit(solution)/shard_map/ppermute | solution.py:269
  27.5 6.6 %collective-permute-start.8 = (bf16[64,2048]{1,0:T(8,128)(2,1)S(1)}, bf16[64,2048]{1,0:T(8,128)(2,1)S(1)}, u32[]{:S(2)}, u32[]{:S(2)}) collective-permute-start(bf16[64,2048]{1,0:T(8,128)(2,1)S(1)} %get-tuple-element.38), channel_id=1, source_target_pairs={{0,1},{1,0},{2,3},{3,2},{4,5},{5,4},{6,7},{7,6},{8,9},{9,8},{10,11... | collective-permute-start | bytes 786440 | tf_op jit(solution)/shard_map/ppermute | solution.py:269
  27.9 13.3 %collective-permute-start.5 = (bf16[64,2048]{1,0:T(8,128)(2,1)S(1)}, bf16[64,2048]{1,0:T(8,128)(2,1)S(1)}, u32[]{:S(2)}, u32[]{:S(2)}) collective-permute-start(bf16[64,2048]{1,0:T(8,128)(2,1)S(1)} %get-tuple-element.35), channel_id=1, source_target_pairs={{0,1},{1,0},{2,3},{3,2},{4,5},{5,4},{6,7},{7,6},{8,9},{9,8},{10,11... | collective-permute-start | bytes 786440 | tf_op jit(solution)/shard_map/ppermute | solution.py:269
  28.0 2.5 %collective-permute-start.7 = (bf16[64,2176]{1,0:T(8,128)(2,1)S(1)}, bf16[64,2176]{1,0:T(8,128)(2,1)S(1)}, u32[]{:S(2)}, u32[]{:S(2)}) collective-permute-start(bf16[64,2176]{1,0:T(8,128)(2,1)S(1)} %collective-permute-done.6.refs_0_), channel_id=1, source_target_pairs={{0,1},{1,0},{2,3},{3,2},{4,5},{5,4},{6,7},{7,6},{8,9},{9,8},{10,11... | collective-permute-start | bytes 835592 | tf_op jit(solution)/shard_map/ppermute | solution.py:269
  29.0 12.3 %copy-start = (f32[2048]{0:T(1024)S(1)}, f32[2048]{0:T(1024)}, u32[]{:S(2)}) copy-start(f32[2048]{0:T(1024)} %param.17) | copy-start | bytes 24580
  29.0 8.5 %collective-permute-start.11 = (bf16[64,2048]{1,0:T(8,128)(2,1)S(1)}, bf16[64,2048]{1,0:T(8,128)(2,1)S(1)}, u32[]{:S(2)}, u32[]{:S(2)}) collective-permute-start(bf16[64,2048]{1,0:T(8,128)(2,1)S(1)} %add_convert_fusion), channel_id=1, source_target_pairs={{0,2},{1,3},{2,0},{3,1},{4,6},{5,7},{6,4},{7,5},{8,10},{9,11},{10,... | collective-permute-start | bytes 786440 | tf_op jit(solution)/shard_map/ppermute | solution.py:269
  34.0 1.6 %collective-permute-start.9 = (bf16[64,2048]{1,0:T(8,128)(2,1)S(1)}, bf16[64,2048]{1,0:T(8,128)(2,1)S(1)}, u32[]{:S(2)}, u32[]{:S(2)}) collective-permute-start(bf16[64,2048]{1,0:T(8,128)(2,1)S(1)} %get-tuple-element.41), channel_id=1, source_target_pairs={{0,1},{1,0},{2,3},{3,2},{4,5},{5,4},{6,7},{7,6},{8,9},{9,8},{10,11... | collective-permute-start | bytes 786440 | tf_op jit(solution)/shard_map/ppermute | solution.py:269
  34.1 12.3 %collective-permute-start.12 = (bf16[64,2048]{1,0:T(8,128)(2,1)S(1)}, bf16[64,2048]{1,0:T(8,128)(2,1)S(1)}, u32[]{:S(2)}, u32[]{:S(2)}) collective-permute-start(bf16[64,2048]{1,0:T(8,128)(2,1)S(1)} %add_convert_fusion.1.near_ref), channel_id=1, source_target_pairs={{0,2},{1,3},{2,0},{3,1},{4,6},{5,7},{6,4},{7,5},{8,10},{9,11},{10,... | collective-permute-start | bytes 786440 | tf_op jit(solution)/shard_map/ppermute | solution.py:269
  37.6 13.3 %collective-permute-start.13 = (bf16[64,2048]{1,0:T(8,128)(2,1)S(1)}, bf16[64,2048]{1,0:T(8,128)(2,1)S(1)}, u32[]{:S(2)}, u32[]{:S(2)}) collective-permute-start(bf16[64,2048]{1,0:T(8,128)(2,1)S(1)} %third_back.1.third_ref), channel_id=1, source_target_pairs={{0,6},{1,7},{2,4},{3,5},{4,2},{5,3},{6,0},{7,1},{8,14},{9,15},{10,... | collective-permute-start | bytes 786440 | tf_op jit(solution)/shard_map/ppermute | solution.py:269
  41.6 3.7 %collective-permute-start.14 = (f32[8,128]{1,0:T(8,128)S(1)}, f32[8,128]{1,0:T(8,128)S(1)}, u32[]{:S(2)}, u32[]{:S(2)}) collective-permute-start(f32[8,128]{1,0:T(8,128)S(1)} %get-tuple-element.45.score_ref), channel_id=1, source_target_pairs={{0,16},{8,24},{16,0},{24,8},{1,17},{9,25},{17,1},{25,9},{2,18},{10... | collective-permute-start | bytes 12296 | tf_op jit(solution)/shard_map/ppermute | solution.py:297
  45.3 5.6 %collective-permute-start.15 = (f32[2,8,128]{2,1,0:T(8,128)S(1)}, f32[2,8,128]{2,1,0:T(8,128)S(1)}, u32[]{:S(2)}, u32[]{:S(2)}) collective-permute-start(f32[2,8,128]{2,1,0:T(8,128)S(1)} %both_scores.1.both_ref), channel_id=1, source_target_pairs={{0,2},{1,3},{2,0},{3,1},{4,6},{5,7},{6,4},{7,5},{8,10},{9,11},{10,... | collective-permute-start | bytes 24584 | tf_op jit(solution)/shard_map/ppermute | solution.py:269
  45.3 5.6 %collective-permute-start.16 = (f32[2,8,128]{2,1,0:T(8,128)S(1)}, f32[2,8,128]{2,1,0:T(8,128)S(1)}, u32[]{:S(2)}, u32[]{:S(2)}) collective-permute-start(f32[2,8,128]{2,1,0:T(8,128)S(1)} %both_scores.1.both_ref), channel_id=1, source_target_pairs={{0,6},{1,7},{2,4},{3,5},{4,2},{5,3},{6,0},{7,1},{8,14},{9,15},{10,... | collective-permute-start | bytes 24584 | tf_op jit(solution)/shard_map/ppermute | solution.py:269
